TPU v7x, 32 devices: a whole 2x2x4 slice. The times are simulated.
32 devices in a mesh: slab: 8 (over y, x, core), xy: 4 (over z).
Axes of the slice: x: 2, y: 2, z: 4, core: 2. Of those that a mesh axis runs over, the one named last changes fastest.
Arguments:
- volume: float32 [16, 32, 512], P('slab', 'xy'), may hold values from 0 to 1
- footprint: bfloat16 [16, 32, 4, 2, 128, 256], P('slab', 'xy'), may hold values from 0.049804688 to 1
- tile_block: int32 [16, 32, 4, 2], P('slab', 'xy'), may hold values from 0 to 511, as said below
- tile_cells: int32 [16, 32, 4, 2], P('slab', 'xy'), may hold values from 1 to 256, as said below
- measured: float32 [2, 131072], replicated, may hold values from 0 to 128
Outputs:
- updated: float32 [16, 32, 512], P('slab', 'xy')
- correction: float32 [2, 131072], P(None, ('slab', 'xy'))
Inputs may be any that keep to these rules, and one draw needn't show every extreme that they name: `tile_cells`: at least one tile of some view has all 256 cells live. `tile_block`: A tile's block lies in detector row about plane * 4, off by at most one below and 4 above (within the detector); its column block follows the tile's place along the row for even views and the row's place in the plane for odd views, off by at most one.
All inputs are finite; a program needn't handle non-finite values.
Results may differ from a plain program's by a relative error of at most 0.0003.
Values may be sent and summed in bfloat16 or wider, within the bound.
No kernel may reach another device: no remote copies, remote signals or barrier semaphores. Data moves between devices by JAX's collectives and lax.ppermute only.
A program may use at most 64 MiB of HBM per device.

v0:
```python
import jax
import jax.numpy as jnp
from jax import lax
from jax.sharding import PartitionSpec as P

RELAX = 1.0
TV_RATE = 0.8
SMOOTHING = 0.01


def extended(cells, sides, width):
    for axis, dim in sides:
        count = lax.axis_size(axis)
        ends = count - 1
        head = lax.slice_in_dim(cells, 0, width, axis=dim)
        tail = lax.slice_in_dim(cells, cells.shape[dim] - width, cells.shape[dim], axis=dim)
        cells = jnp.concatenate(
            [
                lax.ppermute(tail, axis, [(i, (i + 1) % count) for i in range(ends)]),
                cells,
                lax.ppermute(head, axis, [((i + 1) % count, i) for i in range(ends)]),
            ],
            axis=dim,
        )
    return cells


def tv_slope(padded):
    base = padded[:-1, :-1, :-1]
    diff_a = padded[1:, :-1, :-1] - base
    diff_b = padded[:-1, 1:, :-1] - base
    diff_e = padded[:-1, :-1, 1:] - base
    size = jnp.sqrt(diff_a * diff_a + diff_b * diff_b + diff_e * diff_e + SMOOTHING)
    unit_a = diff_a / size
    unit_b = diff_b / size
    unit_e = diff_e / size
    total = unit_a + unit_b + unit_e
    return -total[1:, 1:, 1:] + unit_a[:-1, 1:, 1:] + unit_b[1:, :-1, 1:] + unit_e[1:, 1:, :-1]


def slope_scale(slope):
    return jnp.sqrt(lax.psum(jnp.sum(slope * slope), ("slab", "xy")) + 1e-06)


def body(volume, footprint, tile_block, tile_cells, measured):
    planes, rows, ycells = volume.shape
    views, tvox, tdet = (footprint.shape[3], footprint.shape[4], footprint.shape[5])
    count = planes * rows * footprint.shape[2]
    detector = measured.shape[1]
    nblocks = detector // tdet
    weights = footprint.reshape(count, views, tvox, tdet)
    block_of = tile_block.reshape(count, views)
    lane = jnp.arange(tdet, dtype=jnp.int32)
    live = lane[None, None, :] < tile_cells.reshape(count, views)[:, :, None]
    masked = jnp.where(live[:, :, None, :], weights, jnp.zeros((), jnp.bfloat16))
    voxels = volume.astype(jnp.bfloat16).reshape(count, tvox)
    contrib = jnp.einsum("tj,tvjc->tvc", voxels, masked, preferred_element_type=jnp.float32)
    rays = jnp.sum(masked, axis=2, dtype=jnp.float32)
    onehot = (block_of[:, :, None] == jnp.arange(nblocks, dtype=jnp.int32)).astype(jnp.float32)
    projected = jnp.einsum(
        "tvn,tvc->vnc", onehot, contrib, precision=lax.Precision.HIGHEST
    ).reshape(views, detector)
    ray_weight = jnp.einsum("tvn,tvc->vnc", onehot, rays, precision=lax.Precision.HIGHEST).reshape(
        views, detector
    )
    share = detector // (lax.axis_size("slab") * lax.axis_size("xy"))
    position = lax.axis_index(("slab", "xy")) * share
    projected, ray_weight = lax.psum((projected, ray_weight), ("slab", "xy"))
    correction_all = (measured - projected) / jnp.maximum(ray_weight, 1.0)
    correction = lax.dynamic_slice_in_dim(correction_all, position, share, 1)
    correction_b = correction_all.astype(jnp.bfloat16)
    blocked = correction_b.reshape(views, nblocks, tdet)
    picked = blocked[jnp.arange(views, dtype=jnp.int32)[None, :], block_of]
    back = jnp.einsum("tvjc,tvc->tj", masked, picked, preferred_element_type=jnp.float32)
    column = jnp.sum(masked, axis=(1, 3), dtype=jnp.float32)
    shift = (back / column).reshape(planes, rows, ycells)
    sart = jnp.maximum(volume + RELAX * shift, 0.0)
    step_gap = sart - volume
    update_norm = jnp.sqrt(lax.psum(jnp.sum(step_gap * step_gap), ("slab", "xy")))
    rimmed = extended(sart, (("slab", 0), ("xy", 1)), 2)
    padded = jnp.pad(rimmed, ((0, 0), (0, 0), (2, 2)))
    slope_wide = tv_slope(padded)
    first_slope = slope_wide[1:-1, 1:-1, 1:-1]
    first_step = TV_RATE * update_norm / slope_scale(first_slope)
    wide = padded[1:-1, 1:-1, 1:-1] - first_step * slope_wide
    plane_ids = lax.axis_index("slab") * planes + jnp.arange(planes + 2, dtype=jnp.int32) - 1
    row_ids = lax.axis_index("xy") * rows + jnp.arange(rows + 2, dtype=jnp.int32) - 1
    cell_ids = jnp.arange(ycells + 2, dtype=jnp.int32) - 1
    inside_plane = (plane_ids >= 0) & (plane_ids < lax.axis_size("slab") * planes)
    inside_row = (row_ids >= 0) & (row_ids < lax.axis_size("xy") * rows)
    inside_cell = (cell_ids >= 0) & (cell_ids < ycells)
    inside = inside_plane[:, None, None] & inside_row[None, :, None] & inside_cell[None, None, :]
    wide = jnp.where(inside, wide, 0.0)
    second_slope = tv_slope(wide)
    updated = (
        wide[1:-1, 1:-1, 1:-1] - TV_RATE * update_norm / slope_scale(second_slope) * second_slope
    )
    return (updated, correction)


def solution(mesh):
    placed = (
        P("slab", "xy", None),
        P("slab", "xy", None, None, None, None),
        P("slab", "xy", None, None),
        P("slab", "xy", None, None),
        P(),
    )
    return jax.shard_map(
        body,
        mesh=mesh,
        in_specs=placed,
        out_specs=(P("slab", "xy", None), P(None, ("slab", "xy"))),
        check_vma=False,
    )
```

profile of v0, /device:TPU:0, one launch (start us, length us, event | category | flops | bytes accessed | tf_op | source)
XLA Modules:
  0.0 289.5 jit_solution(4142094065004729563)
XLA Ops:
  7.2 0.8 copy.21
  8.1 0.8 convert_element_type.15
  8.9 0.8 copy.30
  9.7 0.1 iota_compare_fusion.5
  10.0 6.0 %convert_reduce_fusion = (f32[2,8,4,128]{3,2,1,0:T(4,128)S(1)}, f32[2,8,4,2,256]{4,3,2,1,0:T(2,128)S(1)}) fusion(bf16[2,8,4,2,128,256]{5,4,3,2,1,0:T(8,128)(2,1)} %param.6, pred[2,8,4,2,256]{4,3,2,1,0:T(4,128)(4,1)S(1)} %iota_compare_fusion.5), kind=kLoop, calls=%fused_computation.1 | loop fusion | flops 16736256 | bytes 8585216 | tf_op jit(solution)/shard_map/reduce_sum | solution.py:75
  16.0 0.7 convolution_bitcast_fusion
  16.7 1.9 copy.33
  18.6 7.3 %bitcast_select_fusion = bf16[64,2,128,256]{3,2,1,0:T(8,128)(2,1)} fusion(bf16[2,8,4,2,128,256]{5,4,3,2,1,0:T(8,128)(2,1)} %param.6, pred[64,2,256]{2,1,0:T(4,128)(4,1)S(1)} %iota_compare_fusion.6), kind=kLoop, calls=%fused_computation.3 | loop fusion | flops 4194304 | bytes 16809984 | tf_op jit(solution)/shard_map/jit(_where)/select_n | solution.py:55
  25.9 4.7 %fusion.23 = f32[64,1,2,256]{3,1,2,0:T(1,128)S(1)} fusion(bf16[64,2,128,256]{3,2,1,0:T(8,128)(2,1)} %bitcast_select_fusion, bf16[64,128,1,1]{1,2,3,0:T(2,128)(2,1)S(1)} %reshape.143), kind=kOutput, calls=%fused_computation.74 | convolution fusion | flops 8388608 | bytes 8536064 | tf_op jit(solution)/shard_map/tj,tvjc->tvc/dot_general | solution.py:57
  30.6 0.7 convolution_bitcast_fusion.1
  31.3 1.8 copy.32
  33.5 136.4 %all-reduce.5.cloned.1.call-done = (f32[2,131072]{1,0:T(2,128)}, f32[2,131072]{1,0:T(2,128)}) async-done(((f32[2,131072]{1,0:T(2,128)}, f32[2,131072]{1,0:T(2,128)}), (f32[2,131072]{1,0:T(2,128)}, f32[2,131072]{1,0:T(2,128)})) %all-reduce.5.cloned.1.call-update) | async-done | bytes 2097168 | tf_op jit(solution)/shard_map/psum | solution.py:68
  169.9 2.6 fusion.22
  172.6 1.1 gather_fusion
  173.8 5.6 %fusion.24 = f32[64,1,128,1]{2,1,3,0:T(1,128)S(1)} fusion(bf16[64,2,128,256]{3,2,1,0:T(8,128)(2,1)} %bitcast_select_fusion, bf16[64,2,256,1]{2,3,1,0:T(2,128)(2,1)S(1)} %reshape.145), kind=kOutput, calls=%fused_computation.75 | convolution fusion | flops 8388608 | bytes 8486912 | tf_op jit(solution)/shard_map/tvjc,tvc->tj/dot_general | solution.py:74
  179.5 0.6 multiply_reduce_fusion.1
  180.1 1.3 collective-permute-start.1
  181.4 3.0 %collective-permute-start = (f32[2,8,512]{2,1,0:T(8,128)S(1)}, f32[2,8,512]{2,1,0:T(8,128)S(1)}, u32[]{:S(2)}, u32[]{:S(2)}) collective-permute-start(f32[2,8,512]{2,1,0:T(8,128)S(1)} %get-tuple-element.23), channel_id=1, source_target_pairs={{0,4},{4,8},{8,12},{12,16},{16,20},{20,24},{24,28},{1,5},{5,9},{9,... | collective-permute-start | bytes 98312 | tf_op jit(solution)/shard_map/ppermute | solution.py:19
  184.4 0.8 collective-permute-done
  185.3 3.3 %collective-permute-start.2 = (f32[6,2,512]{2,1,0:T(2,128)S(1)}, f32[6,2,512]{2,1,0:T(2,128)S(1)}, u32[]{:S(2)}, u32[]{:S(2)}) collective-permute-start(f32[6,2,512]{2,1,0:T(2,128)S(1)} %get-tuple-element.20), channel_id=1, source_target_pairs={{0,1},{1,2},{2,3},{4,5},{5,6},{6,7},{8,9},{9,10},{10,11},{12,13},{... | collective-permute-start | bytes 73736 | tf_op jit(solution)/shard_map/ppermute | solution.py:19
  188.6 1.5 collective-permute-start.3
  190.1 0.6 constant_dynamic-slice_fusion
  190.7 3.9 %collective-permute-done.3 = f32[6,2,512]{2,1,0:T(2,128)S(1)} collective-permute-done((f32[6,2,512]{2,1,0:T(2,128)S(1)}, f32[6,2,512]{2,1,0:T(2,128)S(1)}, u32[]{:S(2)}, u32[]{:S(2)}) %collective-permute-start.3) | collective-permute-done | bytes 24608 | tf_op jit(solution)/shard_map/ppermute | solution.py:21
  194.6 0.2 select_maximum_fusion
  194.8 0.2 fusion.8
  195.1 0.3 slice_add_fusion
  195.4 0.8 fusion.15
  196.2 40.9 %all-reduce.1 = (f32[]{:T(128)}, f32[]{:T(128)}) all-reduce(f32[]{:T(128)} %get-tuple-element.22, f32[]{:T(128)} %fusion.15), channel_id=1, replica_groups=mesh['slab'=8,'xy'=4] {'slab','xy'}, use_global_device_ids=true, to_apply=%region_5.6 | all-reduce | flops 2 | bytes 16 | tf_op jit(solution)/shard_map/psum | solution.py:79
  238.7 0.1 fusion.11
  238.9 0.7 multiply_reduce_fusion
  239.6 41.6 %psum.39 = f32[]{:T(128)} all-reduce(f32[]{:T(128)} %get-tuple-element.8), channel_id=1, replica_groups=mesh['slab'=8,'xy'=4] {'slab','xy'}, use_global_device_ids=true, to_apply=%region_9.10 | all-reduce | flops 1 | bytes 8 | tf_op jit(solution)/shard_map/psum | solution.py:42
  281.9 0.7 slice_subtract_fusion.7
  (27 shorter events, 1.2 us)
Async XLA Ops:
  7.2 162.7 %all-reduce.5.cloned.1.call-start = ((), (), s32[]{:S(2)}) async-start(), calls=%async_computation | async-start | bytes 4194304 | tf_op jit(solution)/shard_map/psum | solution.py:68
  25.9 144.0 %copy-start = (f32[2,131072]{1,0:T(2,128)S(1)}, f32[2,131072]{1,0:T(2,128)}, u32[]{:S(2)}) copy-start(f32[2,131072]{1,0:T(2,128)} %param.9) | copy-start | bytes 3145732
  33.1 146.4 %copy-start.1 = (f32[2,8,512]{2,1,0:T(8,128)S(1)}, f32[2,8,512]{2,1,0:T(8,128)}, u32[]{:S(2)}) copy-start(f32[2,8,512]{2,1,0:T(8,128)} %param.5) | copy-start | bytes 98308
  180.1 4.4 %collective-permute-start.1 = (f32[2,8,512]{2,1,0:T(8,128)S(1)}, f32[2,8,512]{2,1,0:T(8,128)S(1)}, u32[]{:S(2)}, u32[]{:S(2)}) collective-permute-start(f32[2,8,512]{2,1,0:T(8,128)S(1)} %get-tuple-element.23), channel_id=1, source_target_pairs={{4,0},{8,4},{12,8},{16,12},{20,16},{24,20},{28,24},{5,1},{9,5},{13... | collective-permute-start | bytes 98312 | tf_op jit(solution)/shard_map/ppermute | solution.py:21
  181.4 3.9 %collective-permute-start = (f32[2,8,512]{2,1,0:T(8,128)S(1)}, f32[2,8,512]{2,1,0:T(8,128)S(1)}, u32[]{:S(2)}, u32[]{:S(2)}) collective-permute-start(f32[2,8,512]{2,1,0:T(8,128)S(1)} %get-tuple-element.23), channel_id=1, source_target_pairs={{0,4},{4,8},{8,12},{12,16},{16,20},{20,24},{24,28},{1,5},{5,9},{9,... | collective-permute-start | bytes 98312 | tf_op jit(solution)/shard_map/ppermute | solution.py:19
  185.3 5.5 %collective-permute-start.2 = (f32[6,2,512]{2,1,0:T(2,128)S(1)}, f32[6,2,512]{2,1,0:T(2,128)S(1)}, u32[]{:S(2)}, u32[]{:S(2)}) collective-permute-start(f32[6,2,512]{2,1,0:T(2,128)S(1)} %get-tuple-element.20), channel_id=1, source_target_pairs={{0,1},{1,2},{2,3},{4,5},{5,6},{6,7},{8,9},{9,10},{10,11},{12,13},{... | collective-permute-start | bytes 73736 | tf_op jit(solution)/shard_map/ppermute | solution.py:19
  188.6 6.0 %collective-permute-start.3 = (f32[6,2,512]{2,1,0:T(2,128)S(1)}, f32[6,2,512]{2,1,0:T(2,128)S(1)}, u32[]{:S(2)}, u32[]{:S(2)}) collective-permute-start(f32[6,2,512]{2,1,0:T(2,128)S(1)} %get-tuple-element.21), channel_id=1, source_target_pairs={{1,0},{2,1},{3,2},{5,4},{6,5},{7,6},{9,8},{10,9},{11,10},{13,12},{... | collective-permute-start | bytes 73736 | tf_op jit(solution)/shard_map/ppermute | solution.py:21
Sparse Core Ops, SparseCore 0:
  33.2 136.6 all-reduce.4
where the time goes:
time: 290 us; the launch traced here: 289 us
  waiting for transfers between devices  141 us (49%)
  blocking collectives  82.6 us (28%)
  other arithmetic  21.1 us (7%)
  between operations  16.4 us (6%)
  matrix products  11.7 us (4%)
  starting transfers between devices  9.17 us (3%)
  local copies, waits for them, and re-layouts  7.55 us (3%)
    psum x1, waiting for transfers between devices, body(): projected, ray_weight = lax.psum((projected, ray_weight), ('slab', 'xy'))  136 us
    psum x1, blocking collectives, slope_scale(): return jnp.sqrt(lax.psum(jnp.sum(slope * slope), ('slab', 'xy')) + 1e-06)  41.6 us
    psum x1, blocking collectives, body(): lax.psum(jnp.sum(step_gap * step_gap), ('slab', 'xy'))  40.9 us
    select_n x1, other arithmetic, body(): jnp.where(live[:, :, None, :], weights, jnp.zeros((), jnp.bfloat16))  7.31 us
    ppermute x2, starting transfers between devices, extended(): lax.ppermute(tail, axis, [(i, (i + 1) % count) for i in range(ends)])  6.38 us
    reduce_sum x1, other arithmetic, body(): column = jnp.sum(masked, axis=(1, 3), dtype=jnp.float32)  6.02 us
  transfers between devices with their start and end apart: 5, of which 3 were waited for; matrix products, arithmetic and copies ran while one was open for 0% of the time, Pallas kernels for 0%

commit v1 on v0

v1 whole, which is shorter than its diff:
```python
import functools

import jax
import jax.numpy as jnp
from jax import lax
from jax.experimental import pallas as pl
from jax.experimental.pallas import tpu as pltpu
from jax.sharding import PartitionSpec as P

RELAX = 1.0
TV_RATE = 0.8
SMOOTHING = 0.01
DCOLS = 2048
VMEM_BYTES = 32 * 1024 * 1024


class Plan:
    def __init__(self, slabs, bands, views, nblocks, tdet):
        self.slabs, self.bands, self.views = slabs, bands, views
        self.per_row = DCOLS // tdet
        self.own = nblocks // (slabs * bands)
        self.slab_own = nblocks // slabs
        self.halo = self.per_row
        self.local = self.slab_own + 2 * self.halo
        self.drows = self.local // self.per_row
        narrow = self.per_row // bands
        own_rows = self.own % self.per_row == 0
        self.narrow = narrow if narrow >= 1 and narrow * bands == self.per_row and own_rows else 0
        self.width = [
            self.narrow + 2 if v % 2 and self.narrow else self.per_row for v in range(views)
        ]
        self.base = [sum(self.width[:v]) * self.drows for v in range(views)]
        self.total = sum(self.width) * self.drows

    def first_column(self, v, band):
        return band * self.narrow - 1 if v % 2 and self.narrow else 0


def shift_all(cells, axis, step):
    count = lax.axis_size(axis)
    return lax.ppermute(cells, axis, [(i, (i + step) % count) for i in range(count)])


def swap_all(cells, axis, flip):
    count = lax.axis_size(axis)
    return lax.ppermute(cells, axis, [(i, i ^ flip) for i in range(count)])


def block_index(plan, v, block, slab, band):
    local = block - slab * plan.slab_own + plan.halo
    row = lax.div(local, plan.per_row)
    column = lax.rem(local, plan.per_row) - plan.first_column(v, band)
    index = row * plan.width[v] + column
    return jnp.clip(index, 0, plan.width[v] * plan.drows - 1)


def project_kernel(plan, shape, vol_ref, foot_ref, block_ref, cells_ref, out_ref, acc, foot, sems):
    planes, rows, tiles, views, tvox, tdet = shape
    slab, band = lax.axis_index("slab"), lax.axis_index("xy")
    parts = sems.shape[0]
    step = rows * planes // parts

    def copy(n):
        p, r = n * step // rows, n * step % rows
        return pltpu.make_async_copy(
            foot_ref.at[p, pl.ds(r, step)], foot.at[p, pl.ds(r, step)], sems.at[n]
        )

    for n in range(parts):
        copy(n).start()
    acc[...] = jnp.zeros_like(acc)
    top = lax.broadcasted_iota(jnp.int32, (8, tvox), 0) == 0
    lane = lax.broadcasted_iota(jnp.int32, (8, tdet), 1)
    for n in range(parts):
        copy(n).wait()
        for p, r in [divmod(n * step + k, rows) for k in range(step)]:
            for t in range(tiles):
                voxels = vol_ref[p, r : r + 1, t * tvox : (t + 1) * tvox]
                left = jnp.where(top, jnp.broadcast_to(voxels, (8, tvox)), 1.0)
                left = left.astype(jnp.bfloat16)
                for v in range(views):
                    sums = jnp.dot(left, foot[p, r, t, v], preferred_element_type=jnp.float32)
                    sums = jnp.where(lane < cells_ref[p, r, t, v], sums, 0.0)
                    at = plan.base[v] + block_index(plan, v, block_ref[p, r, t, v], slab, band)
                    acc[at] += sums
    out_ref[0] = acc[:, 0, :]
    out_ref[1] = acc[:, 1, :]


def project(plan, volume, footprint, tile_block, tile_cells):
    shape = footprint.shape
    parts = shape[0] * shape[1]
    tdet = shape[-1]
    return pl.pallas_call(
        functools.partial(project_kernel, plan, shape),
        out_shape=jax.ShapeDtypeStruct((2, plan.total, tdet), jnp.float32),
        in_specs=[
            pl.BlockSpec(memory_space=pltpu.VMEM),
            pl.BlockSpec(memory_space=pl.ANY),
            pl.BlockSpec(memory_space=pltpu.SMEM),
            pl.BlockSpec(memory_space=pltpu.SMEM),
        ],
        out_specs=pl.BlockSpec(memory_space=pltpu.VMEM),
        scratch_shapes=[
            pltpu.VMEM((plan.total, 8, tdet), jnp.float32),
            pltpu.VMEM(shape, jnp.bfloat16),
            pltpu.SemaphoreType.DMA((parts,)),
        ],
        compiler_params=pltpu.CompilerParams(vmem_limit_bytes=VMEM_BYTES),
        name="project",
    )(volume, footprint, tile_block, tile_cells)


def back_kernel(
    plan, shape, vol_ref, foot_ref, block_ref, cells_ref, corr_ref, sart_ref, gap_ref, sums, foot, sems
):
    planes, rows, tiles, views, tvox, tdet = shape
    slab = lax.axis_index("slab")
    parts = sems.shape[0]
    step = rows * planes // parts

    def copy(n):
        p, r = n * step // rows, n * step % rows
        return pltpu.make_async_copy(
            foot_ref.at[p, pl.ds(r, step)], foot.at[p, pl.ds(r, step)], sems.at[n]
        )

    for n in range(parts):
        copy(n).start()
    top = lax.broadcasted_iota(jnp.int32, (8, tdet), 0) == 0
    lane = lax.broadcasted_iota(jnp.int32, (8, tdet), 1)
    for n in range(parts):
        copy(n).wait()
        for p, r in [divmod(n * step + k, rows) for k in range(step)]:
            for t in range(tiles):
                both = 0.0
                for v in range(views):
                    local = block_ref[p, r, t, v] - slab * plan.slab_own + plan.halo
                    local = jnp.clip(local, 0, plan.local - 1)
                    picked = jnp.broadcast_to(corr_ref[v, pl.ds(local, 1), :], (8, tdet))
                    left = jnp.where(top, picked, 1.0)
                    left = jnp.where(lane < cells_ref[p, r, t, v], left, 0.0).astype(jnp.bfloat16)
                    both += lax.dot_general(
                        left,
                        foot[p, r, t, v],
                        (((1,), (1,)), ((), ())),
                        preferred_element_type=jnp.float32,
                    )
                at = slice(t * tvox, (t + 1) * tvox)
                sums[0, p, r : r + 1, at] = both[0:1]
                sums[1, p, r : r + 1, at] = both[1:2]
    volume = vol_ref[...]
    sart = jnp.maximum(volume + RELAX * (sums[0] / sums[1]), 0.0)
    sart_ref[...] = sart
    gap = sart - volume
    gap_ref[...] = jnp.sum(gap * gap, axis=0)


def back_project(plan, volume, footprint, tile_block, tile_cells, corr):
    shape = footprint.shape
    parts = shape[0] * shape[1]
    return pl.pallas_call(
        functools.partial(back_kernel, plan, shape),
        out_shape=(
            jax.ShapeDtypeStruct(volume.shape, jnp.float32),
            jax.ShapeDtypeStruct(volume.shape[1:], jnp.float32),
        ),
        in_specs=[
            pl.BlockSpec(memory_space=pltpu.VMEM),
            pl.BlockSpec(memory_space=pl.ANY),
            pl.BlockSpec(memory_space=pltpu.SMEM),
            pl.BlockSpec(memory_space=pltpu.SMEM),
            pl.BlockSpec(memory_space=pltpu.VMEM),
        ],
        out_specs=(
            pl.BlockSpec(memory_space=pltpu.VMEM),
            pl.BlockSpec(memory_space=pltpu.VMEM),
        ),
        scratch_shapes=[
            pltpu.VMEM((2,) + volume.shape, jnp.float32),
            pltpu.VMEM(shape, jnp.bfloat16),
            pltpu.SemaphoreType.DMA((parts,)),
        ],
        compiler_params=pltpu.CompilerParams(vmem_limit_bytes=VMEM_BYTES),
        name="back_project",
    )(volume, footprint, tile_block, tile_cells, corr)


def part_of(plan, sums, v):
    size = plan.width[v] * plan.drows
    view = lax.slice_in_dim(sums, plan.base[v], plan.base[v] + size, axis=1)
    return view.reshape(2, plan.drows, plan.width[v], sums.shape[2])


def for_owner(plan, views, owner):
    pieces = []
    for view in views:
        width = view.shape[2]
        flat = view.reshape(2, -1, view.shape[3])
        own = plan.own * width // plan.per_row
        mine = lax.dynamic_slice_in_dim(flat, width + owner * own, own, 1)
        halo = lax.dynamic_slice_in_dim(
            flat, jnp.where(owner == 0, 0, flat.shape[1] - width), width, 1
        )
        pieces += [mine, halo]
    return jnp.concatenate(pieces, axis=1)


def place(plan, chunk, source):
    out, at = [], 0
    for v, width in enumerate(plan.width):
        size = plan.own * width // plan.per_row + width
        piece = lax.slice_in_dim(chunk, at, at + size, axis=1)
        at += size
        if width != plan.per_row:
            piece = piece.reshape(2, -1, width, chunk.shape[2])
            room = jnp.zeros((2, piece.shape[1], plan.per_row + 2, chunk.shape[2]), piece.dtype)
            room = lax.dynamic_update_slice_in_dim(room, piece, plan.narrow * source, 2)
            piece = room[:, :, 1:-1].reshape(2, -1, chunk.shape[2])
        out.append(piece)
    return jnp.stack(out, axis=1)


def total_of(parts):
    axes = ("slab", "xy")
    count = lax.axis_size(axes)
    row = jnp.concatenate(parts, axis=0)
    everyone = lax.all_to_all(jnp.broadcast_to(row[None], (count,) + row.shape), axes, 0, 0)
    return jnp.sum(everyone, axis=(0, 2))


def extended(cells, sides, width):
    for axis, dim in sides:
        head = lax.slice_in_dim(cells, 0, width, axis=dim)
        tail = lax.slice_in_dim(cells, cells.shape[dim] - width, cells.shape[dim], axis=dim)
        place_in = lax.axis_index(axis)
        before = jnp.where(place_in == 0, 0.0, shift_all(tail, axis, 1))
        after = jnp.where(place_in == lax.axis_size(axis) - 1, 0.0, shift_all(head, axis, -1))
        cells = jnp.concatenate([before, cells, after], axis=dim)
    return cells


def tv_slope(padded):
    base = padded[:-1, :-1, :-1]
    diff_a = padded[1:, :-1, :-1] - base
    diff_b = padded[:-1, 1:, :-1] - base
    diff_e = padded[:-1, :-1, 1:] - base
    size = jnp.sqrt(diff_a * diff_a + diff_b * diff_b + diff_e * diff_e + SMOOTHING)
    unit_a = diff_a / size
    unit_b = diff_b / size
    unit_e = diff_e / size
    total = unit_a + unit_b + unit_e
    return -total[1:, 1:, 1:] + unit_a[:-1, 1:, 1:] + unit_b[1:, :-1, 1:] + unit_e[1:, 1:, :-1]


def lanes_of(square):
    return jnp.sum(square.reshape(-1, 128), axis=0, keepdims=True)


def body(volume, footprint, tile_block, tile_cells, measured):
    planes, rows, ycells = volume.shape
    views, tdet = footprint.shape[3], footprint.shape[5]
    slabs, bands = lax.axis_size("slab"), lax.axis_size("xy")
    slab, band = lax.axis_index("slab"), lax.axis_index("xy")
    nblocks = measured.shape[1] // tdet
    plan = Plan(slabs, bands, views, nblocks, tdet)

    packed = project(plan, volume, footprint, tile_block, tile_cells)

    sums = [part_of(plan, packed, v) for v in range(views)]
    edge = 2
    low = jnp.concatenate([view[:, :edge] for view in sums], axis=2)
    high = jnp.concatenate([view[:, -edge:] for view in sums], axis=2)
    from_below = jnp.where(slab == 0, 0.0, shift_all(high, "slab", 1))
    from_above = jnp.where(slab == slabs - 1, 0.0, shift_all(low, "slab", -1))
    at = 0
    for v, width in enumerate(plan.width):
        view = sums[v]
        sums[v] = jnp.concatenate(
            [
                view[:, :edge] + from_below[:, :, at : at + width],
                view[:, edge:-edge],
                view[:, -edge:] + from_above[:, :, at : at + width],
            ],
            axis=1,
        )
        at += width

    total = place(plan, for_owner(plan, sums, band), band)
    for flip in range(1, bands):
        total = total + place(
            plan, swap_all(for_owner(plan, sums, band ^ flip), "xy", flip), band ^ flip
        )
    blocked = measured.reshape(views, nblocks, tdet)
    first = (slab * bands + band) * plan.own
    halo_at = jnp.where(
        band == 0, slab * plan.slab_own - plan.halo, (slab + 1) * plan.slab_own
    )
    seen = jnp.concatenate(
        [
            lax.dynamic_slice_in_dim(blocked, first, plan.own, 1),
            lax.dynamic_slice_in_dim(
                blocked, jnp.clip(halo_at, 0, nblocks - plan.halo), plan.halo, 1
            ),
        ],
        axis=1,
    )
    corrected = (seen - total[0]) / jnp.maximum(total[1], 1.0)
    correction = corrected[:, : plan.own].reshape(views, plan.own * tdet)

    rounded = corrected.astype(jnp.bfloat16)
    wide = jnp.zeros((views, plan.local, tdet), jnp.bfloat16)
    for flip in range(bands):
        piece = rounded if flip == 0 else swap_all(rounded, "xy", flip)
        source = band ^ flip
        wide = lax.dynamic_update_slice_in_dim(
            wide, piece[:, : plan.own], plan.halo + source * plan.own, 1
        )
        end = piece[:, plan.own :]
        wide = wide.at[:, : plan.halo].set(
            jnp.where(source == 0, end, wide[:, : plan.halo])
        )
        wide = wide.at[:, -plan.halo :].set(
            jnp.where(source == bands - 1, end, wide[:, -plan.halo :])
        )

    sart, gap = back_project(
        plan, volume, footprint, tile_block, tile_cells, wide.astype(jnp.float32)
    )

    rimmed = extended(sart, (("slab", 0), ("xy", 1)), 2)
    padded = jnp.pad(rimmed, ((0, 0), (0, 0), (2, 2)))
    slope_wide = tv_slope(padded)
    first_slope = slope_wide[1:-1, 1:-1, 1:-1]
    gap_square, first_square = total_of([lanes_of(gap), lanes_of(first_slope * first_slope)])
    update_norm = jnp.sqrt(gap_square)
    first_step = TV_RATE * update_norm / jnp.sqrt(first_square + 1e-06)
    wide = padded[1:-1, 1:-1, 1:-1] - first_step * slope_wide
    plane_ids = slab * planes + jnp.arange(planes + 2, dtype=jnp.int32) - 1
    row_ids = band * rows + jnp.arange(rows + 2, dtype=jnp.int32) - 1
    cell_ids = jnp.arange(ycells + 2, dtype=jnp.int32) - 1
    inside_plane = (plane_ids >= 0) & (plane_ids < slabs * planes)
    inside_row = (row_ids >= 0) & (row_ids < bands * rows)
    inside_cell = (cell_ids >= 0) & (cell_ids < ycells)
    inside = inside_plane[:, None, None] & inside_row[None, :, None] & inside_cell[None, None, :]
    wide = jnp.where(inside, wide, 0.0)
    second_slope = tv_slope(wide)
    (second_square,) = total_of([lanes_of(second_slope * second_slope)])
    second_step = TV_RATE * update_norm / jnp.sqrt(second_square + 1e-06)
    updated = wide[1:-1, 1:-1, 1:-1] - second_step * second_slope
    return (updated, correction)


def solution(mesh):
    placed = (
        P("slab", "xy", None),
        P("slab", "xy", None, None, None, None),
        P("slab", "xy", None, None),
        P("slab", "xy", None, None),
        P(),
    )
    return jax.shard_map(
        body,
        mesh=mesh,
        in_specs=placed,
        out_specs=(P("slab", "xy", None), P(None, ("slab", "xy"))),
        check_vma=False,
    )
```

time: 290 us -> 87.5 us (0.30)
  waiting for transfers between devices: 141 us -> 28.9 us
  blocking collectives: 82.6 us -> 0 us
  other arithmetic: 21.1 us -> 3.3 us
  starting transfers between devices: 9.17 us -> 26.5 us
  between operations: 16.4 us -> 3.51 us
  Pallas kernels: 0 us -> 11.8 us
  matrix products: 11.7 us -> 0 us
  local copies, waits for them, and re-layouts: 7.55 us -> 13 us
    psum x1 -> x0, waiting for transfers between devices: 136 us -> none  [body(): projected, ray_weight = lax.psum((projected, ray_weight), ('slab', 'xy'))]
    psum x2 -> x0, blocking collectives: 82.6 us -> none  [the longest x1 41.6 us: slope_scale(): return jnp.sqrt(lax.psum(jnp.sum(slope * slope), ('slab', 'xy')) + 1e-06)]
    all_to_all x0 -> x2, waiting for transfers between devices: none -> 13.7 us  [total_of(): lax.all_to_all(jnp.broadcast_to(row[None], (count,) + row.shape), axes, 0...]
    pallas_call x0 -> x2, Pallas kernels: none -> 11.8 us  [the longest x1 6.37 us: back_project(): pl.pallas_call(functools.partial(back_kernel, plan, shape), out_shape=(ja...]
    dot_general x4 -> x0, matrix products: 11.7 us -> none  [the longest x1 5.63 us: body(): jnp.einsum('tvjc,tvc->tj', masked, picked, preferred_element_type=jnp.flo...]
    ppermute x4 -> x12, waiting for transfers between devices: 4.67 us -> 15.2 us  [the longest x6 7.69 us: swap_all(): return lax.ppermute(cells, axis, [(i, i ^ flip) for i in range(count)])]
    ppermute x4 -> x12, starting transfers between devices: 9.13 us -> 19 us  [the longest x6 9.99 us: shift_all(): lax.ppermute(cells, axis, [(i, (i + step) % count) for i in range(count)])]
    all_to_all x0 -> x2, starting transfers between devices: none -> 7.47 us  [total_of(): lax.all_to_all(jnp.broadcast_to(row[None], (count,) + row.shape), axes, 0...]
  transfers between devices with their start and end apart: 5 -> 14, of which waited for: 3 -> 11; matrix products, arithmetic and copies ran while one was open for 0% -> 2% of each run, Pallas kernels for 0% -> 0%
where the time goes in v1:
time: 87.5 us; the launch traced here: 87 us
  waiting for transfers between devices  28.9 us (33%)
  starting transfers between devices  26.5 us (30%)
  local copies, waits for them, and re-layouts  13 us (15%)
  Pallas kernels  11.8 us (13%)
  between operations  3.51 us (4%)
  other arithmetic  3.3 us (4%)
    all_to_all x2, waiting for transfers between devices, total_of(): lax.all_to_all(jnp.broadcast_to(row[None], (count,) + row.shape), axes, 0...  13.7 us
    ppermute x6, starting transfers between devices, shift_all(): lax.ppermute(cells, axis, [(i, (i + step) % count) for i in range(count)])  9.99 us
    unnamed x15, local copies, waits for them, and re-layouts  9.88 us
    ppermute x6, starting transfers between devices, swap_all(): return lax.ppermute(cells, axis, [(i, i ^ flip) for i in range(count)])  9.02 us
    ppermute x6, waiting for transfers between devices, swap_all(): return lax.ppermute(cells, axis, [(i, i ^ flip) for i in range(count)])  7.69 us
    ppermute x6, waiting for transfers between devices, shift_all(): lax.ppermute(cells, axis, [(i, (i + step) % count) for i in range(count)])  7.48 us
    all_to_all x2, starting transfers between devices, total_of(): lax.all_to_all(jnp.broadcast_to(row[None], (count,) + row.shape), axes, 0...  7.47 us
    pallas_call x1, Pallas kernels, back_project(): pl.pallas_call(functools.partial(back_kernel, plan, shape), out_shape=(ja...  6.37 us
  transfers between devices with their start and end apart: 14, of which 11 were waited for; matrix products, arithmetic and copies ran while one was open for 2% of the time, Pallas kernels for 0%

profile of v1, /device:TPU:0, one launch (start us, length us, event | category | flops | bytes accessed | tf_op | source)
XLA Modules:
  0.0 87.0 jit_solution(15646785141097063913)
XLA Ops:
  0.6 0.8 copy.49.block_ref
  1.4 0.8 copy.50.cells_ref
  2.3 3.4 %copy-done = bf16[2,8,4,2,128,256]{5,4,3,2,1,0:T(8,128)(2,1)S(1)} copy-done((bf16[2,8,4,2,128,256]{5,4,3,2,1,0:T(8,128)(2,1)S(1)}, bf16[2,8,4,2,128,256]{5,4,3,2,1,0:T(8,128)(2,1)}, u32[]{:S(2)}) %copy-start) | copy-done | bytes 8388632
  5.7 0.8 copy-done.2
  6.4 5.5 %project.1 = f32[2,120,256]{2,1,0:T(8,128)S(1)} custom-call(f32[2,8,512]{2,1,0:T(8,128)S(1)} %copy-done.2, bf16[2,8,4,2,128,256]{5,4,3,2,1,0:T(8,128)(2,1)S(1)} %copy-done, s32[2,8,4,2]{3,2,1,0:T(4,128)S(1)} %copy.49.block_ref, s32[2,8,4,2]{3,2,1,0:T(4,128)S(1)} %copy.50.cells_ref), custom_call_target="tpu_custom_call" | custom-call | tf_op jit(solution)/shard_map/project/pallas_call | solution.py:94
  12.0 3.4 %collective-permute-start.1 = (f32[2,2,12,256]{3,2,1,0:T(8,128)S(1)}, f32[2,2,12,256]{3,2,1,0:T(8,128)S(1)}, u32[]{:S(2)}, u32[]{:S(2)}) collective-permute-start(f32[2,2,12,256]{3,2,1,0:T(8,128)S(1)} %pad_maximum_fusion.5), channel_id=1, source_target_pairs={{0,28},{4,0},{8,4},{12,8},{16,12},{20,16},{24,20},{28,24},{1,29},{... | collective-permute-start | bytes 147464 | tf_op jit(solution)/shard_map/ppermute | solution.py:41
  15.7 1.5 %collective-permute-done.1 = f32[2,2,12,256]{3,2,1,0:T(8,128)S(1)} collective-permute-done((f32[2,2,12,256]{3,2,1,0:T(8,128)S(1)}, f32[2,2,12,256]{3,2,1,0:T(8,128)S(1)}, u32[]{:S(2)}, u32[]{:S(2)}) %collective-permute-start.1) | collective-permute-done | bytes 49184 | tf_op jit(solution)/shard_map/ppermute | solution.py:41
  17.3 2.7 %collective-permute-done = f32[2,2,12,256]{3,2,1,0:T(8,128)S(1)} collective-permute-done((f32[2,2,12,256]{3,2,1,0:T(8,128)S(1)}, f32[2,2,12,256]{3,2,1,0:T(8,128)S(1)}, u32[]{:S(2)}, u32[]{:S(2)}) %collective-permute-start) | collective-permute-done | bytes 49184 | tf_op jit(solution)/shard_map/ppermute | solution.py:41
  20.2 2.7 %collective-permute-start.3 = (f32[2,36,256]{2,1,0:T(8,128)S(1)}, f32[2,36,256]{2,1,0:T(8,128)S(1)}, u32[]{:S(2)}, u32[]{:S(2)}) collective-permute-start(f32[2,36,256]{2,1,0:T(8,128)S(1)} %pad_maximum_fusion.2), channel_id=1, source_target_pairs={{0,2},{1,3},{2,0},{3,1},{4,6},{5,7},{6,4},{7,5},{8,10},{9,11},{10,... | collective-permute-start | bytes 221192 | tf_op jit(solution)/shard_map/ppermute | solution.py:46
  22.9 1.6 %collective-permute-start.2 = (f32[2,36,256]{2,1,0:T(8,128)S(1)}, f32[2,36,256]{2,1,0:T(8,128)S(1)}, u32[]{:S(2)}, u32[]{:S(2)}) collective-permute-start(f32[2,36,256]{2,1,0:T(8,128)S(1)} %pad_maximum_fusion.1), channel_id=1, source_target_pairs={{0,1},{1,0},{2,3},{3,2},{4,5},{5,4},{6,7},{7,6},{8,9},{9,8},{10,11... | collective-permute-start | bytes 221192 | tf_op jit(solution)/shard_map/ppermute | solution.py:46
  25.2 0.5 collective-permute-done.3
  26.0 2.0 %collective-permute-done.2 = f32[2,36,256]{2,1,0:T(8,128)S(1)} collective-permute-done((f32[2,36,256]{2,1,0:T(8,128)S(1)}, f32[2,36,256]{2,1,0:T(8,128)S(1)}, u32[]{:S(2)}, u32[]{:S(2)}) %collective-permute-start.2) | collective-permute-done | bytes 73760 | tf_op jit(solution)/shard_map/ppermute | solution.py:46
  28.2 3.0 %collective-permute-done.4 = f32[2,36,256]{2,1,0:T(8,128)S(1)} collective-permute-done((f32[2,36,256]{2,1,0:T(8,128)S(1)}, f32[2,36,256]{2,1,0:T(8,128)S(1)}, u32[]{:S(2)}, u32[]{:S(2)}) %collective-permute-start.4) | collective-permute-done | bytes 73760 | tf_op jit(solution)/shard_map/ppermute | solution.py:46
  31.7 1.1 %collective-permute-start.6 = (bf16[2,24,256]{2,1,0:T(8,128)(2,1)S(1)}, bf16[2,24,256]{2,1,0:T(8,128)(2,1)S(1)}, u32[]{:S(2)}, u32[]{:S(2)}) collective-permute-start(bf16[2,24,256]{2,1,0:T(8,128)(2,1)S(1)} %get-tuple-element.108), channel_id=1, source_target_pairs={{0,2},{1,3},{2,0},{3,1},{4,6},{5,7},{6,4},{7,5},{8,10},{9,11},{10,... | collective-permute-start | bytes 73736 | tf_op jit(solution)/shard_map/ppermute | solution.py:46
  32.8 3.3 %collective-permute-start.7 = (bf16[2,24,256]{2,1,0:T(8,128)(2,1)S(1)}, bf16[2,24,256]{2,1,0:T(8,128)(2,1)S(1)}, u32[]{:S(2)}, u32[]{:S(2)}) collective-permute-start(bf16[2,24,256]{2,1,0:T(8,128)(2,1)S(1)} %get-tuple-element.108), channel_id=1, source_target_pairs={{0,3},{1,2},{2,1},{3,0},{4,7},{5,6},{6,5},{7,4},{8,11},{9,10},{10,... | collective-permute-start | bytes 73736 | tf_op jit(solution)/shard_map/ppermute | solution.py:46
  36.5 1.9 %collective-permute-done.7 = bf16[2,24,256]{2,1,0:T(8,128)(2,1)S(1)} collective-permute-done((bf16[2,24,256]{2,1,0:T(8,128)(2,1)S(1)}, bf16[2,24,256]{2,1,0:T(8,128)(2,1)S(1)}, u32[]{:S(2)}, u32[]{:S(2)}) %collective-permute-start.7) | collective-permute-done | bytes 24608 | tf_op jit(solution)/shard_map/ppermute | solution.py:46
  38.5 3.4 %copy-done.1 = bf16[2,8,4,2,128,256]{5,4,3,2,1,0:T(8,128)(2,1)S(1)} copy-done((bf16[2,8,4,2,128,256]{5,4,3,2,1,0:T(8,128)(2,1)S(1)}, bf16[2,8,4,2,128,256]{5,4,3,2,1,0:T(8,128)(2,1)}, u32[]{:S(2)}) %copy-start.1) | copy-done | bytes 8388632
  41.9 6.4 %back_project.1 = (f32[2,8,512]{2,1,0:T(8,128)S(1)}, f32[8,512]{1,0:T(8,128)S(1)}) custom-call(f32[2,8,512]{2,1,0:T(8,128)S(1)} %copy-done.3, bf16[2,8,4,2,128,256]{5,4,3,2,1,0:T(8,128)(2,1)S(1)} %copy-done.1, s32[2,8,4,2]{3,2,1,0:T(4,128)S(1)} %copy.49.block_ref, s32[2,8,4,2]{3,2,1,0:T(4,128)S(1)} %copy.50.cells_ref, ...), custom_call_target="tpu_custom_call" | custom-call | tf_op jit(solution)/shard_map/back_project/pallas_call | solution.py:162
  48.3 2.6 %collective-permute-start.9 = (f32[2,8,512]{2,1,0:T(8,128)S(1)}, f32[2,8,512]{2,1,0:T(8,128)S(1)}, u32[]{:S(2)}, u32[]{:S(2)}) collective-permute-start(f32[2,8,512]{2,1,0:T(8,128)S(1)} %get-tuple-element.100), channel_id=1, source_target_pairs={{0,28},{4,0},{8,4},{12,8},{16,12},{20,16},{24,20},{28,24},{1,29},{... | collective-permute-start | bytes 98312 | tf_op jit(solution)/shard_map/ppermute | solution.py:41
  51.0 1.6 %collective-permute-done.8 = f32[2,8,512]{2,1,0:T(8,128)S(1)} collective-permute-done((f32[2,8,512]{2,1,0:T(8,128)S(1)}, f32[2,8,512]{2,1,0:T(8,128)S(1)}, u32[]{:S(2)}, u32[]{:S(2)}) %collective-permute-start.8) | collective-permute-done | bytes 32800 | tf_op jit(solution)/shard_map/ppermute | solution.py:41
  52.8 3.8 %collective-permute-start.11 = (f32[6,2,512]{2,1,0:T(2,128)S(1)}, f32[6,2,512]{2,1,0:T(2,128)S(1)}, u32[]{:S(2)}, u32[]{:S(2)}) collective-permute-start(f32[6,2,512]{2,1,0:T(2,128)S(1)} %get-tuple-element.127), channel_id=1, source_target_pairs={{0,3},{1,0},{2,1},{3,2},{4,7},{5,4},{6,5},{7,6},{8,11},{9,8},{10,9... | collective-permute-start | bytes 73736 | tf_op jit(solution)/shard_map/ppermute | solution.py:41
  56.6 1.7 %collective-permute-done.10 = f32[6,2,512]{2,1,0:T(2,128)S(1)} collective-permute-done((f32[6,2,512]{2,1,0:T(2,128)S(1)}, f32[6,2,512]{2,1,0:T(2,128)S(1)}, u32[]{:S(2)}, u32[]{:S(2)}) %collective-permute-start.10) | collective-permute-done | bytes 24608 | tf_op jit(solution)/shard_map/ppermute | solution.py:41
  59.3 0.6 broadcast_in_dim.48
  59.9 4.9 %all-to-all-start = ((f32[32,2,128]{2,1,0:T(2,128)}), f32[32,2,128]{2,1,0:T(2,128)S(1)}, u32[]{:S(2)}, u32[]{:S(2)}) async-start(f32[32,2,128]{2,1,0:T(2,128)} %broadcast_in_dim.48), calls=%async_computation | async-start | bytes 65536 | tf_op jit(solution)/shard_map/all_to_all | solution.py:228
  64.8 7.3 %all-to-all-done = f32[32,2,128]{2,1,0:T(2,128)S(1)} async-done(((f32[32,2,128]{2,1,0:T(2,128)}), f32[32,2,128]{2,1,0:T(2,128)S(1)}, u32[]{:S(2)}, u32[]{:S(2)}) %all-to-all-start) | async-done | bytes 32800 | tf_op jit(solution)/shard_map/all_to_all | solution.py:228
  72.3 0.6 fusion.30
  74.8 0.6 broadcast_in_dim.50
  75.4 2.5 %all-to-all-start.1 = ((f32[32,1,128]{2,1,0:T(1,128)}), f32[32,1,128]{2,1,0:T(1,128)S(1)}, u32[]{:S(2)}, u32[]{:S(2)}) async-start(f32[32,1,128]{2,1,0:T(1,128)} %broadcast_in_dim.50), calls=%async_computation.1 | async-start | bytes 32768 | tf_op jit(solution)/shard_map/all_to_all | solution.py:228
  78.0 0.6 copy.57
  78.6 6.4 %all-to-all-done.1 = f32[32,1,128]{2,1,0:T(1,128)S(1)} async-done(((f32[32,1,128]{2,1,0:T(1,128)}), f32[32,1,128]{2,1,0:T(1,128)S(1)}, u32[]{:S(2)}, u32[]{:S(2)}) %all-to-all-start.1) | async-done | bytes 16416 | tf_op jit(solution)/shard_map/all_to_all | solution.py:228
  85.0 0.6 reduce_sum.49
  86.3 0.7 slice_subtract_fusion.7
  (112 shorter events, 4.3 us)
Async XLA Ops:
  2.3 3.4 %copy-start = (bf16[2,8,4,2,128,256]{5,4,3,2,1,0:T(8,128)(2,1)S(1)}, bf16[2,8,4,2,128,256]{5,4,3,2,1,0:T(8,128)(2,1)}, u32[]{:S(2)}) copy-start(bf16[2,8,4,2,128,256]{5,4,3,2,1,0:T(8,128)(2,1)} %foot_ref.3) | copy-start | bytes 25165828
  5.6 0.8 copy-start.2
  6.4 9.0 %copy-start.4 = (f32[2,131072]{1,0:T(2,128)S(1)}, f32[2,131072]{1,0:T(2,128)}, u32[]{:S(2)}) copy-start(f32[2,131072]{1,0:T(2,128)} %param.25) | copy-start | bytes 3145732
  6.4 32.1 %copy-start.3 = (f32[2,8,512]{2,1,0:T(8,128)S(1)}, f32[2,8,512]{2,1,0:T(8,128)}, u32[]{:S(2)}) copy-start(f32[2,8,512]{2,1,0:T(8,128)} %vol_ref.3) | copy-start | bytes 98308
  12.0 5.3 %collective-permute-start.1 = (f32[2,2,12,256]{3,2,1,0:T(8,128)S(1)}, f32[2,2,12,256]{3,2,1,0:T(8,128)S(1)}, u32[]{:S(2)}, u32[]{:S(2)}) collective-permute-start(f32[2,2,12,256]{3,2,1,0:T(8,128)S(1)} %pad_maximum_fusion.5), channel_id=1, source_target_pairs={{0,28},{4,0},{8,4},{12,8},{16,12},{20,16},{24,20},{28,24},{1,29},{... | collective-permute-start | bytes 147464 | tf_op jit(solution)/shard_map/ppermute | solution.py:41
  15.4 4.6 %collective-permute-start = (f32[2,2,12,256]{3,2,1,0:T(8,128)S(1)}, f32[2,2,12,256]{3,2,1,0:T(8,128)S(1)}, u32[]{:S(2)}, u32[]{:S(2)}) collective-permute-start(f32[2,2,12,256]{3,2,1,0:T(8,128)S(1)} %pad_maximum_fusion.4), channel_id=1, source_target_pairs={{0,4},{4,8},{8,12},{12,16},{16,20},{20,24},{24,28},{28,0},{1,5},{5... | collective-permute-start | bytes 147464 | tf_op jit(solution)/shard_map/ppermute | solution.py:41
  20.2 5.5 %collective-permute-start.3 = (f32[2,36,256]{2,1,0:T(8,128)S(1)}, f32[2,36,256]{2,1,0:T(8,128)S(1)}, u32[]{:S(2)}, u32[]{:S(2)}) collective-permute-start(f32[2,36,256]{2,1,0:T(8,128)S(1)} %pad_maximum_fusion.2), channel_id=1, source_target_pairs={{0,2},{1,3},{2,0},{3,1},{4,6},{5,7},{6,4},{7,5},{8,10},{9,11},{10,... | collective-permute-start | bytes 221192 | tf_op jit(solution)/shard_map/ppermute | solution.py:46
  22.9 5.0 %collective-permute-start.2 = (f32[2,36,256]{2,1,0:T(8,128)S(1)}, f32[2,36,256]{2,1,0:T(8,128)S(1)}, u32[]{:S(2)}, u32[]{:S(2)}) collective-permute-start(f32[2,36,256]{2,1,0:T(8,128)S(1)} %pad_maximum_fusion.1), channel_id=1, source_target_pairs={{0,1},{1,0},{2,3},{3,2},{4,5},{5,4},{6,7},{7,6},{8,9},{9,8},{10,11... | collective-permute-start | bytes 221192 | tf_op jit(solution)/shard_map/ppermute | solution.py:46
  24.9 6.4 %collective-permute-start.4 = (f32[2,36,256]{2,1,0:T(8,128)S(1)}, f32[2,36,256]{2,1,0:T(8,128)S(1)}, u32[]{:S(2)}, u32[]{:S(2)}) collective-permute-start(f32[2,36,256]{2,1,0:T(8,128)S(1)} %pad_maximum_fusion.3), channel_id=1, source_target_pairs={{0,3},{1,2},{2,1},{3,0},{4,7},{5,6},{6,5},{7,4},{8,11},{9,10},{10,... | collective-permute-start | bytes 221192 | tf_op jit(solution)/shard_map/ppermute | solution.py:46
  31.6 4.5 %collective-permute-start.5 = (bf16[2,24,256]{2,1,0:T(8,128)(2,1)S(1)}, bf16[2,24,256]{2,1,0:T(8,128)(2,1)S(1)}, u32[]{:S(2)}, u32[]{:S(2)}) collective-permute-start(bf16[2,24,256]{2,1,0:T(8,128)(2,1)S(1)} %get-tuple-element.108), channel_id=1, source_target_pairs={{0,1},{1,0},{2,3},{3,2},{4,5},{5,4},{6,7},{7,6},{8,9},{9,8},{10,11... | collective-permute-start | bytes 73736 | tf_op jit(solution)/shard_map/ppermute | solution.py:46
  31.7 4.8 %collective-permute-start.6 = (bf16[2,24,256]{2,1,0:T(8,128)(2,1)S(1)}, bf16[2,24,256]{2,1,0:T(8,128)(2,1)S(1)}, u32[]{:S(2)}, u32[]{:S(2)}) collective-permute-start(bf16[2,24,256]{2,1,0:T(8,128)(2,1)S(1)} %get-tuple-element.108), channel_id=1, source_target_pairs={{0,2},{1,3},{2,0},{3,1},{4,6},{5,7},{6,4},{7,5},{8,10},{9,11},{10,... | collective-permute-start | bytes 73736 | tf_op jit(solution)/shard_map/ppermute | solution.py:46
  32.8 5.6 %collective-permute-start.7 = (bf16[2,24,256]{2,1,0:T(8,128)(2,1)S(1)}, bf16[2,24,256]{2,1,0:T(8,128)(2,1)S(1)}, u32[]{:S(2)}, u32[]{:S(2)}) collective-permute-start(bf16[2,24,256]{2,1,0:T(8,128)(2,1)S(1)} %get-tuple-element.108), channel_id=1, source_target_pairs={{0,3},{1,2},{2,1},{3,0},{4,7},{5,6},{6,5},{7,4},{8,11},{9,10},{10,... | collective-permute-start | bytes 73736 | tf_op jit(solution)/shard_map/ppermute | solution.py:46
  38.5 3.4 %copy-start.1 = (bf16[2,8,4,2,128,256]{5,4,3,2,1,0:T(8,128)(2,1)S(1)}, bf16[2,8,4,2,128,256]{5,4,3,2,1,0:T(8,128)(2,1)}, u32[]{:S(2)}) copy-start(bf16[2,8,4,2,128,256]{5,4,3,2,1,0:T(8,128)(2,1)} %foot_ref.3) | copy-start | bytes 25165828
  48.2 4.3 %collective-permute-start.8 = (f32[2,8,512]{2,1,0:T(8,128)S(1)}, f32[2,8,512]{2,1,0:T(8,128)S(1)}, u32[]{:S(2)}, u32[]{:S(2)}) collective-permute-start(f32[2,8,512]{2,1,0:T(8,128)S(1)} %get-tuple-element.100), channel_id=1, source_target_pairs={{0,4},{4,8},{8,12},{12,16},{16,20},{20,24},{24,28},{28,0},{1,5},{5... | collective-permute-start | bytes 98312 | tf_op jit(solution)/shard_map/ppermute | solution.py:41
  48.3 4.2 %collective-permute-start.9 = (f32[2,8,512]{2,1,0:T(8,128)S(1)}, f32[2,8,512]{2,1,0:T(8,128)S(1)}, u32[]{:S(2)}, u32[]{:S(2)}) collective-permute-start(f32[2,8,512]{2,1,0:T(8,128)S(1)} %get-tuple-element.100), channel_id=1, source_target_pairs={{0,28},{4,0},{8,4},{12,8},{16,12},{20,16},{24,20},{28,24},{1,29},{... | collective-permute-start | bytes 98312 | tf_op jit(solution)/shard_map/ppermute | solution.py:41
  52.6 5.7 %collective-permute-start.10 = (f32[6,2,512]{2,1,0:T(2,128)S(1)}, f32[6,2,512]{2,1,0:T(2,128)S(1)}, u32[]{:S(2)}, u32[]{:S(2)}) collective-permute-start(f32[6,2,512]{2,1,0:T(2,128)S(1)} %get-tuple-element.126), channel_id=1, source_target_pairs={{0,1},{1,2},{2,3},{3,0},{4,5},{5,6},{6,7},{7,4},{8,9},{9,10},{10,1... | collective-permute-start | bytes 73736 | tf_op jit(solution)/shard_map/ppermute | solution.py:41
  52.8 5.5 %collective-permute-start.11 = (f32[6,2,512]{2,1,0:T(2,128)S(1)}, f32[6,2,512]{2,1,0:T(2,128)S(1)}, u32[]{:S(2)}, u32[]{:S(2)}) collective-permute-start(f32[6,2,512]{2,1,0:T(2,128)S(1)} %get-tuple-element.127), channel_id=1, source_target_pairs={{0,3},{1,0},{2,1},{3,2},{4,7},{5,4},{6,5},{7,6},{8,11},{9,8},{10,9... | collective-permute-start | bytes 73736 | tf_op jit(solution)/shard_map/ppermute | solution.py:41
  59.9 12.2 %all-to-all-start = ((f32[32,2,128]{2,1,0:T(2,128)}), f32[32,2,128]{2,1,0:T(2,128)S(1)}, u32[]{:S(2)}, u32[]{:S(2)}) async-start(f32[32,2,128]{2,1,0:T(2,128)} %broadcast_in_dim.48), calls=%async_computation | async-start | bytes 65536 | tf_op jit(solution)/shard_map/all_to_all | solution.py:228
  75.4 9.6 %all-to-all-start.1 = ((f32[32,1,128]{2,1,0:T(1,128)}), f32[32,1,128]{2,1,0:T(1,128)S(1)}, u32[]{:S(2)}, u32[]{:S(2)}) async-start(f32[32,1,128]{2,1,0:T(1,128)} %broadcast_in_dim.50), calls=%async_computation.1 | async-start | bytes 32768 | tf_op jit(solution)/shard_map/all_to_all | solution.py:228

commit v2 on v0

v2 whole, which is shorter than its diff:
```python
import functools

import jax
import jax.numpy as jnp
from jax import lax
from jax.experimental import pallas as pl
from jax.experimental.pallas import tpu as pltpu
from jax.sharding import PartitionSpec as P

RELAX = 1.0
TV_RATE = 0.8
SMOOTHING = 0.01
DCOLS = 2048
VMEM_BYTES = 32 * 1024 * 1024


class Plan:
    def __init__(self, slabs, bands, views, nblocks, tdet):
        self.slabs, self.bands, self.views, self.tdet = slabs, bands, views, tdet
        per_row = DCOLS // tdet
        own = nblocks // (slabs * bands)
        self.slab_own = nblocks // slabs
        self.halo = per_row
        self.unit = min(per_row, own)
        self.own_units = own // self.unit
        self.halo_units = per_row // self.unit
        self.units = self.slab_own // self.unit + 2 * self.halo_units
        self.chunk = self.own_units + self.halo_units
        narrow = per_row // bands
        fits = self.unit == per_row and narrow * bands == per_row and narrow + 2 < per_row
        self.narrow = narrow if fits else 0
        self.width = [
            self.narrow + 2 if v % 2 and self.narrow else self.unit for v in range(views)
        ]
        self.base = [2 * sum(self.width[:v]) for v in range(views)]
        self.lines = 2 * sum(self.width)

    def is_narrow(self, v):
        return self.width[v] != self.unit


def shift_all(cells, axis, step):
    count = lax.axis_size(axis)
    return lax.ppermute(cells, axis, [(i, (i + step) % count) for i in range(count)])


def swap_all(cells, axis, flip):
    count = lax.axis_size(axis)
    return lax.ppermute(cells, axis, [(i, i ^ flip) for i in range(count)])


def unit_of(plan, block, slab):
    local = jnp.clip(
        block - slab * plan.slab_own + plan.halo, 0, plan.units * plan.unit - 1
    )
    return lax.div(local, plan.unit), lax.rem(local, plan.unit)


def copy_all(pairs, sems):
    return [pltpu.make_async_copy(src, dst, sems.at[n]) for n, (src, dst) in enumerate(pairs)]


def project_kernel(
    plan, shape, vol_hbm, foot_hbm, block_hbm, cells_hbm, seen_hbm,
    out_ref, low_ref, high_ref, seen_ref, foot, acc, vol_ref, block_ref, cells_ref, seen, sems, small,
):
    planes, rows, tiles, views, tvox, tdet = shape
    slab, band = lax.axis_index("slab"), lax.axis_index("xy")
    parts = sems.shape[0]
    step = planes * rows // parts
    spans = [(n * step // rows, pl.ds(n * step % rows, step)) for n in range(parts)]
    span = plan.unit * tdet
    own_at = (slab * plan.bands + band) * plan.own_units
    halo_at = jnp.where(
        band == 0,
        slab * (plan.slab_own // plan.unit) - plan.halo_units,
        (slab + 1) * (plan.slab_own // plan.unit),
    )
    halo_at = jnp.clip(halo_at, 0, seen_hbm.shape[1] // span - plan.halo_units)
    own_at, halo_at = (pl.multiple_of(at * span, span) for at in (own_at, halo_at))
    own_size, halo_size = plan.own_units * span, plan.halo_units * span
    first = copy_all(
        [
            (block_hbm, block_ref),
            (cells_hbm, cells_ref),
            (vol_hbm, vol_ref),
            (seen_hbm.at[:, pl.ds(own_at, own_size)], seen.at[:, pl.ds(0, own_size)]),
            (seen_hbm.at[:, pl.ds(halo_at, halo_size)], seen.at[:, pl.ds(own_size, halo_size)]),
        ],
        small,
    )
    stream = copy_all([(foot_hbm.at[p, at], foot.at[p, at]) for p, at in spans], sems)
    for copy in first + stream:
        copy.start()
    acc[...] = jnp.zeros_like(acc)
    top = lax.broadcasted_iota(jnp.int32, (8, tvox), 0) == 0
    lane = lax.broadcasted_iota(jnp.int32, (8, tdet), 1)
    for copy in first:
        copy.wait()
    for v in range(views):
        for i in range(plan.chunk):
            for c in range(plan.unit):
                at = (i * plan.unit + c) * tdet
                seen_ref[v, i, c : c + 1, :] = seen[v : v + 1, at : at + tdet]
    starts = [plan.units * sum(plan.width[:v]) for v in range(views)]
    for n in range(parts):
        stream[n].wait()
        for p, r in [divmod(n * step + k, rows) for k in range(step)]:
            for t in range(tiles):
                voxels = vol_ref[p, r : r + 1, t * tvox : (t + 1) * tvox]
                left = jnp.where(top, jnp.broadcast_to(voxels, (8, tvox)), 1.0)
                left = left.astype(jnp.bfloat16)
                for v in range(views):
                    sums = jnp.dot(left, foot[p, r, t, v], preferred_element_type=jnp.float32)
                    sums = jnp.where(lane < cells_ref[p, t, v, r], sums, 0.0)
                    unit, column = unit_of(plan, block_ref[p, t, v, r], slab)
                    if plan.is_narrow(v):
                        column = column - (band * plan.narrow - 1)
                        column = jnp.clip(column, 0, plan.width[v] - 1)
                    acc[starts[v] + unit * plan.width[v] + column] += sums
    for unit in range(plan.units):
        for v in range(views):
            width = plan.width[v]
            at = starts[v] + unit * width
            for q in range(2):
                line = plan.base[v] + q * width
                out_ref[unit, line : line + width, :] = acc[at : at + width, q, :]
    edge = 2 * plan.halo_units
    low_ref[...] = out_ref[:edge]
    high_ref[...] = out_ref[plan.units - edge :]


def in_vmem(count):
    return [pl.BlockSpec(memory_space=pltpu.VMEM)] * count


def project(plan, volume, footprint, tile_block, tile_cells, measured):
    shape = footprint.shape
    planes, rows = shape[:2]
    views, tdet = plan.views, plan.tdet
    parts = 2 * planes if rows % 2 == 0 else planes
    operands = [
        pltpu.with_memory_space_constraint(operand, pltpu.HBM)
        for operand in (volume, footprint, tile_block, tile_cells, measured)
    ]
    border = (2 * plan.halo_units, plan.lines, tdet)
    return pl.pallas_call(
        functools.partial(project_kernel, plan, shape),
        out_shape=(
            jax.ShapeDtypeStruct((plan.units, plan.lines, tdet), jnp.float32),
            jax.ShapeDtypeStruct(border, jnp.float32),
            jax.ShapeDtypeStruct(border, jnp.float32),
            jax.ShapeDtypeStruct((views, plan.chunk, plan.unit, tdet), jnp.float32),
            pltpu.VMEM(shape, jnp.bfloat16),
        ),
        in_specs=[pl.BlockSpec(memory_space=pltpu.HBM)] * 5,
        out_specs=tuple(in_vmem(5)),
        scratch_shapes=[
            pltpu.VMEM((plan.units * sum(plan.width), 8, tdet), jnp.float32),
            pltpu.VMEM(volume.shape, jnp.float32),
            pltpu.SMEM(tile_block.shape, jnp.int32),
            pltpu.SMEM(tile_cells.shape, jnp.int32),
            pltpu.VMEM((views, plan.chunk * plan.unit * tdet), jnp.float32),
            pltpu.SemaphoreType.DMA((parts,)),
            pltpu.SemaphoreType.DMA((5,)),
        ],
        compiler_params=pltpu.CompilerParams(vmem_limit_bytes=VMEM_BYTES),
        name="project",
    )(*operands)


def share_kernel(plan, packed_ref, below_ref, above_ref, *rest):
    out_refs, total = rest[:-1], rest[-1]
    slab, band = lax.axis_index("slab"), lax.axis_index("xy")
    edge = 2 * plan.halo_units
    total[...] = packed_ref[...]
    total[:edge] += jnp.where(slab == 0, 0.0, below_ref[...])
    total[plan.units - edge :] += jnp.where(slab == plan.slabs - 1, 0.0, above_ref[...])
    for flip, out_ref in enumerate(out_refs):
        owner = band ^ flip
        for i in range(plan.own_units):
            out_ref[i] = total[plan.halo_units + owner * plan.own_units + i]
        halo = jnp.where(owner == 0, 0, plan.units - plan.halo_units)
        for i in range(plan.halo_units):
            out_ref[plan.own_units + i] = total[halo + i]


def shares(plan, packed, below, above):
    chunk = jax.ShapeDtypeStruct((plan.chunk,) + packed.shape[1:], jnp.float32)
    return pl.pallas_call(
        functools.partial(share_kernel, plan),
        out_shape=(chunk,) * plan.bands,
        in_specs=in_vmem(3),
        out_specs=tuple(in_vmem(plan.bands)),
        scratch_shapes=[pltpu.VMEM(packed.shape, jnp.float32)],
        compiler_params=pltpu.CompilerParams(vmem_limit_bytes=VMEM_BYTES // 4),
        name="shares",
    )(packed, below, above)


def correct_kernel(plan, seen_ref, *rest):
    parts, (exact_ref, rounded_ref) = rest[:-2], rest[-2:]
    band = lax.axis_index("xy")
    tdet, unit = plan.tdet, plan.unit
    rounded = []
    for v in range(plan.views):
        width = plan.width[v]
        for i in range(plan.chunk):
            sums = []
            for q in range(2):
                line = plan.base[v] + q * width
                total = 0.0
                for flip, part in enumerate(parts):
                    piece = part[i, line : line + width, :]
                    if plan.is_narrow(v):
                        room = jnp.zeros((unit - width, tdet), jnp.float32)
                        piece = jnp.concatenate([piece, room], axis=0)
                        first = (band ^ flip) * plan.narrow - 1
                        piece = pltpu.roll(piece, lax.rem(first + unit, unit), 0)
                    total = total + piece
                sums.append(total)
            corrected = (seen_ref[v, i] - sums[0]) / jnp.maximum(sums[1], 1.0)
            rounded.append(corrected)
            if i < plan.own_units:
                for c in range(unit):
                    at = (i * unit + c) * tdet
                    exact_ref[v : v + 1, at : at + tdet] = corrected[c : c + 1]
    rounded_ref[...] = jnp.concatenate(rounded, axis=0).astype(jnp.bfloat16)


def correct(plan, seen, parts):
    views, chunk, unit, tdet = seen.shape
    return pl.pallas_call(
        functools.partial(correct_kernel, plan),
        out_shape=(
            jax.ShapeDtypeStruct((views, plan.own_units * unit * tdet), jnp.float32),
            jax.ShapeDtypeStruct((views * chunk * unit, tdet), jnp.bfloat16),
        ),
        in_specs=in_vmem(1 + len(parts)),
        out_specs=tuple(in_vmem(2)),
        compiler_params=pltpu.CompilerParams(vmem_limit_bytes=VMEM_BYTES // 4),
        name="correct",
    )(seen, *parts)


def back_kernel(plan, shape, vol_any, foot, block_any, cells_any, *rest):
    parts, (out_ref, sums, corr, vol_ref, block_ref, cells_ref, small) = rest[:-7], rest[-7:]
    planes, rows, tiles, views, tvox, tdet = shape
    slab, band = lax.axis_index("slab"), lax.axis_index("xy")
    first = copy_all([(block_any, block_ref), (cells_any, cells_ref), (vol_any, vol_ref)], small)
    for copy in first:
        copy.start()
    for flip, part in enumerate(parts):
        source = band ^ flip
        piece = part[...].astype(jnp.float32).reshape(views, plan.chunk, plan.unit, tdet)
        halo = jnp.where(
            source == 0,
            0,
            jnp.where(source == plan.bands - 1, plan.units - plan.halo_units, plan.units),
        )
        for v in range(views):
            for i in range(plan.own_units):
                corr[v, plan.halo_units + source * plan.own_units + i] = piece[v, i]
            for i in range(plan.halo_units):
                corr[v, halo + i] = piece[v, plan.own_units + i]
    top = lax.broadcasted_iota(jnp.int32, (8, tdet), 0) == 0
    lane = lax.broadcasted_iota(jnp.int32, (8, tdet), 1)
    for copy in first:
        copy.wait()
    gap_sum = jnp.zeros((rows, tvox), jnp.float32)
    for p in range(planes):
        for t in range(tiles):
            for r in range(rows):
                both = 0.0
                for v in range(views):
                    unit, column = unit_of(plan, block_ref[p, t, v, r], slab)
                    picked = jnp.broadcast_to(corr[v, unit, pl.ds(column, 1), :], (8, tdet))
                    left = jnp.where(top, picked, 1.0)
                    left = jnp.where(lane < cells_ref[p, t, v, r], left, 0.0).astype(jnp.bfloat16)
                    both += lax.dot_general(
                        left,
                        foot[p, r, t, v],
                        (((1,), (1,)), ((), ())),
                        preferred_element_type=jnp.float32,
                    )
                sums[0, r : r + 1] = both[0:1]
                sums[1, r : r + 1] = both[1:2]
            volume = vol_ref[p, :, t * tvox : (t + 1) * tvox]
            sart = jnp.maximum(volume + RELAX * (sums[0] / sums[1]), 0.0)
            out_ref[p * tiles + t] = sart
            gap = sart - volume
            gap_sum += gap * gap
    out_ref[planes * tiles] = gap_sum


def back_project(plan, volume, footprint, tile_block, tile_cells, parts):
    shape = footprint.shape
    planes, rows, tiles, views, tvox, tdet = shape
    spaces = [pl.ANY, pltpu.VMEM, pl.ANY, pl.ANY] + [pltpu.VMEM] * len(parts)
    footprint = pltpu.with_memory_space_constraint(footprint, pltpu.VMEM)
    return pl.pallas_call(
        functools.partial(back_kernel, plan, shape),
        out_shape=jax.ShapeDtypeStruct((planes * tiles + 1, rows, tvox), jnp.float32),
        in_specs=[pl.BlockSpec(memory_space=space) for space in spaces],
        out_specs=pl.BlockSpec(memory_space=pltpu.VMEM),
        scratch_shapes=[
            pltpu.VMEM((2, rows, tvox), jnp.float32),
            pltpu.VMEM((views, plan.units + plan.halo_units, plan.unit, tdet), jnp.float32),
            pltpu.VMEM(volume.shape, jnp.float32),
            pltpu.SMEM(tile_block.shape, jnp.int32),
            pltpu.SMEM(tile_cells.shape, jnp.int32),
            pltpu.SemaphoreType.DMA((3,)),
        ],
        compiler_params=pltpu.CompilerParams(vmem_limit_bytes=VMEM_BYTES // 2),
        name="back_project",
    )(volume, footprint, tile_block, tile_cells, *parts)


def unit_at_edge(cells):
    return cells * lax.rsqrt(cells * cells + SMOOTHING)


def slope_of(here, after, unit_before, first_row, last_row, first_cell, last_cell):
    rows, cells = here.shape
    diff_a = after - here
    diff_b = jnp.where(last_row, 0.0, pltpu.roll(here, rows - 1, 0)) - here
    diff_e = jnp.where(last_cell, 0.0, pltpu.roll(here, cells - 1, 1)) - here
    scale = lax.rsqrt(diff_a * diff_a + diff_b * diff_b + diff_e * diff_e + SMOOTHING)
    unit_a, unit_b, unit_e = diff_a * scale, diff_b * scale, diff_e * scale
    edge = unit_at_edge(here)
    back_b = jnp.where(first_row, edge, pltpu.roll(unit_b, 1, 0))
    back_e = jnp.where(first_cell, edge, pltpu.roll(unit_e, 1, 1))
    return unit_before + back_b + back_e - (unit_a + unit_b + unit_e), unit_a


def smooth_kernel(sizes, near_ref, far_ref, out_ref, field, slopes):
    slabs, bands, planes, rows, tiles, tvox = sizes
    slab, band = lax.axis_index("slab"), lax.axis_index("xy")
    depth, height, width = slabs * planes, bands * rows, tiles * tvox

    gap = jnp.zeros((rows, tvox), jnp.float32)
    for half, ref in enumerate((near_ref, far_ref)):
        for i in range(slabs // 2):
            for j in range(bands):
                plane = (slab ^ (2 * i + half)) * planes
                row = pl.multiple_of((band ^ j) * rows, rows)
                for p in range(planes):
                    for t in range(tiles):
                        field[plane + p, pl.ds(row, rows), t * tvox : (t + 1) * tvox] = ref[
                            i, j, p * tiles + t
                        ]
                gap += ref[i, j, planes * tiles]
    nothing = jnp.zeros((height, width), jnp.float32)
    field[depth] = nothing
    slopes[depth] = nothing
    row_ids = lax.broadcasted_iota(jnp.int32, (height, width), 0)
    cell_ids = lax.broadcasted_iota(jnp.int32, (height, width), 1)
    rims = (row_ids == 0, row_ids == height - 1, cell_ids == 0, cell_ids == width - 1)

    def total(square):
        return jnp.sum(jnp.sum(square, axis=0, keepdims=True), axis=1, keepdims=True)

    def fold(square):
        return jnp.sum(
            sum(square[:, t * tvox : (t + 1) * tvox] for t in range(tiles)).reshape(
                height // 8, 8, tvox
            ),
            axis=0,
        )

    norm = jnp.sqrt(total(gap))

    def one(p, carry):
        unit_before, square = carry
        slope, unit = slope_of(field[p], field[p + 1], unit_before, *rims)
        slopes[p] = slope
        return unit, square + fold(slope * slope)

    start = unit_at_edge(field[0]), jnp.zeros((8, tvox), jnp.float32)
    _, square = lax.fori_loop(0, depth, one, start)
    step = TV_RATE * norm / jnp.sqrt(total(square) + 1e-06)

    def two(p, carry):
        unit_before, here, square = carry
        after = field[p + 1] - step * slopes[p + 1]
        slope, unit = slope_of(here, after, unit_before, *rims)
        field[p] = here
        slopes[p] = slope
        return unit, after, square + fold(slope * slope)

    here = field[0] - step * slopes[0]
    start = unit_at_edge(here), here, jnp.zeros((8, tvox), jnp.float32)
    _, _, square = lax.fori_loop(0, depth, two, start)
    step = TV_RATE * norm / jnp.sqrt(total(square) + 1e-06)
    mine = pl.ds(pl.multiple_of(band * rows, rows), rows)
    for p in range(planes):
        out_ref[p] = field[slab * planes + p, mine, :] - step * slopes[slab * planes + p, mine, :]


def smooth(volume, near, far, slabs, bands, tiles):
    planes, rows, cells = volume.shape
    sizes = slabs, bands, planes, rows, tiles, cells // tiles
    whole = (slabs * planes + 1, bands * rows, cells)
    return pl.pallas_call(
        functools.partial(smooth_kernel, sizes),
        out_shape=jax.ShapeDtypeStruct(volume.shape, jnp.float32),
        in_specs=[pl.BlockSpec(memory_space=pltpu.VMEM)] * 2,
        out_specs=pl.BlockSpec(memory_space=pltpu.VMEM),
        scratch_shapes=[pltpu.VMEM(whole, jnp.float32)] * 2,
        compiler_params=pltpu.CompilerParams(vmem_limit_bytes=VMEM_BYTES),
        name="smooth",
    )(near, far)


def body(volume, footprint, tile_block, tile_cells, measured):
    views, tdet = footprint.shape[3], footprint.shape[5]
    slabs, bands = lax.axis_size("slab"), lax.axis_size("xy")
    plan = Plan(slabs, bands, views, measured.shape[1] // tdet, tdet)
    block, cells = (jnp.transpose(each, (0, 2, 3, 1)) for each in (tile_block, tile_cells))

    packed, low, high, seen, footprint = project(
        plan, volume, footprint, block, cells, measured
    )
    below, above = shift_all(high, "slab", 1), shift_all(low, "slab", -1)
    chunks = shares(plan, packed, below, above)
    parts = [chunks[0]] + [swap_all(chunks[flip], "xy", flip) for flip in range(1, bands)]
    correction, rounded = correct(plan, seen, parts)
    parts = [rounded] + [swap_all(rounded, "xy", flip) for flip in range(1, bands)]
    tiled = back_project(plan, volume, footprint, block, cells, parts)

    line = jnp.stack([tiled] + [swap_all(tiled, "xy", flip) for flip in range(1, bands)])
    near = jnp.stack([line] + [swap_all(line, "slab", flip) for flip in range(2, slabs, 2)])
    far = swap_all(near, "slab", 1)
    updated = smooth(volume, near, far, slabs, bands, footprint.shape[2])
    return (updated, correction)


def solution(mesh):
    placed = (
        P("slab", "xy", None),
        P("slab", "xy", None, None, None, None),
        P("slab", "xy", None, None),
        P("slab", "xy", None, None),
        P(),
    )
    return jax.shard_map(
        body,
        mesh=mesh,
        in_specs=placed,
        out_specs=(P("slab", "xy", None), P(None, ("slab", "xy"))),
        check_vma=False,
    )
```

time: 290 us -> 58.3 us (0.20)
  waiting for transfers between devices: 141 us -> 20.8 us
  blocking collectives: 82.6 us -> 0 us
  other arithmetic: 21.1 us -> 0.06 us
  Pallas kernels: 0 us -> 15.7 us
  between operations: 16.4 us -> 0.72 us
  starting transfers between devices: 9.17 us -> 20.9 us
  matrix products: 11.7 us -> 0 us
  local copies, waits for them, and re-layouts: 7.55 us -> 0.01 us
    psum x1 -> x0, waiting for transfers between devices: 136 us -> none  [body(): projected, ray_weight = lax.psum((projected, ray_weight), ('slab', 'xy'))]
    psum x2 -> x0, blocking collectives: 82.6 us -> none  [the longest x1 41.6 us: slope_scale(): return jnp.sqrt(lax.psum(jnp.sum(slope * slope), ('slab', 'xy')) + 1e-06)]
    ppermute x4 -> x15, waiting for transfers between devices: 4.67 us -> 20.8 us  [the longest x13 19.1 us: swap_all(): return lax.ppermute(cells, axis, [(i, i ^ flip) for i in range(count)])]
    pallas_call x0 -> x5, Pallas kernels: none -> 15.7 us  [the longest x1 6.78 us: smooth(): pl.pallas_call(functools.partial(smooth_kernel, sizes), out_shape=jax.Sha...]
    ppermute x4 -> x15, starting transfers between devices: 9.13 us -> 20.9 us  [the longest x13 17.4 us: swap_all(): return lax.ppermute(cells, axis, [(i, i ^ flip) for i in range(count)])]
    dot_general x4 -> x0, matrix products: 11.7 us -> none  [the longest x1 5.63 us: body(): jnp.einsum('tvjc,tvc->tj', masked, picked, preferred_element_type=jnp.flo...]
    reduce_sum x4 -> x0, other arithmetic: 8.11 us -> none  [the longest x1 6.02 us: body(): column = jnp.sum(masked, axis=(1, 3), dtype=jnp.float32)]
    select_n x2 -> x0, other arithmetic: 7.43 us -> none  [the longest x1 7.31 us: body(): jnp.where(live[:, :, None, :], weights, jnp.zeros((), jnp.bfloat16))]
  transfers between devices with their start and end apart: 5 -> 15, of which waited for: 3 -> 11; matrix products, arithmetic and copies ran while one was open for 0% -> 0% of each run, Pallas kernels for 0% -> 0%
where the time goes in v2:
time: 58.3 us; the launch traced here: 58.1 us
  starting transfers between devices  20.9 us (36%)
  waiting for transfers between devices  20.8 us (36%)
  Pallas kernels  15.7 us (27%)
  between operations  0.72 us (1%)
    ppermute x13, waiting for transfers between devices, swap_all(): return lax.ppermute(cells, axis, [(i, i ^ flip) for i in range(count)])  19.1 us
    ppermute x13, starting transfers between devices, swap_all(): return lax.ppermute(cells, axis, [(i, i ^ flip) for i in range(count)])  17.4 us
    pallas_call x1, Pallas kernels, smooth(): pl.pallas_call(functools.partial(smooth_kernel, sizes), out_shape=jax.Sha...  6.78 us
    pallas_call x1, Pallas kernels, project(): pl.pallas_call(functools.partial(project_kernel, plan, shape), out_shape=...  5.03 us
    ppermute x2, starting transfers between devices, shift_all(): lax.ppermute(cells, axis, [(i, (i + step) % count) for i in range(count)])  3.45 us
    pallas_call x1, Pallas kernels, back_project(): pl.pallas_call(functools.partial(back_kernel, plan, shape), out_shape=jax...  3.14 us
    ppermute x2, waiting for transfers between devices, shift_all(): lax.ppermute(cells, axis, [(i, (i + step) % count) for i in range(count)])  1.75 us
  transfers between devices with their start and end apart: 15, of which 11 were waited for; matrix products, arithmetic and copies ran while one was open for 0% of the time, Pallas kernels for 0%

profile of v2, /device:TPU:0, one launch (start us, length us, event | category | flops | bytes accessed | tf_op | source)
XLA Modules:
  0.0 58.1 jit_solution(2439940935381098165)
XLA Ops:
  0.7 5.0 %project.1 = (f32[10,24,256]{2,1,0:T(8,128)S(1)}, f32[2,24,256]{2,1,0:T(8,128)S(1)}, f32[2,24,256]{2,1,0:T(8,128)S(1)}, f32[2,3,8,256]{3,2,1,0:T(8,128)S(1)}, bf16[2,8,4,2,128,256]{5,4,3,2,1,0:T(8,128)(2,1)S(1)}) custom-call(f32[2,8,512]{2,1,0:T(8,128)} %vol_any.1, bf16[2,8,4,2,128,256]{5,4,3,2,1,0:T(8,128)(2,1)} %foot_hbm.1, s32[2,4,2,8]{3,2,1,0:T(2,128)} %bitcast.12, ...), custom_call_target="tpu_custom_call" | custom-call | tf_op jit(solution)/shard_map/project/pallas_call | solution.py:147
  5.7 0.5 collective-permute-start
  6.2 2.9 %collective-permute-start.1 = (f32[2,24,256]{2,1,0:T(8,128)S(1)}, f32[2,24,256]{2,1,0:T(8,128)S(1)}, u32[]{:S(2)}, u32[]{:S(2)}) collective-permute-start(f32[2,24,256]{2,1,0:T(8,128)S(1)} %get-tuple-element.17), channel_id=1, source_target_pairs={{0,28},{4,0},{8,4},{12,8},{16,12},{20,16},{24,20},{28,24},{1,29},{... | collective-permute-start | bytes 147464 | tf_op jit(solution)/shard_map/ppermute | solution.py:44
  9.2 1.7 %collective-permute-done.below_ref = f32[2,24,256]{2,1,0:T(8,128)S(1)} collective-permute-done((f32[2,24,256]{2,1,0:T(8,128)S(1)}, f32[2,24,256]{2,1,0:T(8,128)S(1)}, u32[]{:S(2)}, u32[]{:S(2)}) %collective-permute-start) | collective-permute-done | bytes 49184 | tf_op jit(solution)/shard_map/ppermute | solution.py:44
  10.9 0.0 collective-permute-done.1.above_ref
  10.9 0.1 shares.1
  11.0 2.4 %collective-permute-start.2 = (f32[3,24,256]{2,1,0:T(8,128)S(1)}, f32[3,24,256]{2,1,0:T(8,128)S(1)}, u32[]{:S(2)}, u32[]{:S(2)}) collective-permute-start(f32[3,24,256]{2,1,0:T(8,128)S(1)} %get-tuple-element.19), channel_id=1, source_target_pairs={{0,1},{1,0},{2,3},{3,2},{4,5},{5,4},{6,7},{7,6},{8,9},{9,8},{10,11... | collective-permute-start | bytes 221192 | tf_op jit(solution)/shard_map/ppermute | solution.py:49
  13.3 2.6 %collective-permute-start.3 = (f32[3,24,256]{2,1,0:T(8,128)S(1)}, f32[3,24,256]{2,1,0:T(8,128)S(1)}, u32[]{:S(2)}, u32[]{:S(2)}) collective-permute-start(f32[3,24,256]{2,1,0:T(8,128)S(1)} %get-tuple-element.20), channel_id=1, source_target_pairs={{0,2},{1,3},{2,0},{3,1},{4,6},{5,7},{6,4},{7,5},{8,10},{9,11},{10,... | collective-permute-start | bytes 221192 | tf_op jit(solution)/shard_map/ppermute | solution.py:49
  15.9 0.0 collective-permute-start.4
  15.9 0.3 collective-permute-done.2.rest_1_
  16.3 6.1 %collective-permute-done.3.rest_2_ = f32[3,24,256]{2,1,0:T(8,128)S(1)} collective-permute-done((f32[3,24,256]{2,1,0:T(8,128)S(1)}, f32[3,24,256]{2,1,0:T(8,128)S(1)}, u32[]{:S(2)}, u32[]{:S(2)}) %collective-permute-start.3) | collective-permute-done | bytes 73760 | tf_op jit(solution)/shard_map/ppermute | solution.py:49
  22.4 0.7 %correct.1 = (f32[2,4096]{1,0:T(2,128)}, bf16[48,256]{1,0:T(8,128)(2,1)S(1)}) custom-call(f32[2,3,8,256]{3,2,1,0:T(8,128)S(1)} %get-tuple-element.14.seen_ref, f32[3,24,256]{2,1,0:T(8,128)S(1)} %get-tuple-element.18.rest_0_, f32[3,24,256]{2,1,0:T(8,128)S(1)} %collective-permute-done.2.rest_1_, f32[3,24,256]{2,1,0:T(8,128)S(1)} %collective-permute-done.3.rest_2_, ...), custom_call_target="tpu_custom_call" | custom-call | tf_op jit(solution)/shard_map/correct/pallas_call | solution.py:233
  23.0 2.6 %collective-permute-start.7 = (bf16[48,256]{1,0:T(8,128)(2,1)S(1)}, bf16[48,256]{1,0:T(8,128)(2,1)S(1)}, u32[]{:S(2)}, u32[]{:S(2)}) collective-permute-start(bf16[48,256]{1,0:T(8,128)(2,1)S(1)} %get-tuple-element.22.rest_0_), channel_id=1, source_target_pairs={{0,3},{1,2},{2,1},{3,0},{4,7},{5,6},{6,5},{7,4},{8,11},{9,10},{10,... | collective-permute-start | bytes 73736 | tf_op jit(solution)/shard_map/ppermute | solution.py:49
  25.6 0.6 %collective-permute-start.6 = (bf16[48,256]{1,0:T(8,128)(2,1)S(1)}, bf16[48,256]{1,0:T(8,128)(2,1)S(1)}, u32[]{:S(2)}, u32[]{:S(2)}) collective-permute-start(bf16[48,256]{1,0:T(8,128)(2,1)S(1)} %get-tuple-element.22.rest_0_), channel_id=1, source_target_pairs={{0,2},{1,3},{2,0},{3,1},{4,6},{5,7},{6,4},{7,5},{8,10},{9,11},{10,... | collective-permute-start | bytes 73736 | tf_op jit(solution)/shard_map/ppermute | solution.py:49
  26.3 1.2 %collective-permute-start.5 = (bf16[48,256]{1,0:T(8,128)(2,1)S(1)}, bf16[48,256]{1,0:T(8,128)(2,1)S(1)}, u32[]{:S(2)}, u32[]{:S(2)}) collective-permute-start(bf16[48,256]{1,0:T(8,128)(2,1)S(1)} %get-tuple-element.22.rest_0_), channel_id=1, source_target_pairs={{0,1},{1,0},{2,3},{3,2},{4,5},{5,4},{6,7},{7,6},{8,9},{9,8},{10,11... | collective-permute-start | bytes 73736 | tf_op jit(solution)/shard_map/ppermute | solution.py:49
  27.4 1.3 %collective-permute-done.7.rest_3_ = bf16[48,256]{1,0:T(8,128)(2,1)S(1)} collective-permute-done((bf16[48,256]{1,0:T(8,128)(2,1)S(1)}, bf16[48,256]{1,0:T(8,128)(2,1)S(1)}, u32[]{:S(2)}, u32[]{:S(2)}) %collective-permute-start.7) | collective-permute-done | bytes 24608 | tf_op jit(solution)/shard_map/ppermute | solution.py:49
  28.7 1.7 %collective-permute-done.6.rest_2_ = bf16[48,256]{1,0:T(8,128)(2,1)S(1)} collective-permute-done((bf16[48,256]{1,0:T(8,128)(2,1)S(1)}, bf16[48,256]{1,0:T(8,128)(2,1)S(1)}, u32[]{:S(2)}, u32[]{:S(2)}) %collective-permute-start.6) | collective-permute-done | bytes 24608 | tf_op jit(solution)/shard_map/ppermute | solution.py:49
  30.4 3.1 %back_project.1 = f32[9,8,128]{2,1,0:T(8,128)S(1)} custom-call(f32[2,8,512]{2,1,0:T(8,128)S(1)} %copy-done, bf16[2,8,4,2,128,256]{5,4,3,2,1,0:T(8,128)(2,1)S(1)} %get-tuple-element.13.foot, s32[2,4,2,8]{3,2,1,0:T(2,128)S(1)} %bitcast.13, s32[2,4,2,8]{3,2,1,0:T(2,128)S(1)} %bitcast.15, bf16[48,256]{1,0:T(8,128)(2,1)S(1)} %get-tuple-element.22.rest_0_, ...), custom_call_target="tpu_custom_call" | custom-call | tf_op jit(solution)/shard_map/back_project/pallas_call | solution.py:301
  33.5 2.3 %collective-permute-start.10 = (f32[9,8,128]{2,1,0:T(8,128)S(1)}, f32[9,8,128]{2,1,0:T(8,128)S(1)}, u32[]{:S(2)}, u32[]{:S(2)}) collective-permute-start(f32[9,8,128]{2,1,0:T(8,128)S(1)} %back_project.1), channel_id=1, source_target_pairs={{0,3},{1,2},{2,1},{3,0},{4,7},{5,6},{6,5},{7,4},{8,11},{9,10},{10,... | collective-permute-start | bytes 110600 | tf_op jit(solution)/shard_map/ppermute | solution.py:49
  35.8 0.1 collective-permute-start.9
  36.0 2.0 %collective-permute-start.8 = (f32[9,8,128]{2,1,0:T(8,128)S(1)}, f32[9,8,128]{2,1,0:T(8,128)S(1)}, u32[]{:S(2)}, u32[]{:S(2)}) collective-permute-start(f32[9,8,128]{2,1,0:T(8,128)S(1)} %back_project.1), channel_id=1, source_target_pairs={{0,1},{1,0},{2,3},{3,2},{4,5},{5,4},{6,7},{7,6},{8,9},{9,8},{10,11... | collective-permute-start | bytes 110600 | tf_op jit(solution)/shard_map/ppermute | solution.py:49
  38.0 1.4 %collective-permute-done.10 = f32[9,8,128]{2,1,0:T(8,128)S(1)} collective-permute-done((f32[9,8,128]{2,1,0:T(8,128)S(1)}, f32[9,8,128]{2,1,0:T(8,128)S(1)}, u32[]{:S(2)}, u32[]{:S(2)}) %collective-permute-start.10) | collective-permute-done | bytes 36896 | tf_op jit(solution)/shard_map/ppermute | solution.py:49
  39.4 1.5 %collective-permute-done.9 = f32[9,8,128]{2,1,0:T(8,128)S(1)} collective-permute-done((f32[9,8,128]{2,1,0:T(8,128)S(1)}, f32[9,8,128]{2,1,0:T(8,128)S(1)}, u32[]{:S(2)}, u32[]{:S(2)}) %collective-permute-start.9) | collective-permute-done | bytes 36896 | tf_op jit(solution)/shard_map/ppermute | solution.py:49
  40.9 1.6 %collective-permute-start.12 = (f32[4,9,8,128]{3,2,1,0:T(8,128)S(1)}, f32[4,9,8,128]{3,2,1,0:T(8,128)S(1)}, u32[]{:S(2)}, u32[]{:S(2)}) collective-permute-start(f32[4,9,8,128]{3,2,1,0:T(8,128)S(1)} %get-tuple-element.25), channel_id=1, source_target_pairs={{0,16},{4,20},{8,24},{12,28},{16,0},{20,4},{24,8},{28,12},{1,17},{... | collective-permute-start | bytes 442376 | tf_op jit(solution)/shard_map/ppermute | solution.py:49
  42.5 0.7 %collective-permute-start.11 = (f32[4,9,8,128]{3,2,1,0:T(8,128)S(1)}, f32[4,9,8,128]{3,2,1,0:T(8,128)S(1)}, u32[]{:S(2)}, u32[]{:S(2)}) collective-permute-start(f32[4,9,8,128]{3,2,1,0:T(8,128)S(1)} %get-tuple-element.25), channel_id=1, source_target_pairs={{0,8},{4,12},{8,0},{12,4},{16,24},{20,28},{24,16},{28,20},{1,9},{5... | collective-permute-start | bytes 442376 | tf_op jit(solution)/shard_map/ppermute | solution.py:49
  43.2 1.3 %collective-permute-start.13 = (f32[4,9,8,128]{3,2,1,0:T(8,128)S(1)}, f32[4,9,8,128]{3,2,1,0:T(8,128)S(1)}, u32[]{:S(2)}, u32[]{:S(2)}) collective-permute-start(f32[4,9,8,128]{3,2,1,0:T(8,128)S(1)} %get-tuple-element.25), channel_id=1, source_target_pairs={{0,24},{4,28},{8,16},{12,20},{16,8},{20,12},{24,0},{28,4},{1,25},{... | collective-permute-start | bytes 442376 | tf_op jit(solution)/shard_map/ppermute | solution.py:49
  44.5 2.4 %collective-permute-done.12 = f32[4,9,8,128]{3,2,1,0:T(8,128)S(1)} collective-permute-done((f32[4,9,8,128]{3,2,1,0:T(8,128)S(1)}, f32[4,9,8,128]{3,2,1,0:T(8,128)S(1)}, u32[]{:S(2)}, u32[]{:S(2)}) %collective-permute-start.12) | collective-permute-done | bytes 147488 | tf_op jit(solution)/shard_map/ppermute | solution.py:49
  46.9 0.7 %collective-permute-done.11 = f32[4,9,8,128]{3,2,1,0:T(8,128)S(1)} collective-permute-done((f32[4,9,8,128]{3,2,1,0:T(8,128)S(1)}, f32[4,9,8,128]{3,2,1,0:T(8,128)S(1)}, u32[]{:S(2)}, u32[]{:S(2)}) %collective-permute-start.11) | collective-permute-done | bytes 147488 | tf_op jit(solution)/shard_map/ppermute | solution.py:49
  47.6 1.6 %collective-permute-done.13 = f32[4,9,8,128]{3,2,1,0:T(8,128)S(1)} collective-permute-done((f32[4,9,8,128]{3,2,1,0:T(8,128)S(1)}, f32[4,9,8,128]{3,2,1,0:T(8,128)S(1)}, u32[]{:S(2)}, u32[]{:S(2)}) %collective-permute-start.13) | collective-permute-done | bytes 147488 | tf_op jit(solution)/shard_map/ppermute | solution.py:49
  49.3 0.1 collective-permute-start.14
  49.4 2.0 %collective-permute-done.14.far_ref = f32[4,4,9,8,128]{4,3,2,1,0:T(8,128)S(1)} collective-permute-done((f32[4,4,9,8,128]{4,3,2,1,0:T(8,128)S(1)}, f32[4,4,9,8,128]{4,3,2,1,0:T(8,128)S(1)}, u32[]{:S(2)}, u32[]{:S(2)}) %collective-permute-start.14) | collective-permute-done | bytes 589856 | tf_op jit(solution)/shard_map/ppermute | solution.py:49
  51.3 6.8 %smooth.1 = f32[2,8,512]{2,1,0:T(8,128)} custom-call(f32[4,4,9,8,128]{4,3,2,1,0:T(8,128)S(1)} %pad_maximum_fusion.near_ref, f32[4,4,9,8,128]{4,3,2,1,0:T(8,128)S(1)} %collective-permute-done.14.far_ref), custom_call_target="tpu_custom_call" | custom-call | tf_op jit(solution)/shard_map/smooth/pallas_call | solution.py:404
  (11 shorter events, 0.1 us)
Async XLA Ops:
  0.6 29.8 %copy-start = (f32[2,8,512]{2,1,0:T(8,128)S(1)}, f32[2,8,512]{2,1,0:T(8,128)}, u32[]{:S(2)}) copy-start(f32[2,8,512]{2,1,0:T(8,128)} %vol_any.1) | copy-start | bytes 98308
  0.6 29.7 %copy-start.2 = (s32[2,8,4,2]{1,3,2,0:T(2,128)S(1)}, s32[2,8,4,2]{1,3,2,0:T(2,128)}, u32[]{:S(2)}) copy-start(s32[2,8,4,2]{1,3,2,0:T(2,128)} %param.8) | copy-start | bytes 1540
  0.7 29.7 %copy-start.1 = (s32[2,8,4,2]{1,3,2,0:T(2,128)S(1)}, s32[2,8,4,2]{1,3,2,0:T(2,128)}, u32[]{:S(2)}) copy-start(s32[2,8,4,2]{1,3,2,0:T(2,128)} %param.7) | copy-start | bytes 1540
  5.7 5.2 %collective-permute-start = (f32[2,24,256]{2,1,0:T(8,128)S(1)}, f32[2,24,256]{2,1,0:T(8,128)S(1)}, u32[]{:S(2)}, u32[]{:S(2)}) collective-permute-start(f32[2,24,256]{2,1,0:T(8,128)S(1)} %get-tuple-element.16), channel_id=1, source_target_pairs={{0,4},{4,8},{8,12},{12,16},{16,20},{20,24},{24,28},{28,0},{1,5},{5... | collective-permute-start | bytes 147464 | tf_op jit(solution)/shard_map/ppermute | solution.py:44
  6.2 4.7 %collective-permute-start.1 = (f32[2,24,256]{2,1,0:T(8,128)S(1)}, f32[2,24,256]{2,1,0:T(8,128)S(1)}, u32[]{:S(2)}, u32[]{:S(2)}) collective-permute-start(f32[2,24,256]{2,1,0:T(8,128)S(1)} %get-tuple-element.17), channel_id=1, source_target_pairs={{0,28},{4,0},{8,4},{12,8},{16,12},{20,16},{24,20},{28,24},{1,29},{... | collective-permute-start | bytes 147464 | tf_op jit(solution)/shard_map/ppermute | solution.py:44
  11.0 5.3 %collective-permute-start.2 = (f32[3,24,256]{2,1,0:T(8,128)S(1)}, f32[3,24,256]{2,1,0:T(8,128)S(1)}, u32[]{:S(2)}, u32[]{:S(2)}) collective-permute-start(f32[3,24,256]{2,1,0:T(8,128)S(1)} %get-tuple-element.19), channel_id=1, source_target_pairs={{0,1},{1,0},{2,3},{3,2},{4,5},{5,4},{6,7},{7,6},{8,9},{9,8},{10,11... | collective-permute-start | bytes 221192 | tf_op jit(solution)/shard_map/ppermute | solution.py:49
  13.3 9.1 %collective-permute-start.3 = (f32[3,24,256]{2,1,0:T(8,128)S(1)}, f32[3,24,256]{2,1,0:T(8,128)S(1)}, u32[]{:S(2)}, u32[]{:S(2)}) collective-permute-start(f32[3,24,256]{2,1,0:T(8,128)S(1)} %get-tuple-element.20), channel_id=1, source_target_pairs={{0,2},{1,3},{2,0},{3,1},{4,6},{5,7},{6,4},{7,5},{8,10},{9,11},{10,... | collective-permute-start | bytes 221192 | tf_op jit(solution)/shard_map/ppermute | solution.py:49
  15.9 6.5 %collective-permute-start.4 = (f32[3,24,256]{2,1,0:T(8,128)S(1)}, f32[3,24,256]{2,1,0:T(8,128)S(1)}, u32[]{:S(2)}, u32[]{:S(2)}) collective-permute-start(f32[3,24,256]{2,1,0:T(8,128)S(1)} %get-tuple-element.21), channel_id=1, source_target_pairs={{0,3},{1,2},{2,1},{3,0},{4,7},{5,6},{6,5},{7,4},{8,11},{9,10},{10,... | collective-permute-start | bytes 221192 | tf_op jit(solution)/shard_map/ppermute | solution.py:49
  23.0 5.7 %collective-permute-start.7 = (bf16[48,256]{1,0:T(8,128)(2,1)S(1)}, bf16[48,256]{1,0:T(8,128)(2,1)S(1)}, u32[]{:S(2)}, u32[]{:S(2)}) collective-permute-start(bf16[48,256]{1,0:T(8,128)(2,1)S(1)} %get-tuple-element.22.rest_0_), channel_id=1, source_target_pairs={{0,3},{1,2},{2,1},{3,0},{4,7},{5,6},{6,5},{7,4},{8,11},{9,10},{10,... | collective-permute-start | bytes 73736 | tf_op jit(solution)/shard_map/ppermute | solution.py:49
  25.6 4.7 %collective-permute-start.6 = (bf16[48,256]{1,0:T(8,128)(2,1)S(1)}, bf16[48,256]{1,0:T(8,128)(2,1)S(1)}, u32[]{:S(2)}, u32[]{:S(2)}) collective-permute-start(bf16[48,256]{1,0:T(8,128)(2,1)S(1)} %get-tuple-element.22.rest_0_), channel_id=1, source_target_pairs={{0,2},{1,3},{2,0},{3,1},{4,6},{5,7},{6,4},{7,5},{8,10},{9,11},{10,... | collective-permute-start | bytes 73736 | tf_op jit(solution)/shard_map/ppermute | solution.py:49
  26.3 4.1 %collective-permute-start.5 = (bf16[48,256]{1,0:T(8,128)(2,1)S(1)}, bf16[48,256]{1,0:T(8,128)(2,1)S(1)}, u32[]{:S(2)}, u32[]{:S(2)}) collective-permute-start(bf16[48,256]{1,0:T(8,128)(2,1)S(1)} %get-tuple-element.22.rest_0_), channel_id=1, source_target_pairs={{0,1},{1,0},{2,3},{3,2},{4,5},{5,4},{6,7},{7,6},{8,9},{9,8},{10,11... | collective-permute-start | bytes 73736 | tf_op jit(solution)/shard_map/ppermute | solution.py:49
  33.5 5.8 %collective-permute-start.10 = (f32[9,8,128]{2,1,0:T(8,128)S(1)}, f32[9,8,128]{2,1,0:T(8,128)S(1)}, u32[]{:S(2)}, u32[]{:S(2)}) collective-permute-start(f32[9,8,128]{2,1,0:T(8,128)S(1)} %back_project.1), channel_id=1, source_target_pairs={{0,3},{1,2},{2,1},{3,0},{4,7},{5,6},{6,5},{7,4},{8,11},{9,10},{10,... | collective-permute-start | bytes 110600 | tf_op jit(solution)/shard_map/ppermute | solution.py:49
  35.8 5.0 %collective-permute-start.9 = (f32[9,8,128]{2,1,0:T(8,128)S(1)}, f32[9,8,128]{2,1,0:T(8,128)S(1)}, u32[]{:S(2)}, u32[]{:S(2)}) collective-permute-start(f32[9,8,128]{2,1,0:T(8,128)S(1)} %back_project.1), channel_id=1, source_target_pairs={{0,2},{1,3},{2,0},{3,1},{4,6},{5,7},{6,4},{7,5},{8,10},{9,11},{10,... | collective-permute-start | bytes 110600 | tf_op jit(solution)/shard_map/ppermute | solution.py:49
  36.0 4.9 %collective-permute-start.8 = (f32[9,8,128]{2,1,0:T(8,128)S(1)}, f32[9,8,128]{2,1,0:T(8,128)S(1)}, u32[]{:S(2)}, u32[]{:S(2)}) collective-permute-start(f32[9,8,128]{2,1,0:T(8,128)S(1)} %back_project.1), channel_id=1, source_target_pairs={{0,1},{1,0},{2,3},{3,2},{4,5},{5,4},{6,7},{7,6},{8,9},{9,8},{10,11... | collective-permute-start | bytes 110600 | tf_op jit(solution)/shard_map/ppermute | solution.py:49
  40.9 6.0 %collective-permute-start.12 = (f32[4,9,8,128]{3,2,1,0:T(8,128)S(1)}, f32[4,9,8,128]{3,2,1,0:T(8,128)S(1)}, u32[]{:S(2)}, u32[]{:S(2)}) collective-permute-start(f32[4,9,8,128]{3,2,1,0:T(8,128)S(1)} %get-tuple-element.25), channel_id=1, source_target_pairs={{0,16},{4,20},{8,24},{12,28},{16,0},{20,4},{24,8},{28,12},{1,17},{... | collective-permute-start | bytes 442376 | tf_op jit(solution)/shard_map/ppermute | solution.py:49
  42.5 5.1 %collective-permute-start.11 = (f32[4,9,8,128]{3,2,1,0:T(8,128)S(1)}, f32[4,9,8,128]{3,2,1,0:T(8,128)S(1)}, u32[]{:S(2)}, u32[]{:S(2)}) collective-permute-start(f32[4,9,8,128]{3,2,1,0:T(8,128)S(1)} %get-tuple-element.25), channel_id=1, source_target_pairs={{0,8},{4,12},{8,0},{12,4},{16,24},{20,28},{24,16},{28,20},{1,9},{5... | collective-permute-start | bytes 442376 | tf_op jit(solution)/shard_map/ppermute | solution.py:49
  43.2 6.0 %collective-permute-start.13 = (f32[4,9,8,128]{3,2,1,0:T(8,128)S(1)}, f32[4,9,8,128]{3,2,1,0:T(8,128)S(1)}, u32[]{:S(2)}, u32[]{:S(2)}) collective-permute-start(f32[4,9,8,128]{3,2,1,0:T(8,128)S(1)} %get-tuple-element.25), channel_id=1, source_target_pairs={{0,24},{4,28},{8,16},{12,20},{16,8},{20,12},{24,0},{28,4},{1,25},{... | collective-permute-start | bytes 442376 | tf_op jit(solution)/shard_map/ppermute | solution.py:49
  49.3 2.1 %collective-permute-start.14 = (f32[4,4,9,8,128]{4,3,2,1,0:T(8,128)S(1)}, f32[4,4,9,8,128]{4,3,2,1,0:T(8,128)S(1)}, u32[]{:S(2)}, u32[]{:S(2)}) collective-permute-start(f32[4,4,9,8,128]{4,3,2,1,0:T(8,128)S(1)} %pad_maximum_fusion.near_ref), channel_id=1, source_target_pairs={{0,4},{4,0},{8,12},{12,8},{16,20},{20,16},{24,28},{28,24},{1,5},{5... | collective-permute-start | bytes 1769480 | tf_op jit(solution)/shard_map/ppermute | solution.py:49

commit v3 on v2

--- a/solution.py
+++ b/solution.py
@@ -222,9 +222,7 @@
             corrected = (seen_ref[v, i] - sums[0]) / jnp.maximum(sums[1], 1.0)
             rounded.append(corrected)
             if i < plan.own_units:
-                for c in range(unit):
-                    at = (i * unit + c) * tdet
-                    exact_ref[v : v + 1, at : at + tdet] = corrected[c : c + 1]
+                exact_ref[v, i] = corrected
     rounded_ref[...] = jnp.concatenate(rounded, axis=0).astype(jnp.bfloat16)
 
 
@@ -233,7 +231,7 @@
     return pl.pallas_call(
         functools.partial(correct_kernel, plan),
         out_shape=(
-            jax.ShapeDtypeStruct((views, plan.own_units * unit * tdet), jnp.float32),
+            jax.ShapeDtypeStruct((views, plan.own_units, unit, tdet), jnp.float32),
             jax.ShapeDtypeStruct((views * chunk * unit, tdet), jnp.bfloat16),
         ),
         in_specs=in_vmem(1 + len(parts)),
@@ -316,100 +314,140 @@
     )(volume, footprint, tile_block, tile_cells, *parts)
 
 
-def unit_at_edge(cells):
+def unit_at_rim(cells):
     return cells * lax.rsqrt(cells * cells + SMOOTHING)
 
 
-def slope_of(here, after, unit_before, first_row, last_row, first_cell, last_cell):
-    rows, cells = here.shape
-    diff_a = after - here
-    diff_b = jnp.where(last_row, 0.0, pltpu.roll(here, rows - 1, 0)) - here
-    diff_e = jnp.where(last_cell, 0.0, pltpu.roll(here, cells - 1, 1)) - here
-    scale = lax.rsqrt(diff_a * diff_a + diff_b * diff_b + diff_e * diff_e + SMOOTHING)
-    unit_a, unit_b, unit_e = diff_a * scale, diff_b * scale, diff_e * scale
-    edge = unit_at_edge(here)
-    back_b = jnp.where(first_row, edge, pltpu.roll(unit_b, 1, 0))
-    back_e = jnp.where(first_cell, edge, pltpu.roll(unit_e, 1, 1))
-    return unit_before + back_b + back_e - (unit_a + unit_b + unit_e), unit_a
-
-
-def smooth_kernel(sizes, near_ref, far_ref, out_ref, field, slopes):
+def slope_of(here, after, unit_before, size, masks):
+    high, wide = size
+    first_row, last_row, first_cell, last_cell = masks
+    lanes = here[0, 0].shape[1]
+    next_row = {k: pltpu.roll(x, 7, 0) for k, x in here.items()}
+    next_cell = {k: pltpu.roll(x, lanes - 1, 1) for k, x in here.items()}
+    slope, unit_a, unit_b, unit_e = {}, {}, {}, {}
+    for i, t in here:
+        k, x = (i, t), here[i, t]
+        row = next_row[i + 1, t] if i + 1 < high else 0.0
+        cell = next_cell[i, t + 1] if t + 1 < wide else 0.0
+        diff_a = after[k] - x
+        diff_b = jnp.where(last_row, row, next_row[k]) - x
+        diff_e = jnp.where(last_cell, cell, next_cell[k]) - x
+        scale = lax.rsqrt(diff_a * diff_a + diff_b * diff_b + diff_e * diff_e + SMOOTHING)
+        unit_a[k], unit_b[k], unit_e[k] = diff_a * scale, diff_b * scale, diff_e * scale
+        slope[k] = unit_before[k] - (diff_a + diff_b + diff_e) * scale
+    past_row = {k: pltpu.roll(x, 1, 0) for k, x in unit_b.items()}
+    past_cell = {k: pltpu.roll(x, 1, 1) for k, x in unit_e.items()}
+    for i, t in here:
+        k = (i, t)
+        rim = unit_at_rim(here[k]) if i == 0 or t == 0 else None
+        row = past_row[i - 1, t] if i else rim
+        cell = past_cell[i, t - 1] if t else rim
+        slope[k] += jnp.where(first_row, row, past_row[k])
+        slope[k] += jnp.where(first_cell, cell, past_cell[k])
+    return slope, unit_a
+
+
+def smooth_kernel(sizes, near_ref, far_ref, exact_ref, out_ref, seen_ref, field, slopes, units):
     slabs, bands, planes, rows, tiles, tvox = sizes
     slab, band = lax.axis_index("slab"), lax.axis_index("xy")
-    depth, height, width = slabs * planes, bands * rows, tiles * tvox
+    depth, per = slabs * planes, rows // 8
+    size = bands * per, tiles
+    blocks = [(i, t) for i in range(size[0]) for t in range(size[1])]
+
+    views, own, unit, tdet = exact_ref.shape
+    for v in range(views):
+        for i in range(own):
+            for c in range(unit):
+                at = (i * unit + c) * tdet
+                seen_ref[v : v + 1, at : at + tdet] = exact_ref[v, i, c : c + 1, :]
 
     gap = jnp.zeros((rows, tvox), jnp.float32)
     for half, ref in enumerate((near_ref, far_ref)):
         for i in range(slabs // 2):
             for j in range(bands):
-                plane = (slab ^ (2 * i + half)) * planes
-                row = pl.multiple_of((band ^ j) * rows, rows)
+                plane, at = (slab ^ (2 * i + half)) * planes, (band ^ j) * per
                 for p in range(planes):
                     for t in range(tiles):
-                        field[plane + p, pl.ds(row, rows), t * tvox : (t + 1) * tvox] = ref[
-                            i, j, p * tiles + t
-                        ]
+                        tile = ref[i, j, p * tiles + t]
+                        for n in range(per):
+                            field[plane + p, at + n, t] = tile[8 * n : 8 * n + 8]
                 gap += ref[i, j, planes * tiles]
-    nothing = jnp.zeros((height, width), jnp.float32)
-    field[depth] = nothing
-    slopes[depth] = nothing
-    row_ids = lax.broadcasted_iota(jnp.int32, (height, width), 0)
-    cell_ids = lax.broadcasted_iota(jnp.int32, (height, width), 1)
-    rims = (row_ids == 0, row_ids == height - 1, cell_ids == 0, cell_ids == width - 1)
+    nothing = jnp.zeros((8, tvox), jnp.float32)
+    for i, t in blocks:
+        field[depth, i, t] = nothing
+        slopes[depth, i, t] = nothing
+    row_ids = lax.broadcasted_iota(jnp.int32, (8, tvox), 0)
+    cell_ids = lax.broadcasted_iota(jnp.int32, (8, tvox), 1)
+    masks = (row_ids == 0, row_ids == 7, cell_ids == 0, cell_ids == tvox - 1)
 
     def total(square):
         return jnp.sum(jnp.sum(square, axis=0, keepdims=True), axis=1, keepdims=True)
 
-    def fold(square):
-        return jnp.sum(
-            sum(square[:, t * tvox : (t + 1) * tvox] for t in range(tiles)).reshape(
-                height // 8, 8, tvox
-            ),
-            axis=0,
-        )
+    def finish(p, here, after, square):
+        before = {(i, t): units[i, t] for i, t in blocks}
+        slope, unit_a = slope_of(here, after, before, size, masks)
+        for i, t in blocks:
+            slopes[p, i, t] = slope[i, t]
+            units[i, t] = unit_a[i, t]
+            square = square + slope[i, t] * slope[i, t]
+        return square
 
     norm = jnp.sqrt(total(gap))
-
-    def one(p, carry):
-        unit_before, square = carry
-        slope, unit = slope_of(field[p], field[p + 1], unit_before, *rims)
-        slopes[p] = slope
-        return unit, square + fold(slope * slope)
-
-    start = unit_at_edge(field[0]), jnp.zeros((8, tvox), jnp.float32)
-    _, square = lax.fori_loop(0, depth, one, start)
+    unroll = 4 if depth % 4 == 0 and len(blocks) <= 16 else 1
+
+    def one(p, square):
+        here = {(i, t): field[p, i, t] for i, t in blocks}
+        after = {(i, t): field[p + 1, i, t] for i, t in blocks}
+        return finish(p, here, after, square)
+
+    for i, t in blocks:
+        units[i, t] = unit_at_rim(field[0, i, t])
+    square = lax.fori_loop(0, depth, one, nothing, unroll=unroll)
     step = TV_RATE * norm / jnp.sqrt(total(square) + 1e-06)
 
-    def two(p, carry):
-        unit_before, here, square = carry
-        after = field[p + 1] - step * slopes[p + 1]
-        slope, unit = slope_of(here, after, unit_before, *rims)
-        field[p] = here
-        slopes[p] = slope
-        return unit, after, square + fold(slope * slope)
-
-    here = field[0] - step * slopes[0]
-    start = unit_at_edge(here), here, jnp.zeros((8, tvox), jnp.float32)
-    _, _, square = lax.fori_loop(0, depth, two, start)
+    def two(p, square):
+        here = {(i, t): field[p, i, t] for i, t in blocks}
+        after = {(i, t): field[p + 1, i, t] - step * slopes[p + 1, i, t] for i, t in blocks}
+        for i, t in blocks:
+            field[p + 1, i, t] = after[i, t]
+        return finish(p, here, after, square)
+
+    for i, t in blocks:
+        here = field[0, i, t] - step * slopes[0, i, t]
+        field[0, i, t] = here
+        units[i, t] = unit_at_rim(here)
+    square = lax.fori_loop(0, depth, two, nothing, unroll=unroll)
     step = TV_RATE * norm / jnp.sqrt(total(square) + 1e-06)
-    mine = pl.ds(pl.multiple_of(band * rows, rows), rows)
     for p in range(planes):
-        out_ref[p] = field[slab * planes + p, mine, :] - step * slopes[slab * planes + p, mine, :]
-
-
-def smooth(volume, near, far, slabs, bands, tiles):
+        for n in range(per):
+            for t in range(tiles):
+                at = slab * planes + p, band * per + n, t
+                out_ref[p, 8 * n : 8 * n + 8, t * tvox : (t + 1) * tvox] = (
+                    field[at] - step * slopes[at]
+                )
+
+
+def smooth(volume, near, far, exact, slabs, bands, tiles):
     planes, rows, cells = volume.shape
+    views, own, unit, tdet = exact.shape
     sizes = slabs, bands, planes, rows, tiles, cells // tiles
-    whole = (slabs * planes + 1, bands * rows, cells)
+    plane = bands * rows // 8, tiles, 8, cells // tiles
     return pl.pallas_call(
         functools.partial(smooth_kernel, sizes),
-        out_shape=jax.ShapeDtypeStruct(volume.shape, jnp.float32),
-        in_specs=[pl.BlockSpec(memory_space=pltpu.VMEM)] * 2,
-        out_specs=pl.BlockSpec(memory_space=pltpu.VMEM),
-        scratch_shapes=[pltpu.VMEM(whole, jnp.float32)] * 2,
+        out_shape=(
+            jax.ShapeDtypeStruct(volume.shape, jnp.float32),
+            jax.ShapeDtypeStruct((views, own * unit * tdet), jnp.float32),
+        ),
+        in_specs=in_vmem(3),
+        out_specs=tuple(in_vmem(2)),
+        scratch_shapes=[
+            pltpu.VMEM((slabs * planes + 1,) + plane, jnp.float32),
+            pltpu.VMEM((slabs * planes + 1,) + plane, jnp.float32),
+            pltpu.VMEM(plane, jnp.float32),
+        ],
         compiler_params=pltpu.CompilerParams(vmem_limit_bytes=VMEM_BYTES),
         name="smooth",
-    )(near, far)
+    )(near, far, exact)
 
 
 def body(volume, footprint, tile_block, tile_cells, measured):
@@ -424,15 +462,14 @@
     below, above = shift_all(high, "slab", 1), shift_all(low, "slab", -1)
     chunks = shares(plan, packed, below, above)
     parts = [chunks[0]] + [swap_all(chunks[flip], "xy", flip) for flip in range(1, bands)]
-    correction, rounded = correct(plan, seen, parts)
+    exact, rounded = correct(plan, seen, parts)
     parts = [rounded] + [swap_all(rounded, "xy", flip) for flip in range(1, bands)]
     tiled = back_project(plan, volume, footprint, block, cells, parts)
 
     line = jnp.stack([tiled] + [swap_all(tiled, "xy", flip) for flip in range(1, bands)])
     near = jnp.stack([line] + [swap_all(line, "slab", flip) for flip in range(2, slabs, 2)])
     far = swap_all(near, "slab", 1)
-    updated = smooth(volume, near, far, slabs, bands, footprint.shape[2])
-    return (updated, correction)
+    return smooth(volume, near, far, exact, slabs, bands, footprint.shape[2])
 
 
 def solution(mesh):

time: 58.3 us -> 54.2 us (0.930)
  Pallas kernels: 15.7 us -> 11.5 us
    pallas_call x1, Pallas kernels: 6.78 us -> 3.24 us  [smooth(): pl.pallas_call(functools.partial(smooth_kernel, sizes), out_shape=(jax.Sh...]
    pallas_call x1, Pallas kernels: 0.67 us -> 0.05 us  [correct(): pl.pallas_call(functools.partial(correct_kernel, plan), out_shape=(jax.Sh...]
where the time goes in v3:
time: 54.2 us; the launch traced here: 54 us
  starting transfers between devices  20.9 us (39%)
  waiting for transfers between devices  20.8 us (38%)
  Pallas kernels  11.5 us (21%)
  between operations  0.72 us (1%)
    ppermute x13, waiting for transfers between devices, swap_all(): return lax.ppermute(cells, axis, [(i, i ^ flip) for i in range(count)])  19 us
    ppermute x13, starting transfers between devices, swap_all(): return lax.ppermute(cells, axis, [(i, i ^ flip) for i in range(count)])  17.5 us
    pallas_call x1, Pallas kernels, project(): pl.pallas_call(functools.partial(project_kernel, plan, shape), out_shape=...  5.03 us
    ppermute x2, starting transfers between devices, shift_all(): lax.ppermute(cells, axis, [(i, (i + step) % count) for i in range(count)])  3.45 us
    pallas_call x1, Pallas kernels, smooth(): pl.pallas_call(functools.partial(smooth_kernel, sizes), out_shape=(jax.Sh...  3.24 us
    pallas_call x1, Pallas kernels, back_project(): pl.pallas_call(functools.partial(back_kernel, plan, shape), out_shape=jax...  3.14 us
    ppermute x2, waiting for transfers between devices, shift_all(): lax.ppermute(cells, axis, [(i, (i + step) % count) for i in range(count)])  1.75 us
  transfers between devices with their start and end apart: 15, of which 11 were waited for; matrix products, arithmetic and copies ran while one was open for 0% of the time, Pallas kernels for 0%

profile of v3, /device:TPU:0, one launch (start us, length us, event | category | flops | bytes accessed | tf_op | source)
XLA Modules:
  0.0 54.0 jit_solution(9410417713496342845)
XLA Ops:
  0.7 5.0 %project.1 = (f32[10,24,256]{2,1,0:T(8,128)S(1)}, f32[2,24,256]{2,1,0:T(8,128)S(1)}, f32[2,24,256]{2,1,0:T(8,128)S(1)}, f32[2,3,8,256]{3,2,1,0:T(8,128)S(1)}, bf16[2,8,4,2,128,256]{5,4,3,2,1,0:T(8,128)(2,1)S(1)}) custom-call(f32[2,8,512]{2,1,0:T(8,128)} %vol_any.1, bf16[2,8,4,2,128,256]{5,4,3,2,1,0:T(8,128)(2,1)} %foot_hbm.1, s32[2,4,2,8]{3,2,1,0:T(2,128)} %bitcast.12, ...), custom_call_target="tpu_custom_call" | custom-call | tf_op jit(solution)/shard_map/project/pallas_call | solution.py:147
  5.7 0.5 collective-permute-start
  6.2 2.9 %collective-permute-start.1 = (f32[2,24,256]{2,1,0:T(8,128)S(1)}, f32[2,24,256]{2,1,0:T(8,128)S(1)}, u32[]{:S(2)}, u32[]{:S(2)}) collective-permute-start(f32[2,24,256]{2,1,0:T(8,128)S(1)} %get-tuple-element.17), channel_id=1, source_target_pairs={{0,28},{4,0},{8,4},{12,8},{16,12},{20,16},{24,20},{28,24},{1,29},{... | collective-permute-start | bytes 147464 | tf_op jit(solution)/shard_map/ppermute | solution.py:44
  9.2 1.7 %collective-permute-done.below_ref = f32[2,24,256]{2,1,0:T(8,128)S(1)} collective-permute-done((f32[2,24,256]{2,1,0:T(8,128)S(1)}, f32[2,24,256]{2,1,0:T(8,128)S(1)}, u32[]{:S(2)}, u32[]{:S(2)}) %collective-permute-start) | collective-permute-done | bytes 49184 | tf_op jit(solution)/shard_map/ppermute | solution.py:44
  10.9 0.0 collective-permute-done.1.above_ref
  10.9 0.1 shares.1
  11.0 2.4 %collective-permute-start.2 = (f32[3,24,256]{2,1,0:T(8,128)S(1)}, f32[3,24,256]{2,1,0:T(8,128)S(1)}, u32[]{:S(2)}, u32[]{:S(2)}) collective-permute-start(f32[3,24,256]{2,1,0:T(8,128)S(1)} %get-tuple-element.19), channel_id=1, source_target_pairs={{0,1},{1,0},{2,3},{3,2},{4,5},{5,4},{6,7},{7,6},{8,9},{9,8},{10,11... | collective-permute-start | bytes 221192 | tf_op jit(solution)/shard_map/ppermute | solution.py:49
  13.3 2.6 %collective-permute-start.3 = (f32[3,24,256]{2,1,0:T(8,128)S(1)}, f32[3,24,256]{2,1,0:T(8,128)S(1)}, u32[]{:S(2)}, u32[]{:S(2)}) collective-permute-start(f32[3,24,256]{2,1,0:T(8,128)S(1)} %get-tuple-element.20), channel_id=1, source_target_pairs={{0,2},{1,3},{2,0},{3,1},{4,6},{5,7},{6,4},{7,5},{8,10},{9,11},{10,... | collective-permute-start | bytes 221192 | tf_op jit(solution)/shard_map/ppermute | solution.py:49
  15.9 0.0 collective-permute-start.4
  15.9 0.3 collective-permute-done.2.rest_1_
  16.3 6.1 %collective-permute-done.3.rest_2_ = f32[3,24,256]{2,1,0:T(8,128)S(1)} collective-permute-done((f32[3,24,256]{2,1,0:T(8,128)S(1)}, f32[3,24,256]{2,1,0:T(8,128)S(1)}, u32[]{:S(2)}, u32[]{:S(2)}) %collective-permute-start.3) | collective-permute-done | bytes 73760 | tf_op jit(solution)/shard_map/ppermute | solution.py:49
  22.4 0.0 collective-permute-done.4.rest_3_
  22.4 2.7 %collective-permute-start.7 = (bf16[48,256]{1,0:T(8,128)(2,1)S(1)}, bf16[48,256]{1,0:T(8,128)(2,1)S(1)}, u32[]{:S(2)}, u32[]{:S(2)}) collective-permute-start(bf16[48,256]{1,0:T(8,128)(2,1)S(1)} %get-tuple-element.22.rest_0_), channel_id=1, source_target_pairs={{0,3},{1,2},{2,1},{3,0},{4,7},{5,6},{6,5},{7,4},{8,11},{9,10},{10,... | collective-permute-start | bytes 73736 | tf_op jit(solution)/shard_map/ppermute | solution.py:49
  25.1 0.6 %collective-permute-start.6 = (bf16[48,256]{1,0:T(8,128)(2,1)S(1)}, bf16[48,256]{1,0:T(8,128)(2,1)S(1)}, u32[]{:S(2)}, u32[]{:S(2)}) collective-permute-start(bf16[48,256]{1,0:T(8,128)(2,1)S(1)} %get-tuple-element.22.rest_0_), channel_id=1, source_target_pairs={{0,2},{1,3},{2,0},{3,1},{4,6},{5,7},{6,4},{7,5},{8,10},{9,11},{10,... | collective-permute-start | bytes 73736 | tf_op jit(solution)/shard_map/ppermute | solution.py:49
  25.7 1.2 %collective-permute-start.5 = (bf16[48,256]{1,0:T(8,128)(2,1)S(1)}, bf16[48,256]{1,0:T(8,128)(2,1)S(1)}, u32[]{:S(2)}, u32[]{:S(2)}) collective-permute-start(bf16[48,256]{1,0:T(8,128)(2,1)S(1)} %get-tuple-element.22.rest_0_), channel_id=1, source_target_pairs={{0,1},{1,0},{2,3},{3,2},{4,5},{5,4},{6,7},{7,6},{8,9},{9,8},{10,11... | collective-permute-start | bytes 73736 | tf_op jit(solution)/shard_map/ppermute | solution.py:49
  26.9 1.3 %collective-permute-done.7.rest_3_ = bf16[48,256]{1,0:T(8,128)(2,1)S(1)} collective-permute-done((bf16[48,256]{1,0:T(8,128)(2,1)S(1)}, bf16[48,256]{1,0:T(8,128)(2,1)S(1)}, u32[]{:S(2)}, u32[]{:S(2)}) %collective-permute-start.7) | collective-permute-done | bytes 24608 | tf_op jit(solution)/shard_map/ppermute | solution.py:49
  28.2 1.7 %collective-permute-done.6.rest_2_ = bf16[48,256]{1,0:T(8,128)(2,1)S(1)} collective-permute-done((bf16[48,256]{1,0:T(8,128)(2,1)S(1)}, bf16[48,256]{1,0:T(8,128)(2,1)S(1)}, u32[]{:S(2)}, u32[]{:S(2)}) %collective-permute-start.6) | collective-permute-done | bytes 24608 | tf_op jit(solution)/shard_map/ppermute | solution.py:49
  29.8 3.1 %back_project.1 = f32[9,8,128]{2,1,0:T(8,128)S(1)} custom-call(f32[2,8,512]{2,1,0:T(8,128)S(1)} %copy-done, bf16[2,8,4,2,128,256]{5,4,3,2,1,0:T(8,128)(2,1)S(1)} %get-tuple-element.13.foot, s32[2,4,2,8]{3,2,1,0:T(2,128)S(1)} %bitcast.13, s32[2,4,2,8]{3,2,1,0:T(2,128)S(1)} %bitcast.15, bf16[48,256]{1,0:T(8,128)(2,1)S(1)} %get-tuple-element.22.rest_0_, ...), custom_call_target="tpu_custom_call" | custom-call | tf_op jit(solution)/shard_map/back_project/pallas_call | solution.py:299
  33.0 2.3 %collective-permute-start.10 = (f32[9,8,128]{2,1,0:T(8,128)S(1)}, f32[9,8,128]{2,1,0:T(8,128)S(1)}, u32[]{:S(2)}, u32[]{:S(2)}) collective-permute-start(f32[9,8,128]{2,1,0:T(8,128)S(1)} %back_project.1), channel_id=1, source_target_pairs={{0,3},{1,2},{2,1},{3,0},{4,7},{5,6},{6,5},{7,4},{8,11},{9,10},{10,... | collective-permute-start | bytes 110600 | tf_op jit(solution)/shard_map/ppermute | solution.py:49
  35.3 0.1 collective-permute-start.9
  35.4 2.0 %collective-permute-start.8 = (f32[9,8,128]{2,1,0:T(8,128)S(1)}, f32[9,8,128]{2,1,0:T(8,128)S(1)}, u32[]{:S(2)}, u32[]{:S(2)}) collective-permute-start(f32[9,8,128]{2,1,0:T(8,128)S(1)} %back_project.1), channel_id=1, source_target_pairs={{0,1},{1,0},{2,3},{3,2},{4,5},{5,4},{6,7},{7,6},{8,9},{9,8},{10,11... | collective-permute-start | bytes 110600 | tf_op jit(solution)/shard_map/ppermute | solution.py:49
  37.5 1.4 %collective-permute-done.10 = f32[9,8,128]{2,1,0:T(8,128)S(1)} collective-permute-done((f32[9,8,128]{2,1,0:T(8,128)S(1)}, f32[9,8,128]{2,1,0:T(8,128)S(1)}, u32[]{:S(2)}, u32[]{:S(2)}) %collective-permute-start.10) | collective-permute-done | bytes 36896 | tf_op jit(solution)/shard_map/ppermute | solution.py:49
  38.8 1.5 %collective-permute-done.9 = f32[9,8,128]{2,1,0:T(8,128)S(1)} collective-permute-done((f32[9,8,128]{2,1,0:T(8,128)S(1)}, f32[9,8,128]{2,1,0:T(8,128)S(1)}, u32[]{:S(2)}, u32[]{:S(2)}) %collective-permute-start.9) | collective-permute-done | bytes 36896 | tf_op jit(solution)/shard_map/ppermute | solution.py:49
  40.4 1.6 %collective-permute-start.12 = (f32[4,9,8,128]{3,2,1,0:T(8,128)S(1)}, f32[4,9,8,128]{3,2,1,0:T(8,128)S(1)}, u32[]{:S(2)}, u32[]{:S(2)}) collective-permute-start(f32[4,9,8,128]{3,2,1,0:T(8,128)S(1)} %get-tuple-element.25), channel_id=1, source_target_pairs={{0,16},{4,20},{8,24},{12,28},{16,0},{20,4},{24,8},{28,12},{1,17},{... | collective-permute-start | bytes 442376 | tf_op jit(solution)/shard_map/ppermute | solution.py:49
  41.9 0.7 %collective-permute-start.11 = (f32[4,9,8,128]{3,2,1,0:T(8,128)S(1)}, f32[4,9,8,128]{3,2,1,0:T(8,128)S(1)}, u32[]{:S(2)}, u32[]{:S(2)}) collective-permute-start(f32[4,9,8,128]{3,2,1,0:T(8,128)S(1)} %get-tuple-element.25), channel_id=1, source_target_pairs={{0,8},{4,12},{8,0},{12,4},{16,24},{20,28},{24,16},{28,20},{1,9},{5... | collective-permute-start | bytes 442376 | tf_op jit(solution)/shard_map/ppermute | solution.py:49
  42.6 1.3 %collective-permute-start.13 = (f32[4,9,8,128]{3,2,1,0:T(8,128)S(1)}, f32[4,9,8,128]{3,2,1,0:T(8,128)S(1)}, u32[]{:S(2)}, u32[]{:S(2)}) collective-permute-start(f32[4,9,8,128]{3,2,1,0:T(8,128)S(1)} %get-tuple-element.25), channel_id=1, source_target_pairs={{0,24},{4,28},{8,16},{12,20},{16,8},{20,12},{24,0},{28,4},{1,25},{... | collective-permute-start | bytes 442376 | tf_op jit(solution)/shard_map/ppermute | solution.py:49
  43.9 2.4 %collective-permute-done.12 = f32[4,9,8,128]{3,2,1,0:T(8,128)S(1)} collective-permute-done((f32[4,9,8,128]{3,2,1,0:T(8,128)S(1)}, f32[4,9,8,128]{3,2,1,0:T(8,128)S(1)}, u32[]{:S(2)}, u32[]{:S(2)}) %collective-permute-start.12) | collective-permute-done | bytes 147488 | tf_op jit(solution)/shard_map/ppermute | solution.py:49
  46.3 0.7 %collective-permute-done.11 = f32[4,9,8,128]{3,2,1,0:T(8,128)S(1)} collective-permute-done((f32[4,9,8,128]{3,2,1,0:T(8,128)S(1)}, f32[4,9,8,128]{3,2,1,0:T(8,128)S(1)}, u32[]{:S(2)}, u32[]{:S(2)}) %collective-permute-start.11) | collective-permute-done | bytes 147488 | tf_op jit(solution)/shard_map/ppermute | solution.py:49
  47.1 1.6 %collective-permute-done.13 = f32[4,9,8,128]{3,2,1,0:T(8,128)S(1)} collective-permute-done((f32[4,9,8,128]{3,2,1,0:T(8,128)S(1)}, f32[4,9,8,128]{3,2,1,0:T(8,128)S(1)}, u32[]{:S(2)}, u32[]{:S(2)}) %collective-permute-start.13) | collective-permute-done | bytes 147488 | tf_op jit(solution)/shard_map/ppermute | solution.py:49
  48.7 0.1 collective-permute-start.14
  48.8 2.0 %collective-permute-done.14.far_ref = f32[4,4,9,8,128]{4,3,2,1,0:T(8,128)S(1)} collective-permute-done((f32[4,4,9,8,128]{4,3,2,1,0:T(8,128)S(1)}, f32[4,4,9,8,128]{4,3,2,1,0:T(8,128)S(1)}, u32[]{:S(2)}, u32[]{:S(2)}) %collective-permute-start.14) | collective-permute-done | bytes 589856 | tf_op jit(solution)/shard_map/ppermute | solution.py:49
  50.8 3.2 %smooth.1 = (f32[2,8,512]{2,1,0:T(8,128)}, f32[2,4096]{1,0:T(2,128)}) custom-call(f32[4,4,9,8,128]{4,3,2,1,0:T(8,128)S(1)} %pad_maximum_fusion.near_ref, f32[4,4,9,8,128]{4,3,2,1,0:T(8,128)S(1)} %collective-permute-done.14.far_ref, f32[2,2,8,256]{3,2,1,0:T(8,128)S(1)} %get-tuple-element.23.exact_ref), custom_call_target="tpu_custom_call" | custom-call | tf_op jit(solution)/shard_map/smooth/pallas_call | solution.py:435
  (11 shorter events, 0.1 us)
Async XLA Ops:
  0.6 29.2 %copy-start = (f32[2,8,512]{2,1,0:T(8,128)S(1)}, f32[2,8,512]{2,1,0:T(8,128)}, u32[]{:S(2)}) copy-start(f32[2,8,512]{2,1,0:T(8,128)} %vol_any.1) | copy-start | bytes 98308
  0.6 29.2 %copy-start.2 = (s32[2,8,4,2]{1,3,2,0:T(2,128)S(1)}, s32[2,8,4,2]{1,3,2,0:T(2,128)}, u32[]{:S(2)}) copy-start(s32[2,8,4,2]{1,3,2,0:T(2,128)} %param.8) | copy-start | bytes 1540
  0.7 29.2 %copy-start.1 = (s32[2,8,4,2]{1,3,2,0:T(2,128)S(1)}, s32[2,8,4,2]{1,3,2,0:T(2,128)}, u32[]{:S(2)}) copy-start(s32[2,8,4,2]{1,3,2,0:T(2,128)} %param.7) | copy-start | bytes 1540
  5.7 5.2 %collective-permute-start = (f32[2,24,256]{2,1,0:T(8,128)S(1)}, f32[2,24,256]{2,1,0:T(8,128)S(1)}, u32[]{:S(2)}, u32[]{:S(2)}) collective-permute-start(f32[2,24,256]{2,1,0:T(8,128)S(1)} %get-tuple-element.16), channel_id=1, source_target_pairs={{0,4},{4,8},{8,12},{12,16},{16,20},{20,24},{24,28},{28,0},{1,5},{5... | collective-permute-start | bytes 147464 | tf_op jit(solution)/shard_map/ppermute | solution.py:44
  6.2 4.7 %collective-permute-start.1 = (f32[2,24,256]{2,1,0:T(8,128)S(1)}, f32[2,24,256]{2,1,0:T(8,128)S(1)}, u32[]{:S(2)}, u32[]{:S(2)}) collective-permute-start(f32[2,24,256]{2,1,0:T(8,128)S(1)} %get-tuple-element.17), channel_id=1, source_target_pairs={{0,28},{4,0},{8,4},{12,8},{16,12},{20,16},{24,20},{28,24},{1,29},{... | collective-permute-start | bytes 147464 | tf_op jit(solution)/shard_map/ppermute | solution.py:44
  11.0 5.3 %collective-permute-start.2 = (f32[3,24,256]{2,1,0:T(8,128)S(1)}, f32[3,24,256]{2,1,0:T(8,128)S(1)}, u32[]{:S(2)}, u32[]{:S(2)}) collective-permute-start(f32[3,24,256]{2,1,0:T(8,128)S(1)} %get-tuple-element.19), channel_id=1, source_target_pairs={{0,1},{1,0},{2,3},{3,2},{4,5},{5,4},{6,7},{7,6},{8,9},{9,8},{10,11... | collective-permute-start | bytes 221192 | tf_op jit(solution)/shard_map/ppermute | solution.py:49
  13.3 9.1 %collective-permute-start.3 = (f32[3,24,256]{2,1,0:T(8,128)S(1)}, f32[3,24,256]{2,1,0:T(8,128)S(1)}, u32[]{:S(2)}, u32[]{:S(2)}) collective-permute-start(f32[3,24,256]{2,1,0:T(8,128)S(1)} %get-tuple-element.20), channel_id=1, source_target_pairs={{0,2},{1,3},{2,0},{3,1},{4,6},{5,7},{6,4},{7,5},{8,10},{9,11},{10,... | collective-permute-start | bytes 221192 | tf_op jit(solution)/shard_map/ppermute | solution.py:49
  15.9 6.5 %collective-permute-start.4 = (f32[3,24,256]{2,1,0:T(8,128)S(1)}, f32[3,24,256]{2,1,0:T(8,128)S(1)}, u32[]{:S(2)}, u32[]{:S(2)}) collective-permute-start(f32[3,24,256]{2,1,0:T(8,128)S(1)} %get-tuple-element.21), channel_id=1, source_target_pairs={{0,3},{1,2},{2,1},{3,0},{4,7},{5,6},{6,5},{7,4},{8,11},{9,10},{10,... | collective-permute-start | bytes 221192 | tf_op jit(solution)/shard_map/ppermute | solution.py:49
  22.4 5.7 %collective-permute-start.7 = (bf16[48,256]{1,0:T(8,128)(2,1)S(1)}, bf16[48,256]{1,0:T(8,128)(2,1)S(1)}, u32[]{:S(2)}, u32[]{:S(2)}) collective-permute-start(bf16[48,256]{1,0:T(8,128)(2,1)S(1)} %get-tuple-element.22.rest_0_), channel_id=1, source_target_pairs={{0,3},{1,2},{2,1},{3,0},{4,7},{5,6},{6,5},{7,4},{8,11},{9,10},{10,... | collective-permute-start | bytes 73736 | tf_op jit(solution)/shard_map/ppermute | solution.py:49
  25.1 4.7 %collective-permute-start.6 = (bf16[48,256]{1,0:T(8,128)(2,1)S(1)}, bf16[48,256]{1,0:T(8,128)(2,1)S(1)}, u32[]{:S(2)}, u32[]{:S(2)}) collective-permute-start(bf16[48,256]{1,0:T(8,128)(2,1)S(1)} %get-tuple-element.22.rest_0_), channel_id=1, source_target_pairs={{0,2},{1,3},{2,0},{3,1},{4,6},{5,7},{6,4},{7,5},{8,10},{9,11},{10,... | collective-permute-start | bytes 73736 | tf_op jit(solution)/shard_map/ppermute | solution.py:49
  25.7 4.1 %collective-permute-start.5 = (bf16[48,256]{1,0:T(8,128)(2,1)S(1)}, bf16[48,256]{1,0:T(8,128)(2,1)S(1)}, u32[]{:S(2)}, u32[]{:S(2)}) collective-permute-start(bf16[48,256]{1,0:T(8,128)(2,1)S(1)} %get-tuple-element.22.rest_0_), channel_id=1, source_target_pairs={{0,1},{1,0},{2,3},{3,2},{4,5},{5,4},{6,7},{7,6},{8,9},{9,8},{10,11... | collective-permute-start | bytes 73736 | tf_op jit(solution)/shard_map/ppermute | solution.py:49
  33.0 5.8 %collective-permute-start.10 = (f32[9,8,128]{2,1,0:T(8,128)S(1)}, f32[9,8,128]{2,1,0:T(8,128)S(1)}, u32[]{:S(2)}, u32[]{:S(2)}) collective-permute-start(f32[9,8,128]{2,1,0:T(8,128)S(1)} %back_project.1), channel_id=1, source_target_pairs={{0,3},{1,2},{2,1},{3,0},{4,7},{5,6},{6,5},{7,4},{8,11},{9,10},{10,... | collective-permute-start | bytes 110600 | tf_op jit(solution)/shard_map/ppermute | solution.py:49
  35.3 5.0 %collective-permute-start.9 = (f32[9,8,128]{2,1,0:T(8,128)S(1)}, f32[9,8,128]{2,1,0:T(8,128)S(1)}, u32[]{:S(2)}, u32[]{:S(2)}) collective-permute-start(f32[9,8,128]{2,1,0:T(8,128)S(1)} %back_project.1), channel_id=1, source_target_pairs={{0,2},{1,3},{2,0},{3,1},{4,6},{5,7},{6,4},{7,5},{8,10},{9,11},{10,... | collective-permute-start | bytes 110600 | tf_op jit(solution)/shard_map/ppermute | solution.py:49
  35.4 4.9 %collective-permute-start.8 = (f32[9,8,128]{2,1,0:T(8,128)S(1)}, f32[9,8,128]{2,1,0:T(8,128)S(1)}, u32[]{:S(2)}, u32[]{:S(2)}) collective-permute-start(f32[9,8,128]{2,1,0:T(8,128)S(1)} %back_project.1), channel_id=1, source_target_pairs={{0,1},{1,0},{2,3},{3,2},{4,5},{5,4},{6,7},{7,6},{8,9},{9,8},{10,11... | collective-permute-start | bytes 110600 | tf_op jit(solution)/shard_map/ppermute | solution.py:49
  40.4 6.0 %collective-permute-start.12 = (f32[4,9,8,128]{3,2,1,0:T(8,128)S(1)}, f32[4,9,8,128]{3,2,1,0:T(8,128)S(1)}, u32[]{:S(2)}, u32[]{:S(2)}) collective-permute-start(f32[4,9,8,128]{3,2,1,0:T(8,128)S(1)} %get-tuple-element.25), channel_id=1, source_target_pairs={{0,16},{4,20},{8,24},{12,28},{16,0},{20,4},{24,8},{28,12},{1,17},{... | collective-permute-start | bytes 442376 | tf_op jit(solution)/shard_map/ppermute | solution.py:49
  41.9 5.1 %collective-permute-start.11 = (f32[4,9,8,128]{3,2,1,0:T(8,128)S(1)}, f32[4,9,8,128]{3,2,1,0:T(8,128)S(1)}, u32[]{:S(2)}, u32[]{:S(2)}) collective-permute-start(f32[4,9,8,128]{3,2,1,0:T(8,128)S(1)} %get-tuple-element.25), channel_id=1, source_target_pairs={{0,8},{4,12},{8,0},{12,4},{16,24},{20,28},{24,16},{28,20},{1,9},{5... | collective-permute-start | bytes 442376 | tf_op jit(solution)/shard_map/ppermute | solution.py:49
  42.6 6.0 %collective-permute-start.13 = (f32[4,9,8,128]{3,2,1,0:T(8,128)S(1)}, f32[4,9,8,128]{3,2,1,0:T(8,128)S(1)}, u32[]{:S(2)}, u32[]{:S(2)}) collective-permute-start(f32[4,9,8,128]{3,2,1,0:T(8,128)S(1)} %get-tuple-element.25), channel_id=1, source_target_pairs={{0,24},{4,28},{8,16},{12,20},{16,8},{20,12},{24,0},{28,4},{1,25},{... | collective-permute-start | bytes 442376 | tf_op jit(solution)/shard_map/ppermute | solution.py:49
  48.7 2.1 %collective-permute-start.14 = (f32[4,4,9,8,128]{4,3,2,1,0:T(8,128)S(1)}, f32[4,4,9,8,128]{4,3,2,1,0:T(8,128)S(1)}, u32[]{:S(2)}, u32[]{:S(2)}) collective-permute-start(f32[4,4,9,8,128]{4,3,2,1,0:T(8,128)S(1)} %pad_maximum_fusion.near_ref), channel_id=1, source_target_pairs={{0,4},{4,0},{8,12},{12,8},{16,20},{20,16},{24,28},{28,24},{1,5},{5... | collective-permute-start | bytes 1769480 | tf_op jit(solution)/shard_map/ppermute | solution.py:49

commit v4 on v3

--- a/solution.py
+++ b/solution.py
@@ -44,6 +44,10 @@
     return lax.ppermute(cells, axis, [(i, (i + step) % count) for i in range(count)])
 
 
+def reduce_order(bands):
+    return [0] + [flip for flip in (3, 1, 2) if flip < bands] + list(range(4, bands))
+
+
 def swap_all(cells, axis, flip):
     count = lax.axis_size(axis)
     return lax.ppermute(cells, axis, [(i, i ^ flip) for i in range(count)])
@@ -58,6 +62,11 @@
 
 def copy_all(pairs, sems):
     return [pltpu.make_async_copy(src, dst, sems.at[n]) for n, (src, dst) in enumerate(pairs)]
+
+
+def stream_spans(planes, rows):
+    size = max(rows // 4, 1)
+    return [(p, r, min(size, rows - r)) for p in range(planes) for r in range(0, rows, size)]
 
 
 def project_kernel(
@@ -66,9 +75,7 @@
 ):
     planes, rows, tiles, views, tvox, tdet = shape
     slab, band = lax.axis_index("slab"), lax.axis_index("xy")
-    parts = sems.shape[0]
-    step = planes * rows // parts
-    spans = [(n * step // rows, pl.ds(n * step % rows, step)) for n in range(parts)]
+    spans = stream_spans(planes, rows)
     span = plan.unit * tdet
     own_at = (slab * plan.bands + band) * plan.own_units
     halo_at = jnp.where(
@@ -89,9 +96,12 @@
         ],
         small,
     )
-    stream = copy_all([(foot_hbm.at[p, at], foot.at[p, at]) for p, at in spans], sems)
-    for copy in first + stream:
+    stream = [(foot_hbm.at[p, pl.ds(r, n)], foot.at[p, pl.ds(r, n)]) for p, r, n in spans]
+    stream = copy_all(stream, sems)
+    for copy in first:
         copy.start()
+    for copy in stream:
+        copy.start(priority=1)
     acc[...] = jnp.zeros_like(acc)
     top = lax.broadcasted_iota(jnp.int32, (8, tvox), 0) == 0
     lane = lax.broadcasted_iota(jnp.int32, (8, tdet), 1)
@@ -103,9 +113,9 @@
                 at = (i * plan.unit + c) * tdet
                 seen_ref[v, i, c : c + 1, :] = seen[v : v + 1, at : at + tdet]
     starts = [plan.units * sum(plan.width[:v]) for v in range(views)]
-    for n in range(parts):
-        stream[n].wait()
-        for p, r in [divmod(n * step + k, rows) for k in range(step)]:
+    for copy, (p, begin, size) in zip(stream, spans):
+        copy.wait()
+        for r in range(begin, begin + size):
             for t in range(tiles):
                 voxels = vol_ref[p, r : r + 1, t * tvox : (t + 1) * tvox]
                 left = jnp.where(top, jnp.broadcast_to(voxels, (8, tvox)), 1.0)
@@ -136,9 +146,8 @@
 
 def project(plan, volume, footprint, tile_block, tile_cells, measured):
     shape = footprint.shape
-    planes, rows = shape[:2]
     views, tdet = plan.views, plan.tdet
-    parts = 2 * planes if rows % 2 == 0 else planes
+    parts = len(stream_spans(*shape[:2]))
     operands = [
         pltpu.with_memory_space_constraint(operand, pltpu.HBM)
         for operand in (volume, footprint, tile_block, tile_cells, measured)
@@ -210,7 +219,7 @@
             for q in range(2):
                 line = plan.base[v] + q * width
                 total = 0.0
-                for flip, part in enumerate(parts):
+                for flip, part in zip(reduce_order(plan.bands), parts):
                     piece = part[i, line : line + width, :]
                     if plan.is_narrow(v):
                         room = jnp.zeros((unit - width, tdet), jnp.float32)
@@ -363,15 +372,15 @@
 
     gap = jnp.zeros((rows, tvox), jnp.float32)
     for half, ref in enumerate((near_ref, far_ref)):
-        for i in range(slabs // 2):
+        for i, flip in enumerate(range(0, slabs, 2)):
             for j in range(bands):
-                plane, at = (slab ^ (2 * i + half)) * planes, (band ^ j) * per
+                plane, at = (slab ^ (flip + half)) * planes, (band ^ j) * per
                 for p in range(planes):
                     for t in range(tiles):
-                        tile = ref[i, j, p * tiles + t]
+                        tile = ref[i, (j * planes + p) * tiles + t]
                         for n in range(per):
                             field[plane + p, at + n, t] = tile[8 * n : 8 * n + 8]
-                gap += ref[i, j, planes * tiles]
+            gap += ref[i, bands * planes * tiles]
     nothing = jnp.zeros((8, tvox), jnp.float32)
     for i, t in blocks:
         field[depth, i, t] = nothing
@@ -461,12 +470,15 @@
     )
     below, above = shift_all(high, "slab", 1), shift_all(low, "slab", -1)
     chunks = shares(plan, packed, below, above)
-    parts = [chunks[0]] + [swap_all(chunks[flip], "xy", flip) for flip in range(1, bands)]
+    parts = [
+        swap_all(chunks[flip], "xy", flip) if flip else chunks[0] for flip in reduce_order(bands)
+    ]
     exact, rounded = correct(plan, seen, parts)
     parts = [rounded] + [swap_all(rounded, "xy", flip) for flip in range(1, bands)]
     tiled = back_project(plan, volume, footprint, block, cells, parts)
 
-    line = jnp.stack([tiled] + [swap_all(tiled, "xy", flip) for flip in range(1, bands)])
+    line = [tiled] + [swap_all(tiled, "xy", flip) for flip in range(1, bands)]
+    line = jnp.concatenate([each[:-1] for each in line] + [sum(each[-1:] for each in line)])
     near = jnp.stack([line] + [swap_all(line, "slab", flip) for flip in range(2, slabs, 2)])
     far = swap_all(near, "slab", 1)
     return smooth(volume, near, far, exact, slabs, bands, footprint.shape[2])

time: 54.2 us -> 51.8 us (0.956)
  waiting for transfers between devices: 20.8 us -> 19.4 us
  Pallas kernels: 11.5 us -> 10.4 us
    ppermute x13, waiting for transfers between devices: 19 us -> 17.6 us  [swap_all(): return lax.ppermute(cells, axis, [(i, i ^ flip) for i in range(count)])]
    pallas_call x1, Pallas kernels: 5.03 us -> 3.92 us  [project(): pl.pallas_call(functools.partial(project_kernel, plan, shape), out_shape=...]
  transfers between devices with their start and end apart: 15 -> 15, of which waited for: 11 -> 12; matrix products, arithmetic and copies ran while one was open for 0% -> 0% of each run, Pallas kernels for 0% -> 0%
where the time goes in v4:
time: 51.8 us; the launch traced here: 51.6 us
  starting transfers between devices  21 us (41%)
  waiting for transfers between devices  19.4 us (37%)
  Pallas kernels  10.4 us (20%)
  between operations  0.73 us (1%)
    ppermute x13, waiting for transfers between devices, swap_all(): return lax.ppermute(cells, axis, [(i, i ^ flip) for i in range(count)])  17.6 us
    ppermute x13, starting transfers between devices, swap_all(): return lax.ppermute(cells, axis, [(i, i ^ flip) for i in range(count)])  17.6 us
    pallas_call x1, Pallas kernels, project(): pl.pallas_call(functools.partial(project_kernel, plan, shape), out_shape=...  3.92 us
    ppermute x2, starting transfers between devices, shift_all(): lax.ppermute(cells, axis, [(i, (i + step) % count) for i in range(count)])  3.45 us
    pallas_call x1, Pallas kernels, smooth(): pl.pallas_call(functools.partial(smooth_kernel, sizes), out_shape=(jax.Sh...  3.24 us
    pallas_call x1, Pallas kernels, back_project(): pl.pallas_call(functools.partial(back_kernel, plan, shape), out_shape=jax...  3.14 us
    ppermute x2, waiting for transfers between devices, shift_all(): lax.ppermute(cells, axis, [(i, (i + step) % count) for i in range(count)])  1.75 us
  transfers between devices with their start and end apart: 15, of which 12 were waited for; matrix products, arithmetic and copies ran while one was open for 0% of the time, Pallas kernels for 0%

profile of v4, /device:TPU:0, one launch (start us, length us, event | category | flops | bytes accessed | tf_op | source)
XLA Modules:
  0.0 51.6 jit_solution(8895368510384279429)
XLA Ops:
  0.7 3.9 %project.1 = (f32[10,24,256]{2,1,0:T(8,128)S(1)}, f32[2,24,256]{2,1,0:T(8,128)S(1)}, f32[2,24,256]{2,1,0:T(8,128)S(1)}, f32[2,3,8,256]{3,2,1,0:T(8,128)S(1)}, bf16[2,8,4,2,128,256]{5,4,3,2,1,0:T(8,128)(2,1)S(1)}) custom-call(f32[2,8,512]{2,1,0:T(8,128)} %vol_any.1, bf16[2,8,4,2,128,256]{5,4,3,2,1,0:T(8,128)(2,1)} %foot_hbm.1, s32[2,4,2,8]{3,2,1,0:T(2,128)} %bitcast.6, ...), custom_call_target="tpu_custom_call" | custom-call | tf_op jit(solution)/shard_map/project/pallas_call | solution.py:156
  4.6 0.5 collective-permute-start
  5.1 2.9 %collective-permute-start.1 = (f32[2,24,256]{2,1,0:T(8,128)S(1)}, f32[2,24,256]{2,1,0:T(8,128)S(1)}, u32[]{:S(2)}, u32[]{:S(2)}) collective-permute-start(f32[2,24,256]{2,1,0:T(8,128)S(1)} %get-tuple-element.17), channel_id=1, source_target_pairs={{0,28},{4,0},{8,4},{12,8},{16,12},{20,16},{24,20},{28,24},{1,29},{... | collective-permute-start | bytes 147464 | tf_op jit(solution)/shard_map/ppermute | solution.py:44
  8.0 1.7 %collective-permute-done.below_ref = f32[2,24,256]{2,1,0:T(8,128)S(1)} collective-permute-done((f32[2,24,256]{2,1,0:T(8,128)S(1)}, f32[2,24,256]{2,1,0:T(8,128)S(1)}, u32[]{:S(2)}, u32[]{:S(2)}) %collective-permute-start) | collective-permute-done | bytes 49184 | tf_op jit(solution)/shard_map/ppermute | solution.py:44
  9.7 0.0 collective-permute-done.1.above_ref
  9.8 0.1 shares.1
  9.8 4.4 %collective-permute-start.2 = (f32[3,24,256]{2,1,0:T(8,128)S(1)}, f32[3,24,256]{2,1,0:T(8,128)S(1)}, u32[]{:S(2)}, u32[]{:S(2)}) collective-permute-start(f32[3,24,256]{2,1,0:T(8,128)S(1)} %get-tuple-element.19), channel_id=1, source_target_pairs={{0,3},{1,2},{2,1},{3,0},{4,7},{5,6},{6,5},{7,4},{8,11},{9,10},{10,... | collective-permute-start | bytes 221192 | tf_op jit(solution)/shard_map/ppermute | solution.py:53
  14.2 0.0 collective-permute-start.3
  14.2 0.6 %collective-permute-start.4 = (f32[3,24,256]{2,1,0:T(8,128)S(1)}, f32[3,24,256]{2,1,0:T(8,128)S(1)}, u32[]{:S(2)}, u32[]{:S(2)}) collective-permute-start(f32[3,24,256]{2,1,0:T(8,128)S(1)} %get-tuple-element.21), channel_id=1, source_target_pairs={{0,2},{1,3},{2,0},{3,1},{4,6},{5,7},{6,4},{7,5},{8,10},{9,11},{10,... | collective-permute-start | bytes 221192 | tf_op jit(solution)/shard_map/ppermute | solution.py:53
  14.9 2.6 %collective-permute-done.2.rest_1_ = f32[3,24,256]{2,1,0:T(8,128)S(1)} collective-permute-done((f32[3,24,256]{2,1,0:T(8,128)S(1)}, f32[3,24,256]{2,1,0:T(8,128)S(1)}, u32[]{:S(2)}, u32[]{:S(2)}) %collective-permute-start.2) | collective-permute-done | bytes 73760 | tf_op jit(solution)/shard_map/ppermute | solution.py:53
  17.4 2.8 %collective-permute-done.3.rest_2_ = f32[3,24,256]{2,1,0:T(8,128)S(1)} collective-permute-done((f32[3,24,256]{2,1,0:T(8,128)S(1)}, f32[3,24,256]{2,1,0:T(8,128)S(1)}, u32[]{:S(2)}, u32[]{:S(2)}) %collective-permute-start.3) | collective-permute-done | bytes 73760 | tf_op jit(solution)/shard_map/ppermute | solution.py:53
  20.3 1.1 %collective-permute-done.4.rest_3_ = f32[3,24,256]{2,1,0:T(8,128)S(1)} collective-permute-done((f32[3,24,256]{2,1,0:T(8,128)S(1)}, f32[3,24,256]{2,1,0:T(8,128)S(1)}, u32[]{:S(2)}, u32[]{:S(2)}) %collective-permute-start.4) | collective-permute-done | bytes 73760 | tf_op jit(solution)/shard_map/ppermute | solution.py:53
  21.4 1.4 %collective-permute-start.7 = (bf16[48,256]{1,0:T(8,128)(2,1)S(1)}, bf16[48,256]{1,0:T(8,128)(2,1)S(1)}, u32[]{:S(2)}, u32[]{:S(2)}) collective-permute-start(bf16[48,256]{1,0:T(8,128)(2,1)S(1)} %get-tuple-element.22.rest_0_), channel_id=1, source_target_pairs={{0,3},{1,2},{2,1},{3,0},{4,7},{5,6},{6,5},{7,4},{8,11},{9,10},{10,... | collective-permute-start | bytes 73736 | tf_op jit(solution)/shard_map/ppermute | solution.py:53
  22.9 0.5 collective-permute-start.6
  23.4 2.5 %collective-permute-start.5 = (bf16[48,256]{1,0:T(8,128)(2,1)S(1)}, bf16[48,256]{1,0:T(8,128)(2,1)S(1)}, u32[]{:S(2)}, u32[]{:S(2)}) collective-permute-start(bf16[48,256]{1,0:T(8,128)(2,1)S(1)} %get-tuple-element.22.rest_0_), channel_id=1, source_target_pairs={{0,1},{1,0},{2,3},{3,2},{4,5},{5,4},{6,7},{7,6},{8,9},{9,8},{10,11... | collective-permute-start | bytes 73736 | tf_op jit(solution)/shard_map/ppermute | solution.py:53
  25.9 1.2 %collective-permute-done.7.rest_3_ = bf16[48,256]{1,0:T(8,128)(2,1)S(1)} collective-permute-done((bf16[48,256]{1,0:T(8,128)(2,1)S(1)}, bf16[48,256]{1,0:T(8,128)(2,1)S(1)}, u32[]{:S(2)}, u32[]{:S(2)}) %collective-permute-start.7) | collective-permute-done | bytes 24608 | tf_op jit(solution)/shard_map/ppermute | solution.py:53
  27.1 0.5 collective-permute-done.6.rest_2_
  27.6 0.2 collective-permute-done.5.rest_1_
  27.9 3.1 %back_project.1 = f32[9,8,128]{2,1,0:T(8,128)S(1)} custom-call(f32[2,8,512]{2,1,0:T(8,128)S(1)} %copy-done, bf16[2,8,4,2,128,256]{5,4,3,2,1,0:T(8,128)(2,1)S(1)} %get-tuple-element.13.foot, s32[2,4,2,8]{3,2,1,0:T(2,128)S(1)} %bitcast.7, s32[2,4,2,8]{3,2,1,0:T(2,128)S(1)} %bitcast.9, bf16[48,256]{1,0:T(8,128)(2,1)S(1)} %get-tuple-element.22.rest_0_, ...), custom_call_target="tpu_custom_call" | custom-call | tf_op jit(solution)/shard_map/back_project/pallas_call | solution.py:308
  31.0 2.5 %collective-permute-start.10 = (f32[9,8,128]{2,1,0:T(8,128)S(1)}, f32[9,8,128]{2,1,0:T(8,128)S(1)}, u32[]{:S(2)}, u32[]{:S(2)}) collective-permute-start(f32[9,8,128]{2,1,0:T(8,128)S(1)} %back_project.1), channel_id=1, source_target_pairs={{0,3},{1,2},{2,1},{3,0},{4,7},{5,6},{6,5},{7,4},{8,11},{9,10},{10,... | collective-permute-start | bytes 110600 | tf_op jit(solution)/shard_map/ppermute | solution.py:53
  33.5 0.9 %collective-permute-start.9 = (f32[9,8,128]{2,1,0:T(8,128)S(1)}, f32[9,8,128]{2,1,0:T(8,128)S(1)}, u32[]{:S(2)}, u32[]{:S(2)}) collective-permute-start(f32[9,8,128]{2,1,0:T(8,128)S(1)} %back_project.1), channel_id=1, source_target_pairs={{0,2},{1,3},{2,0},{3,1},{4,6},{5,7},{6,4},{7,5},{8,10},{9,11},{10,... | collective-permute-start | bytes 110600 | tf_op jit(solution)/shard_map/ppermute | solution.py:53
  34.4 1.1 %collective-permute-start.8 = (f32[9,8,128]{2,1,0:T(8,128)S(1)}, f32[9,8,128]{2,1,0:T(8,128)S(1)}, u32[]{:S(2)}, u32[]{:S(2)}) collective-permute-start(f32[9,8,128]{2,1,0:T(8,128)S(1)} %back_project.1), channel_id=1, source_target_pairs={{0,1},{1,0},{2,3},{3,2},{4,5},{5,4},{6,7},{7,6},{8,9},{9,8},{10,11... | collective-permute-start | bytes 110600 | tf_op jit(solution)/shard_map/ppermute | solution.py:53
  35.5 3.3 %collective-permute-done.8 = f32[9,8,128]{2,1,0:T(8,128)S(1)} collective-permute-done((f32[9,8,128]{2,1,0:T(8,128)S(1)}, f32[9,8,128]{2,1,0:T(8,128)S(1)}, u32[]{:S(2)}, u32[]{:S(2)}) %collective-permute-start.8) | collective-permute-done | bytes 36896 | tf_op jit(solution)/shard_map/ppermute | solution.py:53
  38.8 1.3 %collective-permute-start.13 = (f32[33,8,128]{2,1,0:T(8,128)S(1)}, f32[33,8,128]{2,1,0:T(8,128)S(1)}, u32[]{:S(2)}, u32[]{:S(2)}) collective-permute-start(f32[33,8,128]{2,1,0:T(8,128)S(1)} %constant_dynamic-update-slice_fusion), channel_id=1, source_target_pairs={{0,24},{4,28},{8,16},{12,20},{16,8},{20,12},{24,0},{28,4},{1,25},{... | collective-permute-start | bytes 405512 | tf_op jit(solution)/shard_map/ppermute | solution.py:53
  40.1 0.8 %collective-permute-start.12 = (f32[33,8,128]{2,1,0:T(8,128)S(1)}, f32[33,8,128]{2,1,0:T(8,128)S(1)}, u32[]{:S(2)}, u32[]{:S(2)}) collective-permute-start(f32[33,8,128]{2,1,0:T(8,128)S(1)} %constant_dynamic-update-slice_fusion), channel_id=1, source_target_pairs={{0,16},{4,20},{8,24},{12,28},{16,0},{20,4},{24,8},{28,12},{1,17},{... | collective-permute-start | bytes 405512 | tf_op jit(solution)/shard_map/ppermute | solution.py:53
  40.9 1.4 %collective-permute-start.11 = (f32[33,8,128]{2,1,0:T(8,128)S(1)}, f32[33,8,128]{2,1,0:T(8,128)S(1)}, u32[]{:S(2)}, u32[]{:S(2)}) collective-permute-start(f32[33,8,128]{2,1,0:T(8,128)S(1)} %constant_dynamic-update-slice_fusion), channel_id=1, source_target_pairs={{0,8},{4,12},{8,0},{12,4},{16,24},{20,28},{24,16},{28,20},{1,9},{5... | collective-permute-start | bytes 405512 | tf_op jit(solution)/shard_map/ppermute | solution.py:53
  42.4 2.5 %collective-permute-done.13 = f32[33,8,128]{2,1,0:T(8,128)S(1)} collective-permute-done((f32[33,8,128]{2,1,0:T(8,128)S(1)}, f32[33,8,128]{2,1,0:T(8,128)S(1)}, u32[]{:S(2)}, u32[]{:S(2)}) %collective-permute-start.13) | collective-permute-done | bytes 135200 | tf_op jit(solution)/shard_map/ppermute | solution.py:53
  44.9 1.3 %collective-permute-done.12 = f32[33,8,128]{2,1,0:T(8,128)S(1)} collective-permute-done((f32[33,8,128]{2,1,0:T(8,128)S(1)}, f32[33,8,128]{2,1,0:T(8,128)S(1)}, u32[]{:S(2)}, u32[]{:S(2)}) %collective-permute-start.12) | collective-permute-done | bytes 135200 | tf_op jit(solution)/shard_map/ppermute | solution.py:53
  46.2 0.1 collective-permute-done.11
  46.4 0.1 collective-permute-start.14
  46.4 1.9 %collective-permute-done.14.far_ref = f32[4,33,8,128]{3,2,1,0:T(8,128)S(1)} collective-permute-done((f32[4,33,8,128]{3,2,1,0:T(8,128)S(1)}, f32[4,33,8,128]{3,2,1,0:T(8,128)S(1)}, u32[]{:S(2)}, u32[]{:S(2)}) %collective-permute-start.14) | collective-permute-done | bytes 540704 | tf_op jit(solution)/shard_map/ppermute | solution.py:53
  48.4 3.2 %smooth.1 = (f32[2,8,512]{2,1,0:T(8,128)}, f32[2,4096]{1,0:T(2,128)}) custom-call(f32[4,33,8,128]{3,2,1,0:T(8,128)S(1)} %pad_maximum_fusion.near_ref, f32[4,33,8,128]{3,2,1,0:T(8,128)S(1)} %collective-permute-done.14.far_ref, f32[2,2,8,256]{3,2,1,0:T(8,128)S(1)} %get-tuple-element.23.exact_ref), custom_call_target="tpu_custom_call" | custom-call | tf_op jit(solution)/shard_map/smooth/pallas_call | solution.py:444
  (15 shorter events, 0.1 us)
Async XLA Ops:
  0.6 27.2 %copy-start = (f32[2,8,512]{2,1,0:T(8,128)S(1)}, f32[2,8,512]{2,1,0:T(8,128)}, u32[]{:S(2)}) copy-start(f32[2,8,512]{2,1,0:T(8,128)} %vol_any.1) | copy-start | bytes 98308
  0.6 27.2 %copy-start.2 = (s32[2,8,4,2]{1,3,2,0:T(2,128)S(1)}, s32[2,8,4,2]{1,3,2,0:T(2,128)}, u32[]{:S(2)}) copy-start(s32[2,8,4,2]{1,3,2,0:T(2,128)} %param.8) | copy-start | bytes 1540
  0.7 27.2 %copy-start.1 = (s32[2,8,4,2]{1,3,2,0:T(2,128)S(1)}, s32[2,8,4,2]{1,3,2,0:T(2,128)}, u32[]{:S(2)}) copy-start(s32[2,8,4,2]{1,3,2,0:T(2,128)} %param.7) | copy-start | bytes 1540
  4.6 5.2 %collective-permute-start = (f32[2,24,256]{2,1,0:T(8,128)S(1)}, f32[2,24,256]{2,1,0:T(8,128)S(1)}, u32[]{:S(2)}, u32[]{:S(2)}) collective-permute-start(f32[2,24,256]{2,1,0:T(8,128)S(1)} %get-tuple-element.16), channel_id=1, source_target_pairs={{0,4},{4,8},{8,12},{12,16},{16,20},{20,24},{24,28},{28,0},{1,5},{5... | collective-permute-start | bytes 147464 | tf_op jit(solution)/shard_map/ppermute | solution.py:44
  5.1 4.7 %collective-permute-start.1 = (f32[2,24,256]{2,1,0:T(8,128)S(1)}, f32[2,24,256]{2,1,0:T(8,128)S(1)}, u32[]{:S(2)}, u32[]{:S(2)}) collective-permute-start(f32[2,24,256]{2,1,0:T(8,128)S(1)} %get-tuple-element.17), channel_id=1, source_target_pairs={{0,28},{4,0},{8,4},{12,8},{16,12},{20,16},{24,20},{28,24},{1,29},{... | collective-permute-start | bytes 147464 | tf_op jit(solution)/shard_map/ppermute | solution.py:44
  9.8 7.6 %collective-permute-start.2 = (f32[3,24,256]{2,1,0:T(8,128)S(1)}, f32[3,24,256]{2,1,0:T(8,128)S(1)}, u32[]{:S(2)}, u32[]{:S(2)}) collective-permute-start(f32[3,24,256]{2,1,0:T(8,128)S(1)} %get-tuple-element.19), channel_id=1, source_target_pairs={{0,3},{1,2},{2,1},{3,0},{4,7},{5,6},{6,5},{7,4},{8,11},{9,10},{10,... | collective-permute-start | bytes 221192 | tf_op jit(solution)/shard_map/ppermute | solution.py:53
  14.2 6.0 %collective-permute-start.3 = (f32[3,24,256]{2,1,0:T(8,128)S(1)}, f32[3,24,256]{2,1,0:T(8,128)S(1)}, u32[]{:S(2)}, u32[]{:S(2)}) collective-permute-start(f32[3,24,256]{2,1,0:T(8,128)S(1)} %get-tuple-element.20), channel_id=1, source_target_pairs={{0,1},{1,0},{2,3},{3,2},{4,5},{5,4},{6,7},{7,6},{8,9},{9,8},{10,11... | collective-permute-start | bytes 221192 | tf_op jit(solution)/shard_map/ppermute | solution.py:53
  14.2 7.1 %collective-permute-start.4 = (f32[3,24,256]{2,1,0:T(8,128)S(1)}, f32[3,24,256]{2,1,0:T(8,128)S(1)}, u32[]{:S(2)}, u32[]{:S(2)}) collective-permute-start(f32[3,24,256]{2,1,0:T(8,128)S(1)} %get-tuple-element.21), channel_id=1, source_target_pairs={{0,2},{1,3},{2,0},{3,1},{4,6},{5,7},{6,4},{7,5},{8,10},{9,11},{10,... | collective-permute-start | bytes 221192 | tf_op jit(solution)/shard_map/ppermute | solution.py:53
  21.4 5.7 %collective-permute-start.7 = (bf16[48,256]{1,0:T(8,128)(2,1)S(1)}, bf16[48,256]{1,0:T(8,128)(2,1)S(1)}, u32[]{:S(2)}, u32[]{:S(2)}) collective-permute-start(bf16[48,256]{1,0:T(8,128)(2,1)S(1)} %get-tuple-element.22.rest_0_), channel_id=1, source_target_pairs={{0,3},{1,2},{2,1},{3,0},{4,7},{5,6},{6,5},{7,4},{8,11},{9,10},{10,... | collective-permute-start | bytes 73736 | tf_op jit(solution)/shard_map/ppermute | solution.py:53
  22.9 4.7 %collective-permute-start.6 = (bf16[48,256]{1,0:T(8,128)(2,1)S(1)}, bf16[48,256]{1,0:T(8,128)(2,1)S(1)}, u32[]{:S(2)}, u32[]{:S(2)}) collective-permute-start(bf16[48,256]{1,0:T(8,128)(2,1)S(1)} %get-tuple-element.22.rest_0_), channel_id=1, source_target_pairs={{0,2},{1,3},{2,0},{3,1},{4,6},{5,7},{6,4},{7,5},{8,10},{9,11},{10,... | collective-permute-start | bytes 73736 | tf_op jit(solution)/shard_map/ppermute | solution.py:53
  23.4 4.5 %collective-permute-start.5 = (bf16[48,256]{1,0:T(8,128)(2,1)S(1)}, bf16[48,256]{1,0:T(8,128)(2,1)S(1)}, u32[]{:S(2)}, u32[]{:S(2)}) collective-permute-start(bf16[48,256]{1,0:T(8,128)(2,1)S(1)} %get-tuple-element.22.rest_0_), channel_id=1, source_target_pairs={{0,1},{1,0},{2,3},{3,2},{4,5},{5,4},{6,7},{7,6},{8,9},{9,8},{10,11... | collective-permute-start | bytes 73736 | tf_op jit(solution)/shard_map/ppermute | solution.py:53
  31.0 7.7 %collective-permute-start.10 = (f32[9,8,128]{2,1,0:T(8,128)S(1)}, f32[9,8,128]{2,1,0:T(8,128)S(1)}, u32[]{:S(2)}, u32[]{:S(2)}) collective-permute-start(f32[9,8,128]{2,1,0:T(8,128)S(1)} %back_project.1), channel_id=1, source_target_pairs={{0,3},{1,2},{2,1},{3,0},{4,7},{5,6},{6,5},{7,4},{8,11},{9,10},{10,... | collective-permute-start | bytes 110600 | tf_op jit(solution)/shard_map/ppermute | solution.py:53
  33.5 5.2 %collective-permute-start.9 = (f32[9,8,128]{2,1,0:T(8,128)S(1)}, f32[9,8,128]{2,1,0:T(8,128)S(1)}, u32[]{:S(2)}, u32[]{:S(2)}) collective-permute-start(f32[9,8,128]{2,1,0:T(8,128)S(1)} %back_project.1), channel_id=1, source_target_pairs={{0,2},{1,3},{2,0},{3,1},{4,6},{5,7},{6,4},{7,5},{8,10},{9,11},{10,... | collective-permute-start | bytes 110600 | tf_op jit(solution)/shard_map/ppermute | solution.py:53
  34.4 4.4 %collective-permute-start.8 = (f32[9,8,128]{2,1,0:T(8,128)S(1)}, f32[9,8,128]{2,1,0:T(8,128)S(1)}, u32[]{:S(2)}, u32[]{:S(2)}) collective-permute-start(f32[9,8,128]{2,1,0:T(8,128)S(1)} %back_project.1), channel_id=1, source_target_pairs={{0,1},{1,0},{2,3},{3,2},{4,5},{5,4},{6,7},{7,6},{8,9},{9,8},{10,11... | collective-permute-start | bytes 110600 | tf_op jit(solution)/shard_map/ppermute | solution.py:53
  38.8 6.1 %collective-permute-start.13 = (f32[33,8,128]{2,1,0:T(8,128)S(1)}, f32[33,8,128]{2,1,0:T(8,128)S(1)}, u32[]{:S(2)}, u32[]{:S(2)}) collective-permute-start(f32[33,8,128]{2,1,0:T(8,128)S(1)} %constant_dynamic-update-slice_fusion), channel_id=1, source_target_pairs={{0,24},{4,28},{8,16},{12,20},{16,8},{20,12},{24,0},{28,4},{1,25},{... | collective-permute-start | bytes 405512 | tf_op jit(solution)/shard_map/ppermute | solution.py:53
  40.1 6.1 %collective-permute-start.12 = (f32[33,8,128]{2,1,0:T(8,128)S(1)}, f32[33,8,128]{2,1,0:T(8,128)S(1)}, u32[]{:S(2)}, u32[]{:S(2)}) collective-permute-start(f32[33,8,128]{2,1,0:T(8,128)S(1)} %constant_dynamic-update-slice_fusion), channel_id=1, source_target_pairs={{0,16},{4,20},{8,24},{12,28},{16,0},{20,4},{24,8},{28,12},{1,17},{... | collective-permute-start | bytes 405512 | tf_op jit(solution)/shard_map/ppermute | solution.py:53
  40.9 5.4 %collective-permute-start.11 = (f32[33,8,128]{2,1,0:T(8,128)S(1)}, f32[33,8,128]{2,1,0:T(8,128)S(1)}, u32[]{:S(2)}, u32[]{:S(2)}) collective-permute-start(f32[33,8,128]{2,1,0:T(8,128)S(1)} %constant_dynamic-update-slice_fusion), channel_id=1, source_target_pairs={{0,8},{4,12},{8,0},{12,4},{16,24},{20,28},{24,16},{28,20},{1,9},{5... | collective-permute-start | bytes 405512 | tf_op jit(solution)/shard_map/ppermute | solution.py:53
  46.4 2.0 %collective-permute-start.14 = (f32[4,33,8,128]{3,2,1,0:T(8,128)S(1)}, f32[4,33,8,128]{3,2,1,0:T(8,128)S(1)}, u32[]{:S(2)}, u32[]{:S(2)}) collective-permute-start(f32[4,33,8,128]{3,2,1,0:T(8,128)S(1)} %pad_maximum_fusion.near_ref), channel_id=1, source_target_pairs={{0,4},{4,0},{8,12},{12,8},{16,20},{20,16},{24,28},{28,24},{1,5},{5... | collective-permute-start | bytes 1622024 | tf_op jit(solution)/shard_map/ppermute | solution.py:53

commit v5 on v4

--- a/solution.py
+++ b/solution.py
@@ -207,7 +207,8 @@
     )(packed, below, above)
 
 
-def correct_kernel(plan, seen_ref, *rest):
+def correct_kernel(plan, seen_ref, ready_ref, *rest):
+    del ready_ref
     parts, (exact_ref, rounded_ref) = rest[:-2], rest[-2:]
     band = lax.axis_index("xy")
     tdet, unit = plan.tdet, plan.unit
@@ -235,7 +236,7 @@
     rounded_ref[...] = jnp.concatenate(rounded, axis=0).astype(jnp.bfloat16)
 
 
-def correct(plan, seen, parts):
+def correct(plan, seen, parts, ready):
     views, chunk, unit, tdet = seen.shape
     return pl.pallas_call(
         functools.partial(correct_kernel, plan),
@@ -243,11 +244,35 @@
             jax.ShapeDtypeStruct((views, plan.own_units, unit, tdet), jnp.float32),
             jax.ShapeDtypeStruct((views * chunk * unit, tdet), jnp.bfloat16),
         ),
-        in_specs=in_vmem(1 + len(parts)),
+        in_specs=in_vmem(1) + [pl.BlockSpec(memory_space=pl.ANY)] + in_vmem(len(parts)),
         out_specs=tuple(in_vmem(2)),
         compiler_params=pltpu.CompilerParams(vmem_limit_bytes=VMEM_BYTES // 4),
         name="correct",
-    )(seen, *parts)
+    )(seen, ready, *parts)
+
+
+def turn_kernel(shape, foot, turned):
+    for p in range(shape[0]):
+        for r in range(shape[1]):
+            for t in range(shape[2]):
+                for v in range(shape[3]):
+                    turned[p, r, t, v] = foot[p, r, t, v].T
+
+
+def turn(footprint):
+    shape = footprint.shape
+    footprint = pltpu.with_memory_space_constraint(footprint, pltpu.VMEM)
+    return pl.pallas_call(
+        functools.partial(turn_kernel, shape),
+        out_shape=pltpu.VMEM(shape[:4] + (shape[5], shape[4]), jnp.bfloat16),
+        in_specs=in_vmem(1),
+        out_specs=pl.BlockSpec(memory_space=pltpu.VMEM),
+        compiler_params=pltpu.CompilerParams(vmem_limit_bytes=VMEM_BYTES // 4),
+        cost_estimate=pl.CostEstimate(
+            flops=0, bytes_accessed=4 * footprint.size, transcendentals=0
+        ),
+        name="turn",
+    )(footprint)
 
 
 def back_kernel(plan, shape, vol_any, foot, block_any, cells_any, *rest):
@@ -257,7 +282,7 @@
     first = copy_all([(block_any, block_ref), (cells_any, cells_ref), (vol_any, vol_ref)], small)
     for copy in first:
         copy.start()
-    for flip, part in enumerate(parts):
+    for flip, part in zip([0] + list(range(plan.bands - 1, 0, -1)), parts):
         source = band ^ flip
         piece = part[...].astype(jnp.float32).reshape(views, plan.chunk, plan.unit, tdet)
         halo = jnp.where(
@@ -284,12 +309,7 @@
                     picked = jnp.broadcast_to(corr[v, unit, pl.ds(column, 1), :], (8, tdet))
                     left = jnp.where(top, picked, 1.0)
                     left = jnp.where(lane < cells_ref[p, t, v, r], left, 0.0).astype(jnp.bfloat16)
-                    both += lax.dot_general(
-                        left,
-                        foot[p, r, t, v],
-                        (((1,), (1,)), ((), ())),
-                        preferred_element_type=jnp.float32,
-                    )
+                    both += jnp.dot(left, foot[p, r, t, v], preferred_element_type=jnp.float32)
                 sums[0, r : r + 1] = both[0:1]
                 sums[1, r : r + 1] = both[1:2]
             volume = vol_ref[p, :, t * tvox : (t + 1) * tvox]
@@ -301,8 +321,8 @@
 
 
 def back_project(plan, volume, footprint, tile_block, tile_cells, parts):
-    shape = footprint.shape
-    planes, rows, tiles, views, tvox, tdet = shape
+    planes, rows, tiles, views, tdet, tvox = footprint.shape
+    shape = planes, rows, tiles, views, tvox, tdet
     spaces = [pl.ANY, pltpu.VMEM, pl.ANY, pl.ANY] + [pltpu.VMEM] * len(parts)
     footprint = pltpu.with_memory_space_constraint(footprint, pltpu.VMEM)
     return pl.pallas_call(
@@ -372,9 +392,9 @@
 
     gap = jnp.zeros((rows, tvox), jnp.float32)
     for half, ref in enumerate((near_ref, far_ref)):
-        for i, flip in enumerate(range(0, slabs, 2)):
+        for i, flip in enumerate([0] + list(range(slabs - 2, 0, -2))):
             for j in range(bands):
-                plane, at = (slab ^ (flip + half)) * planes, (band ^ j) * per
+                plane, at = (slab ^ (flip + half)) * planes, (band ^ ((bands - j) % bands)) * per
                 for p in range(planes):
                     for t in range(tiles):
                         tile = ref[i, (j * planes + p) * tiles + t]
@@ -473,13 +493,14 @@
     parts = [
         swap_all(chunks[flip], "xy", flip) if flip else chunks[0] for flip in reduce_order(bands)
     ]
-    exact, rounded = correct(plan, seen, parts)
-    parts = [rounded] + [swap_all(rounded, "xy", flip) for flip in range(1, bands)]
-    tiled = back_project(plan, volume, footprint, block, cells, parts)
-
-    line = [tiled] + [swap_all(tiled, "xy", flip) for flip in range(1, bands)]
+    turned = turn(footprint)
+    exact, rounded = correct(plan, seen, parts, turned)
+    parts = [rounded] + [swap_all(rounded, "xy", flip) for flip in range(bands - 1, 0, -1)]
+    tiled = back_project(plan, volume, turned, block, cells, parts)
+
+    line = [tiled] + [swap_all(tiled, "xy", flip) for flip in range(bands - 1, 0, -1)]
     line = jnp.concatenate([each[:-1] for each in line] + [sum(each[-1:] for each in line)])
-    near = jnp.stack([line] + [swap_all(line, "slab", flip) for flip in range(2, slabs, 2)])
+    near = jnp.stack([line] + [swap_all(line, "slab", flip) for flip in range(slabs - 2, 0, -2)])
     far = swap_all(near, "slab", 1)
     return smooth(volume, near, far, exact, slabs, bands, footprint.shape[2])
 

time: 51.8 us -> 50.7 us (0.979)
  waiting for transfers between devices: 19.4 us -> 17.1 us
  Pallas kernels: 10.4 us -> 11.6 us
    ppermute x13, waiting for transfers between devices: 17.6 us -> 15.4 us  [swap_all(): return lax.ppermute(cells, axis, [(i, i ^ flip) for i in range(count)])]
    pallas_call x0 -> x1, Pallas kernels: none -> 2.21 us  [turn(): pl.pallas_call(functools.partial(turn_kernel, shape), out_shape=pltpu.VME...]
    pallas_call x1, Pallas kernels: 3.14 us -> 2.15 us  [back_project(): pl.pallas_call(functools.partial(back_kernel, plan, shape), out_shape=jax...]
  transfers between devices with their start and end apart: 15 -> 15, of which waited for: 12 -> 14; matrix products, arithmetic and copies ran while one was open for 0% -> 0% of each run, Pallas kernels for 0% -> 4%
where the time goes in v5:
time: 50.7 us; the launch traced here: 50.5 us
  starting transfers between devices  21 us (41%)
  waiting for transfers between devices  17.1 us (34%)
  Pallas kernels  11.6 us (23%)
  between operations  0.71 us (1%)
    ppermute x13, starting transfers between devices, swap_all(): return lax.ppermute(cells, axis, [(i, i ^ flip) for i in range(count)])  17.6 us
    ppermute x13, waiting for transfers between devices, swap_all(): return lax.ppermute(cells, axis, [(i, i ^ flip) for i in range(count)])  15.4 us
    pallas_call x1, Pallas kernels, project(): pl.pallas_call(functools.partial(project_kernel, plan, shape), out_shape=...  3.9 us
    ppermute x2, starting transfers between devices, shift_all(): lax.ppermute(cells, axis, [(i, (i + step) % count) for i in range(count)])  3.45 us
    pallas_call x1, Pallas kernels, smooth(): pl.pallas_call(functools.partial(smooth_kernel, sizes), out_shape=(jax.Sh...  3.24 us
    pallas_call x1, Pallas kernels, turn(): pl.pallas_call(functools.partial(turn_kernel, shape), out_shape=pltpu.VME...  2.21 us
    pallas_call x1, Pallas kernels, back_project(): pl.pallas_call(functools.partial(back_kernel, plan, shape), out_shape=jax...  2.15 us
    ppermute x2, waiting for transfers between devices, shift_all(): lax.ppermute(cells, axis, [(i, (i + step) % count) for i in range(count)])  1.75 us
  transfers between devices with their start and end apart: 15, of which 14 were waited for; matrix products, arithmetic and copies ran while one was open for 0% of the time, Pallas kernels for 4%

profile of v5, /device:TPU:0, one launch (start us, length us, event | category | flops | bytes accessed | tf_op | source)
XLA Modules:
  0.0 50.5 jit_solution(2489729434796797802)
XLA Ops:
  0.6 3.9 %project.1 = (f32[10,24,256]{2,1,0:T(8,128)S(1)}, f32[2,24,256]{2,1,0:T(8,128)S(1)}, f32[2,24,256]{2,1,0:T(8,128)S(1)}, f32[2,3,8,256]{3,2,1,0:T(8,128)S(1)}, bf16[2,8,4,2,128,256]{5,4,3,2,1,0:T(8,128)(2,1)S(1)}) custom-call(f32[2,8,512]{2,1,0:T(8,128)} %vol_any.1, bf16[2,8,4,2,128,256]{5,4,3,2,1,0:T(8,128)(2,1)} %foot_hbm.1, s32[2,4,2,8]{3,2,1,0:T(2,128)} %bitcast.6, ...), custom_call_target="tpu_custom_call" | custom-call | tf_op jit(solution)/shard_map/project/pallas_call | solution.py:156
  4.5 0.5 collective-permute-start
  5.0 2.9 %collective-permute-start.1 = (f32[2,24,256]{2,1,0:T(8,128)S(1)}, f32[2,24,256]{2,1,0:T(8,128)S(1)}, u32[]{:S(2)}, u32[]{:S(2)}) collective-permute-start(f32[2,24,256]{2,1,0:T(8,128)S(1)} %get-tuple-element.17), channel_id=1, source_target_pairs={{0,28},{4,0},{8,4},{12,8},{16,12},{20,16},{24,20},{28,24},{1,29},{... | collective-permute-start | bytes 147464 | tf_op jit(solution)/shard_map/ppermute | solution.py:44
  8.0 1.7 %collective-permute-done.below_ref = f32[2,24,256]{2,1,0:T(8,128)S(1)} collective-permute-done((f32[2,24,256]{2,1,0:T(8,128)S(1)}, f32[2,24,256]{2,1,0:T(8,128)S(1)}, u32[]{:S(2)}, u32[]{:S(2)}) %collective-permute-start) | collective-permute-done | bytes 49184 | tf_op jit(solution)/shard_map/ppermute | solution.py:44
  9.8 4.4 %collective-permute-start.2 = (f32[3,24,256]{2,1,0:T(8,128)S(1)}, f32[3,24,256]{2,1,0:T(8,128)S(1)}, u32[]{:S(2)}, u32[]{:S(2)}) collective-permute-start(f32[3,24,256]{2,1,0:T(8,128)S(1)} %get-tuple-element.19), channel_id=1, source_target_pairs={{0,3},{1,2},{2,1},{3,0},{4,7},{5,6},{6,5},{7,4},{8,11},{9,10},{10,... | collective-permute-start | bytes 221192 | tf_op jit(solution)/shard_map/ppermute | solution.py:53
  14.2 0.6 %collective-permute-start.4 = (f32[3,24,256]{2,1,0:T(8,128)S(1)}, f32[3,24,256]{2,1,0:T(8,128)S(1)}, u32[]{:S(2)}, u32[]{:S(2)}) collective-permute-start(f32[3,24,256]{2,1,0:T(8,128)S(1)} %get-tuple-element.21), channel_id=1, source_target_pairs={{0,2},{1,3},{2,0},{3,1},{4,6},{5,7},{6,4},{7,5},{8,10},{9,11},{10,... | collective-permute-start | bytes 221192 | tf_op jit(solution)/shard_map/ppermute | solution.py:53
  14.8 2.2 %turn.1.ready_ref.foot = bf16[2,8,4,2,256,128]{5,4,3,2,1,0:T(8,128)(2,1)S(1)} custom-call(bf16[2,8,4,2,128,256]{5,4,3,2,1,0:T(8,128)(2,1)S(1)} %get-tuple-element.13.foot), custom_call_target="tpu_custom_call" | custom-call | bytes 16777216 | tf_op jit(solution)/shard_map/turn/pallas_call | solution.py:265
  17.1 0.3 collective-permute-done.2.rest_1_
  17.4 2.8 %collective-permute-done.3.rest_2_ = f32[3,24,256]{2,1,0:T(8,128)S(1)} collective-permute-done((f32[3,24,256]{2,1,0:T(8,128)S(1)}, f32[3,24,256]{2,1,0:T(8,128)S(1)}, u32[]{:S(2)}, u32[]{:S(2)}) %collective-permute-start.3) | collective-permute-done | bytes 73760 | tf_op jit(solution)/shard_map/ppermute | solution.py:53
  20.2 1.1 %collective-permute-done.4.rest_3_ = f32[3,24,256]{2,1,0:T(8,128)S(1)} collective-permute-done((f32[3,24,256]{2,1,0:T(8,128)S(1)}, f32[3,24,256]{2,1,0:T(8,128)S(1)}, u32[]{:S(2)}, u32[]{:S(2)}) %collective-permute-start.4) | collective-permute-done | bytes 73760 | tf_op jit(solution)/shard_map/ppermute | solution.py:53
  21.4 1.4 %collective-permute-start.5 = (bf16[48,256]{1,0:T(8,128)(2,1)S(1)}, bf16[48,256]{1,0:T(8,128)(2,1)S(1)}, u32[]{:S(2)}, u32[]{:S(2)}) collective-permute-start(bf16[48,256]{1,0:T(8,128)(2,1)S(1)} %get-tuple-element.22.rest_0_), channel_id=1, source_target_pairs={{0,3},{1,2},{2,1},{3,0},{4,7},{5,6},{6,5},{7,4},{8,11},{9,10},{10,... | collective-permute-start | bytes 73736 | tf_op jit(solution)/shard_map/ppermute | solution.py:53
  22.8 0.5 collective-permute-start.6
  23.3 2.5 %collective-permute-start.7 = (bf16[48,256]{1,0:T(8,128)(2,1)S(1)}, bf16[48,256]{1,0:T(8,128)(2,1)S(1)}, u32[]{:S(2)}, u32[]{:S(2)}) collective-permute-start(bf16[48,256]{1,0:T(8,128)(2,1)S(1)} %get-tuple-element.22.rest_0_), channel_id=1, source_target_pairs={{0,1},{1,0},{2,3},{3,2},{4,5},{5,4},{6,7},{7,6},{8,9},{9,8},{10,11... | collective-permute-start | bytes 73736 | tf_op jit(solution)/shard_map/ppermute | solution.py:53
  25.8 1.2 %collective-permute-done.5.rest_1_ = bf16[48,256]{1,0:T(8,128)(2,1)S(1)} collective-permute-done((bf16[48,256]{1,0:T(8,128)(2,1)S(1)}, bf16[48,256]{1,0:T(8,128)(2,1)S(1)}, u32[]{:S(2)}, u32[]{:S(2)}) %collective-permute-start.5) | collective-permute-done | bytes 24608 | tf_op jit(solution)/shard_map/ppermute | solution.py:53
  27.1 0.5 collective-permute-done.6.rest_2_
  27.6 0.2 collective-permute-done.7.rest_3_
  27.8 2.1 %back_project.1 = f32[9,8,128]{2,1,0:T(8,128)S(1)} custom-call(f32[2,8,512]{2,1,0:T(8,128)S(1)} %copy-done, bf16[2,8,4,2,256,128]{5,4,3,2,1,0:T(8,128)(2,1)S(1)} %turn.1.ready_ref.foot, s32[2,4,2,8]{3,2,1,0:T(2,128)S(1)} %bitcast.7, s32[2,4,2,8]{3,2,1,0:T(2,128)S(1)} %bitcast.9, bf16[48,256]{1,0:T(8,128)(2,1)S(1)} %get-tuple-element.22.rest_0_, ...), custom_call_target="tpu_custom_call" | custom-call | tf_op jit(solution)/shard_map/back_project/pallas_call | solution.py:328
  30.0 2.5 %collective-permute-start.8 = (f32[9,8,128]{2,1,0:T(8,128)S(1)}, f32[9,8,128]{2,1,0:T(8,128)S(1)}, u32[]{:S(2)}, u32[]{:S(2)}) collective-permute-start(f32[9,8,128]{2,1,0:T(8,128)S(1)} %back_project.1), channel_id=1, source_target_pairs={{0,3},{1,2},{2,1},{3,0},{4,7},{5,6},{6,5},{7,4},{8,11},{9,10},{10,... | collective-permute-start | bytes 110600 | tf_op jit(solution)/shard_map/ppermute | solution.py:53
  32.5 0.9 %collective-permute-start.9 = (f32[9,8,128]{2,1,0:T(8,128)S(1)}, f32[9,8,128]{2,1,0:T(8,128)S(1)}, u32[]{:S(2)}, u32[]{:S(2)}) collective-permute-start(f32[9,8,128]{2,1,0:T(8,128)S(1)} %back_project.1), channel_id=1, source_target_pairs={{0,2},{1,3},{2,0},{3,1},{4,6},{5,7},{6,4},{7,5},{8,10},{9,11},{10,... | collective-permute-start | bytes 110600 | tf_op jit(solution)/shard_map/ppermute | solution.py:53
  33.3 1.1 %collective-permute-start.10 = (f32[9,8,128]{2,1,0:T(8,128)S(1)}, f32[9,8,128]{2,1,0:T(8,128)S(1)}, u32[]{:S(2)}, u32[]{:S(2)}) collective-permute-start(f32[9,8,128]{2,1,0:T(8,128)S(1)} %back_project.1), channel_id=1, source_target_pairs={{0,1},{1,0},{2,3},{3,2},{4,5},{5,4},{6,7},{7,6},{8,9},{9,8},{10,11... | collective-permute-start | bytes 110600 | tf_op jit(solution)/shard_map/ppermute | solution.py:53
  34.4 1.7 %collective-permute-done.8 = f32[9,8,128]{2,1,0:T(8,128)S(1)} collective-permute-done((f32[9,8,128]{2,1,0:T(8,128)S(1)}, f32[9,8,128]{2,1,0:T(8,128)S(1)}, u32[]{:S(2)}, u32[]{:S(2)}) %collective-permute-start.8) | collective-permute-done | bytes 36896 | tf_op jit(solution)/shard_map/ppermute | solution.py:53
  36.1 1.4 %collective-permute-done.9 = f32[9,8,128]{2,1,0:T(8,128)S(1)} collective-permute-done((f32[9,8,128]{2,1,0:T(8,128)S(1)}, f32[9,8,128]{2,1,0:T(8,128)S(1)}, u32[]{:S(2)}, u32[]{:S(2)}) %collective-permute-start.9) | collective-permute-done | bytes 36896 | tf_op jit(solution)/shard_map/ppermute | solution.py:53
  37.5 0.2 collective-permute-done.10
  37.7 1.4 %collective-permute-start.11 = (f32[33,8,128]{2,1,0:T(8,128)S(1)}, f32[33,8,128]{2,1,0:T(8,128)S(1)}, u32[]{:S(2)}, u32[]{:S(2)}) collective-permute-start(f32[33,8,128]{2,1,0:T(8,128)S(1)} %constant_dynamic-update-slice_fusion), channel_id=1, source_target_pairs={{0,24},{4,28},{8,16},{12,20},{16,8},{20,12},{24,0},{28,4},{1,25},{... | collective-permute-start | bytes 405512 | tf_op jit(solution)/shard_map/ppermute | solution.py:53
  39.1 0.8 %collective-permute-start.12 = (f32[33,8,128]{2,1,0:T(8,128)S(1)}, f32[33,8,128]{2,1,0:T(8,128)S(1)}, u32[]{:S(2)}, u32[]{:S(2)}) collective-permute-start(f32[33,8,128]{2,1,0:T(8,128)S(1)} %constant_dynamic-update-slice_fusion), channel_id=1, source_target_pairs={{0,16},{4,20},{8,24},{12,28},{16,0},{20,4},{24,8},{28,12},{1,17},{... | collective-permute-start | bytes 405512 | tf_op jit(solution)/shard_map/ppermute | solution.py:53
  39.9 1.4 %collective-permute-start.13 = (f32[33,8,128]{2,1,0:T(8,128)S(1)}, f32[33,8,128]{2,1,0:T(8,128)S(1)}, u32[]{:S(2)}, u32[]{:S(2)}) collective-permute-start(f32[33,8,128]{2,1,0:T(8,128)S(1)} %constant_dynamic-update-slice_fusion), channel_id=1, source_target_pairs={{0,8},{4,12},{8,0},{12,4},{16,24},{20,28},{24,16},{28,20},{1,9},{5... | collective-permute-start | bytes 405512 | tf_op jit(solution)/shard_map/ppermute | solution.py:53
  41.3 2.5 %collective-permute-done.11 = f32[33,8,128]{2,1,0:T(8,128)S(1)} collective-permute-done((f32[33,8,128]{2,1,0:T(8,128)S(1)}, f32[33,8,128]{2,1,0:T(8,128)S(1)}, u32[]{:S(2)}, u32[]{:S(2)}) %collective-permute-start.11) | collective-permute-done | bytes 135200 | tf_op jit(solution)/shard_map/ppermute | solution.py:53
  43.8 1.3 %collective-permute-done.12 = f32[33,8,128]{2,1,0:T(8,128)S(1)} collective-permute-done((f32[33,8,128]{2,1,0:T(8,128)S(1)}, f32[33,8,128]{2,1,0:T(8,128)S(1)}, u32[]{:S(2)}, u32[]{:S(2)}) %collective-permute-start.12) | collective-permute-done | bytes 135200 | tf_op jit(solution)/shard_map/ppermute | solution.py:53
  45.1 0.1 collective-permute-done.13
  45.3 0.1 collective-permute-start.14
  45.4 1.9 %collective-permute-done.14.far_ref = f32[4,33,8,128]{3,2,1,0:T(8,128)S(1)} collective-permute-done((f32[4,33,8,128]{3,2,1,0:T(8,128)S(1)}, f32[4,33,8,128]{3,2,1,0:T(8,128)S(1)}, u32[]{:S(2)}, u32[]{:S(2)}) %collective-permute-start.14) | collective-permute-done | bytes 540704 | tf_op jit(solution)/shard_map/ppermute | solution.py:53
  47.3 3.2 %smooth.1 = (f32[2,8,512]{2,1,0:T(8,128)}, f32[2,4096]{1,0:T(2,128)}) custom-call(f32[4,33,8,128]{3,2,1,0:T(8,128)S(1)} %pad_maximum_fusion.near_ref, f32[4,33,8,128]{3,2,1,0:T(8,128)S(1)} %collective-permute-done.14.far_ref, f32[2,2,8,256]{3,2,1,0:T(8,128)S(1)} %get-tuple-element.23.exact_ref), custom_call_target="tpu_custom_call" | custom-call | tf_op jit(solution)/shard_map/smooth/pallas_call | solution.py:464
  (16 shorter events, 0.2 us)
Async XLA Ops:
  4.5 5.2 %collective-permute-start = (f32[2,24,256]{2,1,0:T(8,128)S(1)}, f32[2,24,256]{2,1,0:T(8,128)S(1)}, u32[]{:S(2)}, u32[]{:S(2)}) collective-permute-start(f32[2,24,256]{2,1,0:T(8,128)S(1)} %get-tuple-element.16), channel_id=1, source_target_pairs={{0,4},{4,8},{8,12},{12,16},{16,20},{20,24},{24,28},{28,0},{1,5},{5... | collective-permute-start | bytes 147464 | tf_op jit(solution)/shard_map/ppermute | solution.py:44
  5.0 4.7 %collective-permute-start.1 = (f32[2,24,256]{2,1,0:T(8,128)S(1)}, f32[2,24,256]{2,1,0:T(8,128)S(1)}, u32[]{:S(2)}, u32[]{:S(2)}) collective-permute-start(f32[2,24,256]{2,1,0:T(8,128)S(1)} %get-tuple-element.17), channel_id=1, source_target_pairs={{0,28},{4,0},{8,4},{12,8},{16,12},{20,16},{24,20},{28,24},{1,29},{... | collective-permute-start | bytes 147464 | tf_op jit(solution)/shard_map/ppermute | solution.py:44
  9.8 7.6 %collective-permute-start.2 = (f32[3,24,256]{2,1,0:T(8,128)S(1)}, f32[3,24,256]{2,1,0:T(8,128)S(1)}, u32[]{:S(2)}, u32[]{:S(2)}) collective-permute-start(f32[3,24,256]{2,1,0:T(8,128)S(1)} %get-tuple-element.19), channel_id=1, source_target_pairs={{0,3},{1,2},{2,1},{3,0},{4,7},{5,6},{6,5},{7,4},{8,11},{9,10},{10,... | collective-permute-start | bytes 221192 | tf_op jit(solution)/shard_map/ppermute | solution.py:53
  14.2 6.0 %collective-permute-start.3 = (f32[3,24,256]{2,1,0:T(8,128)S(1)}, f32[3,24,256]{2,1,0:T(8,128)S(1)}, u32[]{:S(2)}, u32[]{:S(2)}) collective-permute-start(f32[3,24,256]{2,1,0:T(8,128)S(1)} %get-tuple-element.20), channel_id=1, source_target_pairs={{0,1},{1,0},{2,3},{3,2},{4,5},{5,4},{6,7},{7,6},{8,9},{9,8},{10,11... | collective-permute-start | bytes 221192 | tf_op jit(solution)/shard_map/ppermute | solution.py:53
  14.2 7.1 %collective-permute-start.4 = (f32[3,24,256]{2,1,0:T(8,128)S(1)}, f32[3,24,256]{2,1,0:T(8,128)S(1)}, u32[]{:S(2)}, u32[]{:S(2)}) collective-permute-start(f32[3,24,256]{2,1,0:T(8,128)S(1)} %get-tuple-element.21), channel_id=1, source_target_pairs={{0,2},{1,3},{2,0},{3,1},{4,6},{5,7},{6,4},{7,5},{8,10},{9,11},{10,... | collective-permute-start | bytes 221192 | tf_op jit(solution)/shard_map/ppermute | solution.py:53
  17.0 10.8 %copy-start = (f32[2,8,512]{2,1,0:T(8,128)S(1)}, f32[2,8,512]{2,1,0:T(8,128)}, u32[]{:S(2)}) copy-start(f32[2,8,512]{2,1,0:T(8,128)} %vol_any.1) | copy-start | bytes 98308
  17.1 10.8 %copy-start.1 = (s32[2,8,4,2]{1,3,2,0:T(2,128)S(1)}, s32[2,8,4,2]{1,3,2,0:T(2,128)}, u32[]{:S(2)}) copy-start(s32[2,8,4,2]{1,3,2,0:T(2,128)} %param.7) | copy-start | bytes 1540
  17.1 10.8 %copy-start.2 = (s32[2,8,4,2]{1,3,2,0:T(2,128)S(1)}, s32[2,8,4,2]{1,3,2,0:T(2,128)}, u32[]{:S(2)}) copy-start(s32[2,8,4,2]{1,3,2,0:T(2,128)} %param.8) | copy-start | bytes 1540
  21.4 5.7 %collective-permute-start.5 = (bf16[48,256]{1,0:T(8,128)(2,1)S(1)}, bf16[48,256]{1,0:T(8,128)(2,1)S(1)}, u32[]{:S(2)}, u32[]{:S(2)}) collective-permute-start(bf16[48,256]{1,0:T(8,128)(2,1)S(1)} %get-tuple-element.22.rest_0_), channel_id=1, source_target_pairs={{0,3},{1,2},{2,1},{3,0},{4,7},{5,6},{6,5},{7,4},{8,11},{9,10},{10,... | collective-permute-start | bytes 73736 | tf_op jit(solution)/shard_map/ppermute | solution.py:53
  22.8 4.7 %collective-permute-start.6 = (bf16[48,256]{1,0:T(8,128)(2,1)S(1)}, bf16[48,256]{1,0:T(8,128)(2,1)S(1)}, u32[]{:S(2)}, u32[]{:S(2)}) collective-permute-start(bf16[48,256]{1,0:T(8,128)(2,1)S(1)} %get-tuple-element.22.rest_0_), channel_id=1, source_target_pairs={{0,2},{1,3},{2,0},{3,1},{4,6},{5,7},{6,4},{7,5},{8,10},{9,11},{10,... | collective-permute-start | bytes 73736 | tf_op jit(solution)/shard_map/ppermute | solution.py:53
  23.3 4.5 %collective-permute-start.7 = (bf16[48,256]{1,0:T(8,128)(2,1)S(1)}, bf16[48,256]{1,0:T(8,128)(2,1)S(1)}, u32[]{:S(2)}, u32[]{:S(2)}) collective-permute-start(bf16[48,256]{1,0:T(8,128)(2,1)S(1)} %get-tuple-element.22.rest_0_), channel_id=1, source_target_pairs={{0,1},{1,0},{2,3},{3,2},{4,5},{5,4},{6,7},{7,6},{8,9},{9,8},{10,11... | collective-permute-start | bytes 73736 | tf_op jit(solution)/shard_map/ppermute | solution.py:53
  30.0 6.1 %collective-permute-start.8 = (f32[9,8,128]{2,1,0:T(8,128)S(1)}, f32[9,8,128]{2,1,0:T(8,128)S(1)}, u32[]{:S(2)}, u32[]{:S(2)}) collective-permute-start(f32[9,8,128]{2,1,0:T(8,128)S(1)} %back_project.1), channel_id=1, source_target_pairs={{0,3},{1,2},{2,1},{3,0},{4,7},{5,6},{6,5},{7,4},{8,11},{9,10},{10,... | collective-permute-start | bytes 110600 | tf_op jit(solution)/shard_map/ppermute | solution.py:53
  32.5 5.0 %collective-permute-start.9 = (f32[9,8,128]{2,1,0:T(8,128)S(1)}, f32[9,8,128]{2,1,0:T(8,128)S(1)}, u32[]{:S(2)}, u32[]{:S(2)}) collective-permute-start(f32[9,8,128]{2,1,0:T(8,128)S(1)} %back_project.1), channel_id=1, source_target_pairs={{0,2},{1,3},{2,0},{3,1},{4,6},{5,7},{6,4},{7,5},{8,10},{9,11},{10,... | collective-permute-start | bytes 110600 | tf_op jit(solution)/shard_map/ppermute | solution.py:53
  33.3 4.4 %collective-permute-start.10 = (f32[9,8,128]{2,1,0:T(8,128)S(1)}, f32[9,8,128]{2,1,0:T(8,128)S(1)}, u32[]{:S(2)}, u32[]{:S(2)}) collective-permute-start(f32[9,8,128]{2,1,0:T(8,128)S(1)} %back_project.1), channel_id=1, source_target_pairs={{0,1},{1,0},{2,3},{3,2},{4,5},{5,4},{6,7},{7,6},{8,9},{9,8},{10,11... | collective-permute-start | bytes 110600 | tf_op jit(solution)/shard_map/ppermute | solution.py:53
  37.7 6.1 %collective-permute-start.11 = (f32[33,8,128]{2,1,0:T(8,128)S(1)}, f32[33,8,128]{2,1,0:T(8,128)S(1)}, u32[]{:S(2)}, u32[]{:S(2)}) collective-permute-start(f32[33,8,128]{2,1,0:T(8,128)S(1)} %constant_dynamic-update-slice_fusion), channel_id=1, source_target_pairs={{0,24},{4,28},{8,16},{12,20},{16,8},{20,12},{24,0},{28,4},{1,25},{... | collective-permute-start | bytes 405512 | tf_op jit(solution)/shard_map/ppermute | solution.py:53
  39.1 6.0 %collective-permute-start.12 = (f32[33,8,128]{2,1,0:T(8,128)S(1)}, f32[33,8,128]{2,1,0:T(8,128)S(1)}, u32[]{:S(2)}, u32[]{:S(2)}) collective-permute-start(f32[33,8,128]{2,1,0:T(8,128)S(1)} %constant_dynamic-update-slice_fusion), channel_id=1, source_target_pairs={{0,16},{4,20},{8,24},{12,28},{16,0},{20,4},{24,8},{28,12},{1,17},{... | collective-permute-start | bytes 405512 | tf_op jit(solution)/shard_map/ppermute | solution.py:53
  39.9 5.3 %collective-permute-start.13 = (f32[33,8,128]{2,1,0:T(8,128)S(1)}, f32[33,8,128]{2,1,0:T(8,128)S(1)}, u32[]{:S(2)}, u32[]{:S(2)}) collective-permute-start(f32[33,8,128]{2,1,0:T(8,128)S(1)} %constant_dynamic-update-slice_fusion), channel_id=1, source_target_pairs={{0,8},{4,12},{8,0},{12,4},{16,24},{20,28},{24,16},{28,20},{1,9},{5... | collective-permute-start | bytes 405512 | tf_op jit(solution)/shard_map/ppermute | solution.py:53
  45.3 2.0 %collective-permute-start.14 = (f32[4,33,8,128]{3,2,1,0:T(8,128)S(1)}, f32[4,33,8,128]{3,2,1,0:T(8,128)S(1)}, u32[]{:S(2)}, u32[]{:S(2)}) collective-permute-start(f32[4,33,8,128]{3,2,1,0:T(8,128)S(1)} %pad_maximum_fusion.near_ref), channel_id=1, source_target_pairs={{0,4},{4,0},{8,12},{12,8},{16,20},{20,16},{24,28},{28,24},{1,5},{5... | collective-permute-start | bytes 1622024 | tf_op jit(solution)/shard_map/ppermute | solution.py:53

commit v6 on v5

--- a/solution.py
+++ b/solution.py
@@ -282,7 +282,7 @@
     first = copy_all([(block_any, block_ref), (cells_any, cells_ref), (vol_any, vol_ref)], small)
     for copy in first:
         copy.start()
-    for flip, part in zip([0] + list(range(plan.bands - 1, 0, -1)), parts):
+    for flip, part in enumerate(parts):
         source = band ^ flip
         piece = part[...].astype(jnp.float32).reshape(views, plan.chunk, plan.unit, tdet)
         halo = jnp.where(
@@ -376,7 +376,8 @@
     return slope, unit_a
 
 
-def smooth_kernel(sizes, near_ref, far_ref, exact_ref, out_ref, seen_ref, field, slopes, units):
+def smooth_kernel(sizes, exact_ref, *rest):
+    chip_refs, (out_ref, seen_ref, field, slopes, units) = rest[:-5], rest[-5:]
     slabs, bands, planes, rows, tiles, tvox = sizes
     slab, band = lax.axis_index("slab"), lax.axis_index("xy")
     depth, per = slabs * planes, rows // 8
@@ -391,16 +392,17 @@
                 seen_ref[v : v + 1, at : at + tdet] = exact_ref[v, i, c : c + 1, :]
 
     gap = jnp.zeros((rows, tvox), jnp.float32)
-    for half, ref in enumerate((near_ref, far_ref)):
-        for i, flip in enumerate([0] + list(range(slabs - 2, 0, -2))):
-            for j in range(bands):
-                plane, at = (slab ^ (flip + half)) * planes, (band ^ ((bands - j) % bands)) * per
-                for p in range(planes):
-                    for t in range(tiles):
-                        tile = ref[i, (j * planes + p) * tiles + t]
-                        for n in range(per):
-                            field[plane + p, at + n, t] = tile[8 * n : 8 * n + 8]
-            gap += ref[i, bands * planes * tiles]
+    flips = list(range(0, slabs, 2))
+    flips += [flip ^ 1 for flip in flips[::-1]]
+    for flip, ref in zip(flips, chip_refs):
+        for j in range(bands):
+            plane, at = (slab ^ flip) * planes, (band ^ j) * per
+            for p in range(planes):
+                for t in range(tiles):
+                    tile = ref[(j * planes + p) * tiles + t]
+                    for n in range(per):
+                        field[plane + p, at + n, t] = tile[8 * n : 8 * n + 8]
+        gap += ref[bands * planes * tiles]
     nothing = jnp.zeros((8, tvox), jnp.float32)
     for i, t in blocks:
         field[depth, i, t] = nothing
@@ -456,7 +458,7 @@
                 )
 
 
-def smooth(volume, near, far, exact, slabs, bands, tiles):
+def smooth(volume, chips, exact, slabs, bands, tiles):
     planes, rows, cells = volume.shape
     views, own, unit, tdet = exact.shape
     sizes = slabs, bands, planes, rows, tiles, cells // tiles
@@ -467,7 +469,7 @@
             jax.ShapeDtypeStruct(volume.shape, jnp.float32),
             jax.ShapeDtypeStruct((views, own * unit * tdet), jnp.float32),
         ),
-        in_specs=in_vmem(3),
+        in_specs=in_vmem(1 + len(chips)),
         out_specs=tuple(in_vmem(2)),
         scratch_shapes=[
             pltpu.VMEM((slabs * planes + 1,) + plane, jnp.float32),
@@ -476,7 +478,7 @@
         ],
         compiler_params=pltpu.CompilerParams(vmem_limit_bytes=VMEM_BYTES),
         name="smooth",
-    )(near, far, exact)
+    )(exact, *chips)
 
 
 def body(volume, footprint, tile_block, tile_cells, measured):
@@ -495,14 +497,14 @@
     ]
     turned = turn(footprint)
     exact, rounded = correct(plan, seen, parts, turned)
-    parts = [rounded] + [swap_all(rounded, "xy", flip) for flip in range(bands - 1, 0, -1)]
+    parts = [rounded] + [swap_all(rounded, "xy", flip) for flip in range(1, bands)]
     tiled = back_project(plan, volume, turned, block, cells, parts)
 
-    line = [tiled] + [swap_all(tiled, "xy", flip) for flip in range(bands - 1, 0, -1)]
+    line = [tiled] + [swap_all(tiled, "xy", flip) for flip in range(1, bands)]
     line = jnp.concatenate([each[:-1] for each in line] + [sum(each[-1:] for each in line)])
-    near = jnp.stack([line] + [swap_all(line, "slab", flip) for flip in range(slabs - 2, 0, -2)])
-    far = swap_all(near, "slab", 1)
-    return smooth(volume, near, far, exact, slabs, bands, footprint.shape[2])
+    chips = [line] + [swap_all(line, "slab", flip) for flip in range(2, slabs, 2)]
+    chips += [swap_all(each, "slab", 1) for each in chips[::-1]]
+    return smooth(volume, chips, exact, slabs, bands, footprint.shape[2])
 
 
 def solution(mesh):

time: 50.7 us -> 50.1 us (0.988)
  waiting for transfers between devices: 17.1 us -> 16.2 us
    ppermute x13 -> x16, waiting for transfers between devices: 15.4 us -> 14.5 us  [swap_all(): return lax.ppermute(cells, axis, [(i, i ^ flip) for i in range(count)])]
    ppermute x13 -> x16, starting transfers between devices: 17.6 us -> 17.9 us  [swap_all(): return lax.ppermute(cells, axis, [(i, i ^ flip) for i in range(count)])]
  transfers between devices with their start and end apart: 15 -> 18, of which waited for: 14 -> 13; matrix products, arithmetic and copies ran while one was open for 0% -> 0% of each run, Pallas kernels for 4% -> 4%
where the time goes in v6:
time: 50.1 us; the launch traced here: 50 us
  starting transfers between devices  21.4 us (43%)
  waiting for transfers between devices  16.2 us (32%)
  Pallas kernels  11.6 us (23%)
  between operations  0.73 us (1%)
    ppermute x16, starting transfers between devices, swap_all(): return lax.ppermute(cells, axis, [(i, i ^ flip) for i in range(count)])  17.9 us
    ppermute x16, waiting for transfers between devices, swap_all(): return lax.ppermute(cells, axis, [(i, i ^ flip) for i in range(count)])  14.5 us
    pallas_call x1, Pallas kernels, project(): pl.pallas_call(functools.partial(project_kernel, plan, shape), out_shape=...  3.9 us
    ppermute x2, starting transfers between devices, shift_all(): lax.ppermute(cells, axis, [(i, (i + step) % count) for i in range(count)])  3.45 us
    pallas_call x1, Pallas kernels, smooth(): pl.pallas_call(functools.partial(smooth_kernel, sizes), out_shape=(jax.Sh...  3.24 us
    pallas_call x1, Pallas kernels, turn(): pl.pallas_call(functools.partial(turn_kernel, shape), out_shape=pltpu.VME...  2.21 us
    pallas_call x1, Pallas kernels, back_project(): pl.pallas_call(functools.partial(back_kernel, plan, shape), out_shape=jax...  2.14 us
    ppermute x2, waiting for transfers between devices, shift_all(): lax.ppermute(cells, axis, [(i, (i + step) % count) for i in range(count)])  1.75 us
  transfers between devices with their start and end apart: 18, of which 13 were waited for; matrix products, arithmetic and copies ran while one was open for 0% of the time, Pallas kernels for 4%

profile of v6, /device:TPU:0, one launch (start us, length us, event | category | flops | bytes accessed | tf_op | source)
XLA Modules:
  0.0 50.0 jit_solution(6069446025009454611)
XLA Ops:
  0.6 3.9 %project.1 = (f32[10,24,256]{2,1,0:T(8,128)S(1)}, f32[2,24,256]{2,1,0:T(8,128)S(1)}, f32[2,24,256]{2,1,0:T(8,128)S(1)}, f32[2,3,8,256]{3,2,1,0:T(8,128)S(1)}, bf16[2,8,4,2,128,256]{5,4,3,2,1,0:T(8,128)(2,1)S(1)}) custom-call(f32[2,8,512]{2,1,0:T(8,128)} %vol_any.1, bf16[2,8,4,2,128,256]{5,4,3,2,1,0:T(8,128)(2,1)} %foot_hbm.1, s32[2,4,2,8]{3,2,1,0:T(2,128)} %bitcast.2, ...), custom_call_target="tpu_custom_call" | custom-call | tf_op jit(solution)/shard_map/project/pallas_call | solution.py:156
  4.5 0.5 %collective-permute-start = (f32[2,24,256]{2,1,0:T(8,128)S(1)}, f32[2,24,256]{2,1,0:T(8,128)S(1)}, u32[]{:S(2)}, u32[]{:S(2)}) collective-permute-start(f32[2,24,256]{2,1,0:T(8,128)S(1)} %get-tuple-element.16), channel_id=1, source_target_pairs={{0,4},{4,8},{8,12},{12,16},{16,20},{20,24},{24,28},{28,0},{1,5},{5... | collective-permute-start | bytes 147464 | tf_op jit(solution)/shard_map/ppermute | solution.py:44
  5.0 2.9 %collective-permute-start.1 = (f32[2,24,256]{2,1,0:T(8,128)S(1)}, f32[2,24,256]{2,1,0:T(8,128)S(1)}, u32[]{:S(2)}, u32[]{:S(2)}) collective-permute-start(f32[2,24,256]{2,1,0:T(8,128)S(1)} %get-tuple-element.17), channel_id=1, source_target_pairs={{0,28},{4,0},{8,4},{12,8},{16,12},{20,16},{24,20},{28,24},{1,29},{... | collective-permute-start | bytes 147464 | tf_op jit(solution)/shard_map/ppermute | solution.py:44
  8.0 1.7 %collective-permute-done.below_ref = f32[2,24,256]{2,1,0:T(8,128)S(1)} collective-permute-done((f32[2,24,256]{2,1,0:T(8,128)S(1)}, f32[2,24,256]{2,1,0:T(8,128)S(1)}, u32[]{:S(2)}, u32[]{:S(2)}) %collective-permute-start) | collective-permute-done | bytes 49184 | tf_op jit(solution)/shard_map/ppermute | solution.py:44
  9.7 0.1 shares.1
  9.8 4.4 %collective-permute-start.2 = (f32[3,24,256]{2,1,0:T(8,128)S(1)}, f32[3,24,256]{2,1,0:T(8,128)S(1)}, u32[]{:S(2)}, u32[]{:S(2)}) collective-permute-start(f32[3,24,256]{2,1,0:T(8,128)S(1)} %get-tuple-element.19), channel_id=1, source_target_pairs={{0,3},{1,2},{2,1},{3,0},{4,7},{5,6},{6,5},{7,4},{8,11},{9,10},{10,... | collective-permute-start | bytes 221192 | tf_op jit(solution)/shard_map/ppermute | solution.py:53
  14.2 0.6 %collective-permute-start.4 = (f32[3,24,256]{2,1,0:T(8,128)S(1)}, f32[3,24,256]{2,1,0:T(8,128)S(1)}, u32[]{:S(2)}, u32[]{:S(2)}) collective-permute-start(f32[3,24,256]{2,1,0:T(8,128)S(1)} %get-tuple-element.21), channel_id=1, source_target_pairs={{0,2},{1,3},{2,0},{3,1},{4,6},{5,7},{6,4},{7,5},{8,10},{9,11},{10,... | collective-permute-start | bytes 221192 | tf_op jit(solution)/shard_map/ppermute | solution.py:53
  14.8 2.2 %turn.1.ready_ref.foot = bf16[2,8,4,2,256,128]{5,4,3,2,1,0:T(8,128)(2,1)S(1)} custom-call(bf16[2,8,4,2,128,256]{5,4,3,2,1,0:T(8,128)(2,1)S(1)} %get-tuple-element.14.foot), custom_call_target="tpu_custom_call" | custom-call | bytes 16777216 | tf_op jit(solution)/shard_map/turn/pallas_call | solution.py:265
  17.1 0.3 collective-permute-done.2.rest_1_
  17.4 2.8 %collective-permute-done.3.rest_2_ = f32[3,24,256]{2,1,0:T(8,128)S(1)} collective-permute-done((f32[3,24,256]{2,1,0:T(8,128)S(1)}, f32[3,24,256]{2,1,0:T(8,128)S(1)}, u32[]{:S(2)}, u32[]{:S(2)}) %collective-permute-start.3) | collective-permute-done | bytes 73760 | tf_op jit(solution)/shard_map/ppermute | solution.py:53
  20.2 1.1 %collective-permute-done.4.rest_3_ = f32[3,24,256]{2,1,0:T(8,128)S(1)} collective-permute-done((f32[3,24,256]{2,1,0:T(8,128)S(1)}, f32[3,24,256]{2,1,0:T(8,128)S(1)}, u32[]{:S(2)}, u32[]{:S(2)}) %collective-permute-start.4) | collective-permute-done | bytes 73760 | tf_op jit(solution)/shard_map/ppermute | solution.py:53
  21.4 1.4 %collective-permute-start.7 = (bf16[48,256]{1,0:T(8,128)(2,1)S(1)}, bf16[48,256]{1,0:T(8,128)(2,1)S(1)}, u32[]{:S(2)}, u32[]{:S(2)}) collective-permute-start(bf16[48,256]{1,0:T(8,128)(2,1)S(1)} %get-tuple-element.23.rest_0_), channel_id=1, source_target_pairs={{0,3},{1,2},{2,1},{3,0},{4,7},{5,6},{6,5},{7,4},{8,11},{9,10},{10,... | collective-permute-start | bytes 73736 | tf_op jit(solution)/shard_map/ppermute | solution.py:53
  22.8 0.5 collective-permute-start.6
  23.3 2.5 %collective-permute-start.5 = (bf16[48,256]{1,0:T(8,128)(2,1)S(1)}, bf16[48,256]{1,0:T(8,128)(2,1)S(1)}, u32[]{:S(2)}, u32[]{:S(2)}) collective-permute-start(bf16[48,256]{1,0:T(8,128)(2,1)S(1)} %get-tuple-element.23.rest_0_), channel_id=1, source_target_pairs={{0,1},{1,0},{2,3},{3,2},{4,5},{5,4},{6,7},{7,6},{8,9},{9,8},{10,11... | collective-permute-start | bytes 73736 | tf_op jit(solution)/shard_map/ppermute | solution.py:53
  25.8 1.2 %collective-permute-done.7.rest_3_ = bf16[48,256]{1,0:T(8,128)(2,1)S(1)} collective-permute-done((bf16[48,256]{1,0:T(8,128)(2,1)S(1)}, bf16[48,256]{1,0:T(8,128)(2,1)S(1)}, u32[]{:S(2)}, u32[]{:S(2)}) %collective-permute-start.7) | collective-permute-done | bytes 24608 | tf_op jit(solution)/shard_map/ppermute | solution.py:53
  27.1 0.5 collective-permute-done.6.rest_2_
  27.6 0.2 collective-permute-done.5.rest_1_
  27.8 2.1 %back_project.1 = f32[9,8,128]{2,1,0:T(8,128)S(1)} custom-call(f32[2,8,512]{2,1,0:T(8,128)S(1)} %copy-done, bf16[2,8,4,2,256,128]{5,4,3,2,1,0:T(8,128)(2,1)S(1)} %turn.1.ready_ref.foot, s32[2,4,2,8]{3,2,1,0:T(2,128)S(1)} %bitcast.3, s32[2,4,2,8]{3,2,1,0:T(2,128)S(1)} %bitcast.5, bf16[48,256]{1,0:T(8,128)(2,1)S(1)} %get-tuple-element.23.rest_0_, ...), custom_call_target="tpu_custom_call" | custom-call | tf_op jit(solution)/shard_map/back_project/pallas_call | solution.py:328
  30.0 2.5 %collective-permute-start.10 = (f32[9,8,128]{2,1,0:T(8,128)S(1)}, f32[9,8,128]{2,1,0:T(8,128)S(1)}, u32[]{:S(2)}, u32[]{:S(2)}) collective-permute-start(f32[9,8,128]{2,1,0:T(8,128)S(1)} %back_project.1), channel_id=1, source_target_pairs={{0,3},{1,2},{2,1},{3,0},{4,7},{5,6},{6,5},{7,4},{8,11},{9,10},{10,... | collective-permute-start | bytes 110600 | tf_op jit(solution)/shard_map/ppermute | solution.py:53
  32.5 0.9 %collective-permute-start.9 = (f32[9,8,128]{2,1,0:T(8,128)S(1)}, f32[9,8,128]{2,1,0:T(8,128)S(1)}, u32[]{:S(2)}, u32[]{:S(2)}) collective-permute-start(f32[9,8,128]{2,1,0:T(8,128)S(1)} %back_project.1), channel_id=1, source_target_pairs={{0,2},{1,3},{2,0},{3,1},{4,6},{5,7},{6,4},{7,5},{8,10},{9,11},{10,... | collective-permute-start | bytes 110600 | tf_op jit(solution)/shard_map/ppermute | solution.py:53
  33.3 1.1 %collective-permute-start.8 = (f32[9,8,128]{2,1,0:T(8,128)S(1)}, f32[9,8,128]{2,1,0:T(8,128)S(1)}, u32[]{:S(2)}, u32[]{:S(2)}) collective-permute-start(f32[9,8,128]{2,1,0:T(8,128)S(1)} %back_project.1), channel_id=1, source_target_pairs={{0,1},{1,0},{2,3},{3,2},{4,5},{5,4},{6,7},{7,6},{8,9},{9,8},{10,11... | collective-permute-start | bytes 110600 | tf_op jit(solution)/shard_map/ppermute | solution.py:53
  34.4 3.3 %collective-permute-done.8 = f32[9,8,128]{2,1,0:T(8,128)S(1)} collective-permute-done((f32[9,8,128]{2,1,0:T(8,128)S(1)}, f32[9,8,128]{2,1,0:T(8,128)S(1)}, u32[]{:S(2)}, u32[]{:S(2)}) %collective-permute-start.8) | collective-permute-done | bytes 36896 | tf_op jit(solution)/shard_map/ppermute | solution.py:53
  37.8 1.3 %collective-permute-start.13 = (f32[33,8,128]{2,1,0:T(8,128)S(1)}, f32[33,8,128]{2,1,0:T(8,128)S(1)}, u32[]{:S(2)}, u32[]{:S(2)}) collective-permute-start(f32[33,8,128]{2,1,0:T(8,128)S(1)} %constant_dynamic-update-slice_fusion.rest_0_), channel_id=1, source_target_pairs={{0,24},{4,28},{8,16},{12,20},{16,8},{20,12},{24,0},{28,4},{1,25},{... | collective-permute-start | bytes 405512 | tf_op jit(solution)/shard_map/ppermute | solution.py:53
  39.1 0.8 %collective-permute-start.12 = (f32[33,8,128]{2,1,0:T(8,128)S(1)}, f32[33,8,128]{2,1,0:T(8,128)S(1)}, u32[]{:S(2)}, u32[]{:S(2)}) collective-permute-start(f32[33,8,128]{2,1,0:T(8,128)S(1)} %constant_dynamic-update-slice_fusion.rest_0_), channel_id=1, source_target_pairs={{0,16},{4,20},{8,24},{12,28},{16,0},{20,4},{24,8},{28,12},{1,17},{... | collective-permute-start | bytes 405512 | tf_op jit(solution)/shard_map/ppermute | solution.py:53
  39.9 1.4 %collective-permute-start.11 = (f32[33,8,128]{2,1,0:T(8,128)S(1)}, f32[33,8,128]{2,1,0:T(8,128)S(1)}, u32[]{:S(2)}, u32[]{:S(2)}) collective-permute-start(f32[33,8,128]{2,1,0:T(8,128)S(1)} %constant_dynamic-update-slice_fusion.rest_0_), channel_id=1, source_target_pairs={{0,8},{4,12},{8,0},{12,4},{16,24},{20,28},{24,16},{28,20},{1,9},{5... | collective-permute-start | bytes 405512 | tf_op jit(solution)/shard_map/ppermute | solution.py:53
  41.3 2.5 %collective-permute-done.13.rest_3_ = f32[33,8,128]{2,1,0:T(8,128)S(1)} collective-permute-done((f32[33,8,128]{2,1,0:T(8,128)S(1)}, f32[33,8,128]{2,1,0:T(8,128)S(1)}, u32[]{:S(2)}, u32[]{:S(2)}) %collective-permute-start.13) | collective-permute-done | bytes 135200 | tf_op jit(solution)/shard_map/ppermute | solution.py:53
  43.8 1.3 %collective-permute-done.12.rest_2_ = f32[33,8,128]{2,1,0:T(8,128)S(1)} collective-permute-done((f32[33,8,128]{2,1,0:T(8,128)S(1)}, f32[33,8,128]{2,1,0:T(8,128)S(1)}, u32[]{:S(2)}, u32[]{:S(2)}) %collective-permute-start.12) | collective-permute-done | bytes 135200 | tf_op jit(solution)/shard_map/ppermute | solution.py:53
  45.2 0.1 collective-permute-done.11.rest_1_
  45.3 0.4 collective-permute-start.16
  45.7 0.8 %collective-permute-done.15.rest_5_ = f32[33,8,128]{2,1,0:T(8,128)S(1)} collective-permute-done((f32[33,8,128]{2,1,0:T(8,128)S(1)}, f32[33,8,128]{2,1,0:T(8,128)S(1)}, u32[]{:S(2)}, u32[]{:S(2)}) %collective-permute-start.15) | collective-permute-done | bytes 135200 | tf_op jit(solution)/shard_map/ppermute | solution.py:53
  46.5 0.2 collective-permute-done.16.rest_6_
  46.7 3.2 %smooth.1 = (f32[2,8,512]{2,1,0:T(8,128)}, f32[2,4096]{1,0:T(2,128)}) custom-call(f32[2,2,8,256]{3,2,1,0:T(8,128)S(1)} %get-tuple-element.22.exact_ref, f32[33,8,128]{2,1,0:T(8,128)S(1)} %constant_dynamic-update-slice_fusion.rest_0_, f32[33,8,128]{2,1,0:T(8,128)S(1)} %collective-permute-done.11.rest_1_, f32[33,8,128]{2,1,0:T(8,128)S(1)} %collective-permute-done.12.rest_2_, ...), custom_call_target="tpu_custom_call" | custom-call | tf_op jit(solution)/shard_map/smooth/pallas_call | solution.py:466
  (21 shorter events, 0.2 us)
Async XLA Ops:
  4.5 5.2 %collective-permute-start = (f32[2,24,256]{2,1,0:T(8,128)S(1)}, f32[2,24,256]{2,1,0:T(8,128)S(1)}, u32[]{:S(2)}, u32[]{:S(2)}) collective-permute-start(f32[2,24,256]{2,1,0:T(8,128)S(1)} %get-tuple-element.16), channel_id=1, source_target_pairs={{0,4},{4,8},{8,12},{12,16},{16,20},{20,24},{24,28},{28,0},{1,5},{5... | collective-permute-start | bytes 147464 | tf_op jit(solution)/shard_map/ppermute | solution.py:44
  5.0 4.7 %collective-permute-start.1 = (f32[2,24,256]{2,1,0:T(8,128)S(1)}, f32[2,24,256]{2,1,0:T(8,128)S(1)}, u32[]{:S(2)}, u32[]{:S(2)}) collective-permute-start(f32[2,24,256]{2,1,0:T(8,128)S(1)} %get-tuple-element.17), channel_id=1, source_target_pairs={{0,28},{4,0},{8,4},{12,8},{16,12},{20,16},{24,20},{28,24},{1,29},{... | collective-permute-start | bytes 147464 | tf_op jit(solution)/shard_map/ppermute | solution.py:44
  9.8 7.6 %collective-permute-start.2 = (f32[3,24,256]{2,1,0:T(8,128)S(1)}, f32[3,24,256]{2,1,0:T(8,128)S(1)}, u32[]{:S(2)}, u32[]{:S(2)}) collective-permute-start(f32[3,24,256]{2,1,0:T(8,128)S(1)} %get-tuple-element.19), channel_id=1, source_target_pairs={{0,3},{1,2},{2,1},{3,0},{4,7},{5,6},{6,5},{7,4},{8,11},{9,10},{10,... | collective-permute-start | bytes 221192 | tf_op jit(solution)/shard_map/ppermute | solution.py:53
  14.2 6.0 %collective-permute-start.3 = (f32[3,24,256]{2,1,0:T(8,128)S(1)}, f32[3,24,256]{2,1,0:T(8,128)S(1)}, u32[]{:S(2)}, u32[]{:S(2)}) collective-permute-start(f32[3,24,256]{2,1,0:T(8,128)S(1)} %get-tuple-element.20), channel_id=1, source_target_pairs={{0,1},{1,0},{2,3},{3,2},{4,5},{5,4},{6,7},{7,6},{8,9},{9,8},{10,11... | collective-permute-start | bytes 221192 | tf_op jit(solution)/shard_map/ppermute | solution.py:53
  14.2 7.1 %collective-permute-start.4 = (f32[3,24,256]{2,1,0:T(8,128)S(1)}, f32[3,24,256]{2,1,0:T(8,128)S(1)}, u32[]{:S(2)}, u32[]{:S(2)}) collective-permute-start(f32[3,24,256]{2,1,0:T(8,128)S(1)} %get-tuple-element.21), channel_id=1, source_target_pairs={{0,2},{1,3},{2,0},{3,1},{4,6},{5,7},{6,4},{7,5},{8,10},{9,11},{10,... | collective-permute-start | bytes 221192 | tf_op jit(solution)/shard_map/ppermute | solution.py:53
  17.0 10.8 %copy-start = (f32[2,8,512]{2,1,0:T(8,128)S(1)}, f32[2,8,512]{2,1,0:T(8,128)}, u32[]{:S(2)}) copy-start(f32[2,8,512]{2,1,0:T(8,128)} %vol_any.1) | copy-start | bytes 98308
  17.1 10.8 %copy-start.1 = (s32[2,8,4,2]{1,3,2,0:T(2,128)S(1)}, s32[2,8,4,2]{1,3,2,0:T(2,128)}, u32[]{:S(2)}) copy-start(s32[2,8,4,2]{1,3,2,0:T(2,128)} %param.7) | copy-start | bytes 1540
  17.1 10.8 %copy-start.2 = (s32[2,8,4,2]{1,3,2,0:T(2,128)S(1)}, s32[2,8,4,2]{1,3,2,0:T(2,128)}, u32[]{:S(2)}) copy-start(s32[2,8,4,2]{1,3,2,0:T(2,128)} %param.8) | copy-start | bytes 1540
  21.4 5.7 %collective-permute-start.7 = (bf16[48,256]{1,0:T(8,128)(2,1)S(1)}, bf16[48,256]{1,0:T(8,128)(2,1)S(1)}, u32[]{:S(2)}, u32[]{:S(2)}) collective-permute-start(bf16[48,256]{1,0:T(8,128)(2,1)S(1)} %get-tuple-element.23.rest_0_), channel_id=1, source_target_pairs={{0,3},{1,2},{2,1},{3,0},{4,7},{5,6},{6,5},{7,4},{8,11},{9,10},{10,... | collective-permute-start | bytes 73736 | tf_op jit(solution)/shard_map/ppermute | solution.py:53
  22.8 4.7 %collective-permute-start.6 = (bf16[48,256]{1,0:T(8,128)(2,1)S(1)}, bf16[48,256]{1,0:T(8,128)(2,1)S(1)}, u32[]{:S(2)}, u32[]{:S(2)}) collective-permute-start(bf16[48,256]{1,0:T(8,128)(2,1)S(1)} %get-tuple-element.23.rest_0_), channel_id=1, source_target_pairs={{0,2},{1,3},{2,0},{3,1},{4,6},{5,7},{6,4},{7,5},{8,10},{9,11},{10,... | collective-permute-start | bytes 73736 | tf_op jit(solution)/shard_map/ppermute | solution.py:53
  23.3 4.5 %collective-permute-start.5 = (bf16[48,256]{1,0:T(8,128)(2,1)S(1)}, bf16[48,256]{1,0:T(8,128)(2,1)S(1)}, u32[]{:S(2)}, u32[]{:S(2)}) collective-permute-start(bf16[48,256]{1,0:T(8,128)(2,1)S(1)} %get-tuple-element.23.rest_0_), channel_id=1, source_target_pairs={{0,1},{1,0},{2,3},{3,2},{4,5},{5,4},{6,7},{7,6},{8,9},{9,8},{10,11... | collective-permute-start | bytes 73736 | tf_op jit(solution)/shard_map/ppermute | solution.py:53
  30.0 7.7 %collective-permute-start.10 = (f32[9,8,128]{2,1,0:T(8,128)S(1)}, f32[9,8,128]{2,1,0:T(8,128)S(1)}, u32[]{:S(2)}, u32[]{:S(2)}) collective-permute-start(f32[9,8,128]{2,1,0:T(8,128)S(1)} %back_project.1), channel_id=1, source_target_pairs={{0,3},{1,2},{2,1},{3,0},{4,7},{5,6},{6,5},{7,4},{8,11},{9,10},{10,... | collective-permute-start | bytes 110600 | tf_op jit(solution)/shard_map/ppermute | solution.py:53
  32.5 5.2 %collective-permute-start.9 = (f32[9,8,128]{2,1,0:T(8,128)S(1)}, f32[9,8,128]{2,1,0:T(8,128)S(1)}, u32[]{:S(2)}, u32[]{:S(2)}) collective-permute-start(f32[9,8,128]{2,1,0:T(8,128)S(1)} %back_project.1), channel_id=1, source_target_pairs={{0,2},{1,3},{2,0},{3,1},{4,6},{5,7},{6,4},{7,5},{8,10},{9,11},{10,... | collective-permute-start | bytes 110600 | tf_op jit(solution)/shard_map/ppermute | solution.py:53
  33.3 4.4 %collective-permute-start.8 = (f32[9,8,128]{2,1,0:T(8,128)S(1)}, f32[9,8,128]{2,1,0:T(8,128)S(1)}, u32[]{:S(2)}, u32[]{:S(2)}) collective-permute-start(f32[9,8,128]{2,1,0:T(8,128)S(1)} %back_project.1), channel_id=1, source_target_pairs={{0,1},{1,0},{2,3},{3,2},{4,5},{5,4},{6,7},{7,6},{8,9},{9,8},{10,11... | collective-permute-start | bytes 110600 | tf_op jit(solution)/shard_map/ppermute | solution.py:53
  37.8 6.1 %collective-permute-start.13 = (f32[33,8,128]{2,1,0:T(8,128)S(1)}, f32[33,8,128]{2,1,0:T(8,128)S(1)}, u32[]{:S(2)}, u32[]{:S(2)}) collective-permute-start(f32[33,8,128]{2,1,0:T(8,128)S(1)} %constant_dynamic-update-slice_fusion.rest_0_), channel_id=1, source_target_pairs={{0,24},{4,28},{8,16},{12,20},{16,8},{20,12},{24,0},{28,4},{1,25},{... | collective-permute-start | bytes 405512 | tf_op jit(solution)/shard_map/ppermute | solution.py:53
  39.1 6.1 %collective-permute-start.12 = (f32[33,8,128]{2,1,0:T(8,128)S(1)}, f32[33,8,128]{2,1,0:T(8,128)S(1)}, u32[]{:S(2)}, u32[]{:S(2)}) collective-permute-start(f32[33,8,128]{2,1,0:T(8,128)S(1)} %constant_dynamic-update-slice_fusion.rest_0_), channel_id=1, source_target_pairs={{0,16},{4,20},{8,24},{12,28},{16,0},{20,4},{24,8},{28,12},{1,17},{... | collective-permute-start | bytes 405512 | tf_op jit(solution)/shard_map/ppermute | solution.py:53
  39.9 5.4 %collective-permute-start.11 = (f32[33,8,128]{2,1,0:T(8,128)S(1)}, f32[33,8,128]{2,1,0:T(8,128)S(1)}, u32[]{:S(2)}, u32[]{:S(2)}) collective-permute-start(f32[33,8,128]{2,1,0:T(8,128)S(1)} %constant_dynamic-update-slice_fusion.rest_0_), channel_id=1, source_target_pairs={{0,8},{4,12},{8,0},{12,4},{16,24},{20,28},{24,16},{28,20},{1,9},{5... | collective-permute-start | bytes 405512 | tf_op jit(solution)/shard_map/ppermute | solution.py:53
  41.3 4.4 %collective-permute-start.17 = (f32[33,8,128]{2,1,0:T(8,128)S(1)}, f32[33,8,128]{2,1,0:T(8,128)S(1)}, u32[]{:S(2)}, u32[]{:S(2)}) collective-permute-start(f32[33,8,128]{2,1,0:T(8,128)S(1)} %constant_dynamic-update-slice_fusion.rest_0_), channel_id=1, source_target_pairs={{0,4},{4,0},{8,12},{12,8},{16,20},{20,16},{24,28},{28,24},{1,5},{5... | collective-permute-start | bytes 405512 | tf_op jit(solution)/shard_map/ppermute | solution.py:53
  43.8 1.9 %collective-permute-start.14 = (f32[33,8,128]{2,1,0:T(8,128)S(1)}, f32[33,8,128]{2,1,0:T(8,128)S(1)}, u32[]{:S(2)}, u32[]{:S(2)}) collective-permute-start(f32[33,8,128]{2,1,0:T(8,128)S(1)} %collective-permute-done.13.rest_3_), channel_id=1, source_target_pairs={{0,4},{4,0},{8,12},{12,8},{16,20},{20,16},{24,28},{28,24},{1,5},{5... | collective-permute-start | bytes 405512 | tf_op jit(solution)/shard_map/ppermute | solution.py:53
  45.2 1.4 %collective-permute-start.15 = (f32[33,8,128]{2,1,0:T(8,128)S(1)}, f32[33,8,128]{2,1,0:T(8,128)S(1)}, u32[]{:S(2)}, u32[]{:S(2)}) collective-permute-start(f32[33,8,128]{2,1,0:T(8,128)S(1)} %collective-permute-done.12.rest_2_), channel_id=1, source_target_pairs={{0,4},{4,0},{8,12},{12,8},{16,20},{20,16},{24,28},{28,24},{1,5},{5... | collective-permute-start | bytes 405512 | tf_op jit(solution)/shard_map/ppermute | solution.py:53
  45.3 1.4 %collective-permute-start.16 = (f32[33,8,128]{2,1,0:T(8,128)S(1)}, f32[33,8,128]{2,1,0:T(8,128)S(1)}, u32[]{:S(2)}, u32[]{:S(2)}) collective-permute-start(f32[33,8,128]{2,1,0:T(8,128)S(1)} %collective-permute-done.11.rest_1_), channel_id=1, source_target_pairs={{0,4},{4,0},{8,12},{12,8},{16,20},{20,16},{24,28},{28,24},{1,5},{5... | collective-permute-start | bytes 405512 | tf_op jit(solution)/shard_map/ppermute | solution.py:53

commit v7 on v6

--- a/solution.py
+++ b/solution.py
@@ -57,7 +57,9 @@
     local = jnp.clip(
         block - slab * plan.slab_own + plan.halo, 0, plan.units * plan.unit - 1
     )
-    return lax.div(local, plan.unit), lax.rem(local, plan.unit)
+    if plan.unit & (plan.unit - 1):
+        return lax.div(local, plan.unit), lax.rem(local, plan.unit)
+    return local >> (plan.unit.bit_length() - 1), local & (plan.unit - 1)
 
 
 def copy_all(pairs, sems):
@@ -303,13 +305,18 @@
     for p in range(planes):
         for t in range(tiles):
             for r in range(rows):
-                both = 0.0
+                lefts = []
                 for v in range(views):
                     unit, column = unit_of(plan, block_ref[p, t, v, r], slab)
                     picked = jnp.broadcast_to(corr[v, unit, pl.ds(column, 1), :], (8, tdet))
                     left = jnp.where(top, picked, 1.0)
-                    left = jnp.where(lane < cells_ref[p, t, v, r], left, 0.0).astype(jnp.bfloat16)
-                    both += jnp.dot(left, foot[p, r, t, v], preferred_element_type=jnp.float32)
+                    left = jnp.where(lane < cells_ref[p, t, v, r], left, 0.0)
+                    lefts.append(left.astype(jnp.bfloat16))
+                both = jnp.dot(
+                    jnp.concatenate(lefts, axis=1),
+                    foot[p, r, t].reshape(views * tdet, tvox),
+                    preferred_element_type=jnp.float32,
+                )
                 sums[0, r : r + 1] = both[0:1]
                 sums[1, r : r + 1] = both[1:2]
             volume = vol_ref[p, :, t * tvox : (t + 1) * tvox]

time: 50.1 us -> 50.1 us (level)
  no operation moved by 1% of the time
where the time goes in v7:
time: 50.1 us; the launch traced here: 49.9 us
  starting transfers between devices  21.4 us (43%)
  waiting for transfers between devices  16.2 us (32%)
  Pallas kernels  11.6 us (23%)
  between operations  0.73 us (1%)
    ppermute x16, starting transfers between devices, swap_all(): return lax.ppermute(cells, axis, [(i, i ^ flip) for i in range(count)])  17.9 us
    ppermute x16, waiting for transfers between devices, swap_all(): return lax.ppermute(cells, axis, [(i, i ^ flip) for i in range(count)])  14.5 us
    pallas_call x1, Pallas kernels, project(): pl.pallas_call(functools.partial(project_kernel, plan, shape), out_shape=...  3.9 us
    ppermute x2, starting transfers between devices, shift_all(): lax.ppermute(cells, axis, [(i, (i + step) % count) for i in range(count)])  3.45 us
    pallas_call x1, Pallas kernels, smooth(): pl.pallas_call(functools.partial(smooth_kernel, sizes), out_shape=(jax.Sh...  3.24 us
    pallas_call x1, Pallas kernels, turn(): pl.pallas_call(functools.partial(turn_kernel, shape), out_shape=pltpu.VME...  2.21 us
    pallas_call x1, Pallas kernels, back_project(): pl.pallas_call(functools.partial(back_kernel, plan, shape), out_shape=jax...  2.11 us
    ppermute x2, waiting for transfers between devices, shift_all(): lax.ppermute(cells, axis, [(i, (i + step) % count) for i in range(count)])  1.75 us
  transfers between devices with their start and end apart: 18, of which 13 were waited for; matrix products, arithmetic and copies ran while one was open for 0% of the time, Pallas kernels for 4%

profile of v7, /device:TPU:0, one launch (start us, length us, event | category | flops | bytes accessed | tf_op | source)
XLA Modules:
  0.0 49.9 jit_solution(11564249419235359248)
XLA Ops:
  0.6 3.9 %project.1 = (f32[10,24,256]{2,1,0:T(8,128)S(1)}, f32[2,24,256]{2,1,0:T(8,128)S(1)}, f32[2,24,256]{2,1,0:T(8,128)S(1)}, f32[2,3,8,256]{3,2,1,0:T(8,128)S(1)}, bf16[2,8,4,2,128,256]{5,4,3,2,1,0:T(8,128)(2,1)S(1)}) custom-call(f32[2,8,512]{2,1,0:T(8,128)} %vol_any.1, bf16[2,8,4,2,128,256]{5,4,3,2,1,0:T(8,128)(2,1)} %foot_hbm.1, s32[2,4,2,8]{3,2,1,0:T(2,128)} %bitcast.2, ...), custom_call_target="tpu_custom_call" | custom-call | tf_op jit(solution)/shard_map/project/pallas_call | solution.py:158
  4.5 0.5 %collective-permute-start = (f32[2,24,256]{2,1,0:T(8,128)S(1)}, f32[2,24,256]{2,1,0:T(8,128)S(1)}, u32[]{:S(2)}, u32[]{:S(2)}) collective-permute-start(f32[2,24,256]{2,1,0:T(8,128)S(1)} %get-tuple-element.16), channel_id=1, source_target_pairs={{0,4},{4,8},{8,12},{12,16},{16,20},{20,24},{24,28},{28,0},{1,5},{5... | collective-permute-start | bytes 147464 | tf_op jit(solution)/shard_map/ppermute | solution.py:44
  5.0 2.9 %collective-permute-start.1 = (f32[2,24,256]{2,1,0:T(8,128)S(1)}, f32[2,24,256]{2,1,0:T(8,128)S(1)}, u32[]{:S(2)}, u32[]{:S(2)}) collective-permute-start(f32[2,24,256]{2,1,0:T(8,128)S(1)} %get-tuple-element.17), channel_id=1, source_target_pairs={{0,28},{4,0},{8,4},{12,8},{16,12},{20,16},{24,20},{28,24},{1,29},{... | collective-permute-start | bytes 147464 | tf_op jit(solution)/shard_map/ppermute | solution.py:44
  8.0 1.7 %collective-permute-done.below_ref = f32[2,24,256]{2,1,0:T(8,128)S(1)} collective-permute-done((f32[2,24,256]{2,1,0:T(8,128)S(1)}, f32[2,24,256]{2,1,0:T(8,128)S(1)}, u32[]{:S(2)}, u32[]{:S(2)}) %collective-permute-start) | collective-permute-done | bytes 49184 | tf_op jit(solution)/shard_map/ppermute | solution.py:44
  9.7 0.1 shares.1
  9.8 4.4 %collective-permute-start.2 = (f32[3,24,256]{2,1,0:T(8,128)S(1)}, f32[3,24,256]{2,1,0:T(8,128)S(1)}, u32[]{:S(2)}, u32[]{:S(2)}) collective-permute-start(f32[3,24,256]{2,1,0:T(8,128)S(1)} %get-tuple-element.19), channel_id=1, source_target_pairs={{0,3},{1,2},{2,1},{3,0},{4,7},{5,6},{6,5},{7,4},{8,11},{9,10},{10,... | collective-permute-start | bytes 221192 | tf_op jit(solution)/shard_map/ppermute | solution.py:53
  14.2 0.6 %collective-permute-start.4 = (f32[3,24,256]{2,1,0:T(8,128)S(1)}, f32[3,24,256]{2,1,0:T(8,128)S(1)}, u32[]{:S(2)}, u32[]{:S(2)}) collective-permute-start(f32[3,24,256]{2,1,0:T(8,128)S(1)} %get-tuple-element.21), channel_id=1, source_target_pairs={{0,2},{1,3},{2,0},{3,1},{4,6},{5,7},{6,4},{7,5},{8,10},{9,11},{10,... | collective-permute-start | bytes 221192 | tf_op jit(solution)/shard_map/ppermute | solution.py:53
  14.8 2.2 %turn.1.ready_ref.foot = bf16[2,8,4,2,256,128]{5,4,3,2,1,0:T(8,128)(2,1)S(1)} custom-call(bf16[2,8,4,2,128,256]{5,4,3,2,1,0:T(8,128)(2,1)S(1)} %get-tuple-element.14.foot), custom_call_target="tpu_custom_call" | custom-call | bytes 16777216 | tf_op jit(solution)/shard_map/turn/pallas_call | solution.py:267
  17.1 0.3 collective-permute-done.2.rest_1_
  17.4 2.8 %collective-permute-done.3.rest_2_ = f32[3,24,256]{2,1,0:T(8,128)S(1)} collective-permute-done((f32[3,24,256]{2,1,0:T(8,128)S(1)}, f32[3,24,256]{2,1,0:T(8,128)S(1)}, u32[]{:S(2)}, u32[]{:S(2)}) %collective-permute-start.3) | collective-permute-done | bytes 73760 | tf_op jit(solution)/shard_map/ppermute | solution.py:53
  20.2 1.1 %collective-permute-done.4.rest_3_ = f32[3,24,256]{2,1,0:T(8,128)S(1)} collective-permute-done((f32[3,24,256]{2,1,0:T(8,128)S(1)}, f32[3,24,256]{2,1,0:T(8,128)S(1)}, u32[]{:S(2)}, u32[]{:S(2)}) %collective-permute-start.4) | collective-permute-done | bytes 73760 | tf_op jit(solution)/shard_map/ppermute | solution.py:53
  21.4 1.4 %collective-permute-start.7 = (bf16[48,256]{1,0:T(8,128)(2,1)S(1)}, bf16[48,256]{1,0:T(8,128)(2,1)S(1)}, u32[]{:S(2)}, u32[]{:S(2)}) collective-permute-start(bf16[48,256]{1,0:T(8,128)(2,1)S(1)} %get-tuple-element.23.rest_0_), channel_id=1, source_target_pairs={{0,3},{1,2},{2,1},{3,0},{4,7},{5,6},{6,5},{7,4},{8,11},{9,10},{10,... | collective-permute-start | bytes 73736 | tf_op jit(solution)/shard_map/ppermute | solution.py:53
  22.8 0.5 collective-permute-start.6
  23.3 2.5 %collective-permute-start.5 = (bf16[48,256]{1,0:T(8,128)(2,1)S(1)}, bf16[48,256]{1,0:T(8,128)(2,1)S(1)}, u32[]{:S(2)}, u32[]{:S(2)}) collective-permute-start(bf16[48,256]{1,0:T(8,128)(2,1)S(1)} %get-tuple-element.23.rest_0_), channel_id=1, source_target_pairs={{0,1},{1,0},{2,3},{3,2},{4,5},{5,4},{6,7},{7,6},{8,9},{9,8},{10,11... | collective-permute-start | bytes 73736 | tf_op jit(solution)/shard_map/ppermute | solution.py:53
  25.8 1.2 %collective-permute-done.7.rest_3_ = bf16[48,256]{1,0:T(8,128)(2,1)S(1)} collective-permute-done((bf16[48,256]{1,0:T(8,128)(2,1)S(1)}, bf16[48,256]{1,0:T(8,128)(2,1)S(1)}, u32[]{:S(2)}, u32[]{:S(2)}) %collective-permute-start.7) | collective-permute-done | bytes 24608 | tf_op jit(solution)/shard_map/ppermute | solution.py:53
  27.1 0.5 collective-permute-done.6.rest_2_
  27.6 0.2 collective-permute-done.5.rest_1_
  27.8 2.1 %back_project.1 = f32[9,8,128]{2,1,0:T(8,128)S(1)} custom-call(f32[2,8,512]{2,1,0:T(8,128)S(1)} %copy-done, bf16[2,8,4,2,256,128]{5,4,3,2,1,0:T(8,128)(2,1)S(1)} %turn.1.ready_ref.foot, s32[2,4,2,8]{3,2,1,0:T(2,128)S(1)} %bitcast.3, s32[2,4,2,8]{3,2,1,0:T(2,128)S(1)} %bitcast.5, bf16[48,256]{1,0:T(8,128)(2,1)S(1)} %get-tuple-element.23.rest_0_, ...), custom_call_target="tpu_custom_call" | custom-call | tf_op jit(solution)/shard_map/back_project/pallas_call | solution.py:335
  29.9 2.5 %collective-permute-start.10 = (f32[9,8,128]{2,1,0:T(8,128)S(1)}, f32[9,8,128]{2,1,0:T(8,128)S(1)}, u32[]{:S(2)}, u32[]{:S(2)}) collective-permute-start(f32[9,8,128]{2,1,0:T(8,128)S(1)} %back_project.1), channel_id=1, source_target_pairs={{0,3},{1,2},{2,1},{3,0},{4,7},{5,6},{6,5},{7,4},{8,11},{9,10},{10,... | collective-permute-start | bytes 110600 | tf_op jit(solution)/shard_map/ppermute | solution.py:53
  32.4 0.9 %collective-permute-start.9 = (f32[9,8,128]{2,1,0:T(8,128)S(1)}, f32[9,8,128]{2,1,0:T(8,128)S(1)}, u32[]{:S(2)}, u32[]{:S(2)}) collective-permute-start(f32[9,8,128]{2,1,0:T(8,128)S(1)} %back_project.1), channel_id=1, source_target_pairs={{0,2},{1,3},{2,0},{3,1},{4,6},{5,7},{6,4},{7,5},{8,10},{9,11},{10,... | collective-permute-start | bytes 110600 | tf_op jit(solution)/shard_map/ppermute | solution.py:53
  33.3 1.1 %collective-permute-start.8 = (f32[9,8,128]{2,1,0:T(8,128)S(1)}, f32[9,8,128]{2,1,0:T(8,128)S(1)}, u32[]{:S(2)}, u32[]{:S(2)}) collective-permute-start(f32[9,8,128]{2,1,0:T(8,128)S(1)} %back_project.1), channel_id=1, source_target_pairs={{0,1},{1,0},{2,3},{3,2},{4,5},{5,4},{6,7},{7,6},{8,9},{9,8},{10,11... | collective-permute-start | bytes 110600 | tf_op jit(solution)/shard_map/ppermute | solution.py:53
  34.4 3.3 %collective-permute-done.8 = f32[9,8,128]{2,1,0:T(8,128)S(1)} collective-permute-done((f32[9,8,128]{2,1,0:T(8,128)S(1)}, f32[9,8,128]{2,1,0:T(8,128)S(1)}, u32[]{:S(2)}, u32[]{:S(2)}) %collective-permute-start.8) | collective-permute-done | bytes 36896 | tf_op jit(solution)/shard_map/ppermute | solution.py:53
  37.7 1.3 %collective-permute-start.13 = (f32[33,8,128]{2,1,0:T(8,128)S(1)}, f32[33,8,128]{2,1,0:T(8,128)S(1)}, u32[]{:S(2)}, u32[]{:S(2)}) collective-permute-start(f32[33,8,128]{2,1,0:T(8,128)S(1)} %constant_dynamic-update-slice_fusion.rest_0_), channel_id=1, source_target_pairs={{0,24},{4,28},{8,16},{12,20},{16,8},{20,12},{24,0},{28,4},{1,25},{... | collective-permute-start | bytes 405512 | tf_op jit(solution)/shard_map/ppermute | solution.py:53
  39.1 0.8 %collective-permute-start.12 = (f32[33,8,128]{2,1,0:T(8,128)S(1)}, f32[33,8,128]{2,1,0:T(8,128)S(1)}, u32[]{:S(2)}, u32[]{:S(2)}) collective-permute-start(f32[33,8,128]{2,1,0:T(8,128)S(1)} %constant_dynamic-update-slice_fusion.rest_0_), channel_id=1, source_target_pairs={{0,16},{4,20},{8,24},{12,28},{16,0},{20,4},{24,8},{28,12},{1,17},{... | collective-permute-start | bytes 405512 | tf_op jit(solution)/shard_map/ppermute | solution.py:53
  39.8 1.4 %collective-permute-start.11 = (f32[33,8,128]{2,1,0:T(8,128)S(1)}, f32[33,8,128]{2,1,0:T(8,128)S(1)}, u32[]{:S(2)}, u32[]{:S(2)}) collective-permute-start(f32[33,8,128]{2,1,0:T(8,128)S(1)} %constant_dynamic-update-slice_fusion.rest_0_), channel_id=1, source_target_pairs={{0,8},{4,12},{8,0},{12,4},{16,24},{20,28},{24,16},{28,20},{1,9},{5... | collective-permute-start | bytes 405512 | tf_op jit(solution)/shard_map/ppermute | solution.py:53
  41.3 2.5 %collective-permute-done.13.rest_3_ = f32[33,8,128]{2,1,0:T(8,128)S(1)} collective-permute-done((f32[33,8,128]{2,1,0:T(8,128)S(1)}, f32[33,8,128]{2,1,0:T(8,128)S(1)}, u32[]{:S(2)}, u32[]{:S(2)}) %collective-permute-start.13) | collective-permute-done | bytes 135200 | tf_op jit(solution)/shard_map/ppermute | solution.py:53
  43.8 1.3 %collective-permute-done.12.rest_2_ = f32[33,8,128]{2,1,0:T(8,128)S(1)} collective-permute-done((f32[33,8,128]{2,1,0:T(8,128)S(1)}, f32[33,8,128]{2,1,0:T(8,128)S(1)}, u32[]{:S(2)}, u32[]{:S(2)}) %collective-permute-start.12) | collective-permute-done | bytes 135200 | tf_op jit(solution)/shard_map/ppermute | solution.py:53
  45.1 0.1 collective-permute-done.11.rest_1_
  45.2 0.4 collective-permute-start.16
  45.7 0.8 %collective-permute-done.15.rest_5_ = f32[33,8,128]{2,1,0:T(8,128)S(1)} collective-permute-done((f32[33,8,128]{2,1,0:T(8,128)S(1)}, f32[33,8,128]{2,1,0:T(8,128)S(1)}, u32[]{:S(2)}, u32[]{:S(2)}) %collective-permute-start.15) | collective-permute-done | bytes 135200 | tf_op jit(solution)/shard_map/ppermute | solution.py:53
  46.5 0.2 collective-permute-done.16.rest_6_
  46.7 3.2 %smooth.1 = (f32[2,8,512]{2,1,0:T(8,128)}, f32[2,4096]{1,0:T(2,128)}) custom-call(f32[2,2,8,256]{3,2,1,0:T(8,128)S(1)} %get-tuple-element.22.exact_ref, f32[33,8,128]{2,1,0:T(8,128)S(1)} %constant_dynamic-update-slice_fusion.rest_0_, f32[33,8,128]{2,1,0:T(8,128)S(1)} %collective-permute-done.11.rest_1_, f32[33,8,128]{2,1,0:T(8,128)S(1)} %collective-permute-done.12.rest_2_, ...), custom_call_target="tpu_custom_call" | custom-call | tf_op jit(solution)/shard_map/smooth/pallas_call | solution.py:473
  (21 shorter events, 0.2 us)
Async XLA Ops:
  4.5 5.2 %collective-permute-start = (f32[2,24,256]{2,1,0:T(8,128)S(1)}, f32[2,24,256]{2,1,0:T(8,128)S(1)}, u32[]{:S(2)}, u32[]{:S(2)}) collective-permute-start(f32[2,24,256]{2,1,0:T(8,128)S(1)} %get-tuple-element.16), channel_id=1, source_target_pairs={{0,4},{4,8},{8,12},{12,16},{16,20},{20,24},{24,28},{28,0},{1,5},{5... | collective-permute-start | bytes 147464 | tf_op jit(solution)/shard_map/ppermute | solution.py:44
  5.0 4.7 %collective-permute-start.1 = (f32[2,24,256]{2,1,0:T(8,128)S(1)}, f32[2,24,256]{2,1,0:T(8,128)S(1)}, u32[]{:S(2)}, u32[]{:S(2)}) collective-permute-start(f32[2,24,256]{2,1,0:T(8,128)S(1)} %get-tuple-element.17), channel_id=1, source_target_pairs={{0,28},{4,0},{8,4},{12,8},{16,12},{20,16},{24,20},{28,24},{1,29},{... | collective-permute-start | bytes 147464 | tf_op jit(solution)/shard_map/ppermute | solution.py:44
  9.8 7.6 %collective-permute-start.2 = (f32[3,24,256]{2,1,0:T(8,128)S(1)}, f32[3,24,256]{2,1,0:T(8,128)S(1)}, u32[]{:S(2)}, u32[]{:S(2)}) collective-permute-start(f32[3,24,256]{2,1,0:T(8,128)S(1)} %get-tuple-element.19), channel_id=1, source_target_pairs={{0,3},{1,2},{2,1},{3,0},{4,7},{5,6},{6,5},{7,4},{8,11},{9,10},{10,... | collective-permute-start | bytes 221192 | tf_op jit(solution)/shard_map/ppermute | solution.py:53
  14.2 6.0 %collective-permute-start.3 = (f32[3,24,256]{2,1,0:T(8,128)S(1)}, f32[3,24,256]{2,1,0:T(8,128)S(1)}, u32[]{:S(2)}, u32[]{:S(2)}) collective-permute-start(f32[3,24,256]{2,1,0:T(8,128)S(1)} %get-tuple-element.20), channel_id=1, source_target_pairs={{0,1},{1,0},{2,3},{3,2},{4,5},{5,4},{6,7},{7,6},{8,9},{9,8},{10,11... | collective-permute-start | bytes 221192 | tf_op jit(solution)/shard_map/ppermute | solution.py:53
  14.2 7.1 %collective-permute-start.4 = (f32[3,24,256]{2,1,0:T(8,128)S(1)}, f32[3,24,256]{2,1,0:T(8,128)S(1)}, u32[]{:S(2)}, u32[]{:S(2)}) collective-permute-start(f32[3,24,256]{2,1,0:T(8,128)S(1)} %get-tuple-element.21), channel_id=1, source_target_pairs={{0,2},{1,3},{2,0},{3,1},{4,6},{5,7},{6,4},{7,5},{8,10},{9,11},{10,... | collective-permute-start | bytes 221192 | tf_op jit(solution)/shard_map/ppermute | solution.py:53
  17.0 10.8 %copy-start = (f32[2,8,512]{2,1,0:T(8,128)S(1)}, f32[2,8,512]{2,1,0:T(8,128)}, u32[]{:S(2)}) copy-start(f32[2,8,512]{2,1,0:T(8,128)} %vol_any.1) | copy-start | bytes 98308
  17.1 10.8 %copy-start.1 = (s32[2,8,4,2]{1,3,2,0:T(2,128)S(1)}, s32[2,8,4,2]{1,3,2,0:T(2,128)}, u32[]{:S(2)}) copy-start(s32[2,8,4,2]{1,3,2,0:T(2,128)} %param.7) | copy-start | bytes 1540
  17.1 10.8 %copy-start.2 = (s32[2,8,4,2]{1,3,2,0:T(2,128)S(1)}, s32[2,8,4,2]{1,3,2,0:T(2,128)}, u32[]{:S(2)}) copy-start(s32[2,8,4,2]{1,3,2,0:T(2,128)} %param.8) | copy-start | bytes 1540
  21.4 5.7 %collective-permute-start.7 = (bf16[48,256]{1,0:T(8,128)(2,1)S(1)}, bf16[48,256]{1,0:T(8,128)(2,1)S(1)}, u32[]{:S(2)}, u32[]{:S(2)}) collective-permute-start(bf16[48,256]{1,0:T(8,128)(2,1)S(1)} %get-tuple-element.23.rest_0_), channel_id=1, source_target_pairs={{0,3},{1,2},{2,1},{3,0},{4,7},{5,6},{6,5},{7,4},{8,11},{9,10},{10,... | collective-permute-start | bytes 73736 | tf_op jit(solution)/shard_map/ppermute | solution.py:53
  22.8 4.7 %collective-permute-start.6 = (bf16[48,256]{1,0:T(8,128)(2,1)S(1)}, bf16[48,256]{1,0:T(8,128)(2,1)S(1)}, u32[]{:S(2)}, u32[]{:S(2)}) collective-permute-start(bf16[48,256]{1,0:T(8,128)(2,1)S(1)} %get-tuple-element.23.rest_0_), channel_id=1, source_target_pairs={{0,2},{1,3},{2,0},{3,1},{4,6},{5,7},{6,4},{7,5},{8,10},{9,11},{10,... | collective-permute-start | bytes 73736 | tf_op jit(solution)/shard_map/ppermute | solution.py:53
  23.3 4.5 %collective-permute-start.5 = (bf16[48,256]{1,0:T(8,128)(2,1)S(1)}, bf16[48,256]{1,0:T(8,128)(2,1)S(1)}, u32[]{:S(2)}, u32[]{:S(2)}) collective-permute-start(bf16[48,256]{1,0:T(8,128)(2,1)S(1)} %get-tuple-element.23.rest_0_), channel_id=1, source_target_pairs={{0,1},{1,0},{2,3},{3,2},{4,5},{5,4},{6,7},{7,6},{8,9},{9,8},{10,11... | collective-permute-start | bytes 73736 | tf_op jit(solution)/shard_map/ppermute | solution.py:53
  29.9 7.7 %collective-permute-start.10 = (f32[9,8,128]{2,1,0:T(8,128)S(1)}, f32[9,8,128]{2,1,0:T(8,128)S(1)}, u32[]{:S(2)}, u32[]{:S(2)}) collective-permute-start(f32[9,8,128]{2,1,0:T(8,128)S(1)} %back_project.1), channel_id=1, source_target_pairs={{0,3},{1,2},{2,1},{3,0},{4,7},{5,6},{6,5},{7,4},{8,11},{9,10},{10,... | collective-permute-start | bytes 110600 | tf_op jit(solution)/shard_map/ppermute | solution.py:53
  32.4 5.2 %collective-permute-start.9 = (f32[9,8,128]{2,1,0:T(8,128)S(1)}, f32[9,8,128]{2,1,0:T(8,128)S(1)}, u32[]{:S(2)}, u32[]{:S(2)}) collective-permute-start(f32[9,8,128]{2,1,0:T(8,128)S(1)} %back_project.1), channel_id=1, source_target_pairs={{0,2},{1,3},{2,0},{3,1},{4,6},{5,7},{6,4},{7,5},{8,10},{9,11},{10,... | collective-permute-start | bytes 110600 | tf_op jit(solution)/shard_map/ppermute | solution.py:53
  33.3 4.4 %collective-permute-start.8 = (f32[9,8,128]{2,1,0:T(8,128)S(1)}, f32[9,8,128]{2,1,0:T(8,128)S(1)}, u32[]{:S(2)}, u32[]{:S(2)}) collective-permute-start(f32[9,8,128]{2,1,0:T(8,128)S(1)} %back_project.1), channel_id=1, source_target_pairs={{0,1},{1,0},{2,3},{3,2},{4,5},{5,4},{6,7},{7,6},{8,9},{9,8},{10,11... | collective-permute-start | bytes 110600 | tf_op jit(solution)/shard_map/ppermute | solution.py:53
  37.7 6.1 %collective-permute-start.13 = (f32[33,8,128]{2,1,0:T(8,128)S(1)}, f32[33,8,128]{2,1,0:T(8,128)S(1)}, u32[]{:S(2)}, u32[]{:S(2)}) collective-permute-start(f32[33,8,128]{2,1,0:T(8,128)S(1)} %constant_dynamic-update-slice_fusion.rest_0_), channel_id=1, source_target_pairs={{0,24},{4,28},{8,16},{12,20},{16,8},{20,12},{24,0},{28,4},{1,25},{... | collective-permute-start | bytes 405512 | tf_op jit(solution)/shard_map/ppermute | solution.py:53
  39.1 6.1 %collective-permute-start.12 = (f32[33,8,128]{2,1,0:T(8,128)S(1)}, f32[33,8,128]{2,1,0:T(8,128)S(1)}, u32[]{:S(2)}, u32[]{:S(2)}) collective-permute-start(f32[33,8,128]{2,1,0:T(8,128)S(1)} %constant_dynamic-update-slice_fusion.rest_0_), channel_id=1, source_target_pairs={{0,16},{4,20},{8,24},{12,28},{16,0},{20,4},{24,8},{28,12},{1,17},{... | collective-permute-start | bytes 405512 | tf_op jit(solution)/shard_map/ppermute | solution.py:53
  39.8 5.4 %collective-permute-start.11 = (f32[33,8,128]{2,1,0:T(8,128)S(1)}, f32[33,8,128]{2,1,0:T(8,128)S(1)}, u32[]{:S(2)}, u32[]{:S(2)}) collective-permute-start(f32[33,8,128]{2,1,0:T(8,128)S(1)} %constant_dynamic-update-slice_fusion.rest_0_), channel_id=1, source_target_pairs={{0,8},{4,12},{8,0},{12,4},{16,24},{20,28},{24,16},{28,20},{1,9},{5... | collective-permute-start | bytes 405512 | tf_op jit(solution)/shard_map/ppermute | solution.py:53
  41.3 4.4 %collective-permute-start.17 = (f32[33,8,128]{2,1,0:T(8,128)S(1)}, f32[33,8,128]{2,1,0:T(8,128)S(1)}, u32[]{:S(2)}, u32[]{:S(2)}) collective-permute-start(f32[33,8,128]{2,1,0:T(8,128)S(1)} %constant_dynamic-update-slice_fusion.rest_0_), channel_id=1, source_target_pairs={{0,4},{4,0},{8,12},{12,8},{16,20},{20,16},{24,28},{28,24},{1,5},{5... | collective-permute-start | bytes 405512 | tf_op jit(solution)/shard_map/ppermute | solution.py:53
  43.8 1.9 %collective-permute-start.14 = (f32[33,8,128]{2,1,0:T(8,128)S(1)}, f32[33,8,128]{2,1,0:T(8,128)S(1)}, u32[]{:S(2)}, u32[]{:S(2)}) collective-permute-start(f32[33,8,128]{2,1,0:T(8,128)S(1)} %collective-permute-done.13.rest_3_), channel_id=1, source_target_pairs={{0,4},{4,0},{8,12},{12,8},{16,20},{20,16},{24,28},{28,24},{1,5},{5... | collective-permute-start | bytes 405512 | tf_op jit(solution)/shard_map/ppermute | solution.py:53
  45.1 1.4 %collective-permute-start.15 = (f32[33,8,128]{2,1,0:T(8,128)S(1)}, f32[33,8,128]{2,1,0:T(8,128)S(1)}, u32[]{:S(2)}, u32[]{:S(2)}) collective-permute-start(f32[33,8,128]{2,1,0:T(8,128)S(1)} %collective-permute-done.12.rest_2_), channel_id=1, source_target_pairs={{0,4},{4,0},{8,12},{12,8},{16,20},{20,16},{24,28},{28,24},{1,5},{5... | collective-permute-start | bytes 405512 | tf_op jit(solution)/shard_map/ppermute | solution.py:53
  45.2 1.4 %collective-permute-start.16 = (f32[33,8,128]{2,1,0:T(8,128)S(1)}, f32[33,8,128]{2,1,0:T(8,128)S(1)}, u32[]{:S(2)}, u32[]{:S(2)}) collective-permute-start(f32[33,8,128]{2,1,0:T(8,128)S(1)} %collective-permute-done.11.rest_1_), channel_id=1, source_target_pairs={{0,4},{4,0},{8,12},{12,8},{16,20},{20,16},{24,28},{28,24},{1,5},{5... | collective-permute-start | bytes 405512 | tf_op jit(solution)/shard_map/ppermute | solution.py:53

commit v8 on v7

--- a/solution.py
+++ b/solution.py
@@ -277,11 +277,11 @@
     )(footprint)
 
 
-def back_kernel(plan, shape, vol_any, foot, block_any, cells_any, *rest):
-    parts, (out_ref, sums, corr, vol_ref, block_ref, cells_ref, small) = rest[:-7], rest[-7:]
+def back_kernel(plan, shape, vol_ref, foot, block_any, cells_any, *rest):
+    parts, (out_ref, sums, corr, block_ref, cells_ref, small) = rest[:-6], rest[-6:]
     planes, rows, tiles, views, tvox, tdet = shape
     slab, band = lax.axis_index("slab"), lax.axis_index("xy")
-    first = copy_all([(block_any, block_ref), (cells_any, cells_ref), (vol_any, vol_ref)], small)
+    first = copy_all([(block_any, block_ref), (cells_any, cells_ref)], small)
     for copy in first:
         copy.start()
     for flip, part in enumerate(parts):
@@ -330,7 +330,7 @@
 def back_project(plan, volume, footprint, tile_block, tile_cells, parts):
     planes, rows, tiles, views, tdet, tvox = footprint.shape
     shape = planes, rows, tiles, views, tvox, tdet
-    spaces = [pl.ANY, pltpu.VMEM, pl.ANY, pl.ANY] + [pltpu.VMEM] * len(parts)
+    spaces = [pltpu.VMEM, pltpu.VMEM, pl.ANY, pl.ANY] + [pltpu.VMEM] * len(parts)
     footprint = pltpu.with_memory_space_constraint(footprint, pltpu.VMEM)
     return pl.pallas_call(
         functools.partial(back_kernel, plan, shape),
@@ -340,10 +340,9 @@
         scratch_shapes=[
             pltpu.VMEM((2, rows, tvox), jnp.float32),
             pltpu.VMEM((views, plan.units + plan.halo_units, plan.unit, tdet), jnp.float32),
-            pltpu.VMEM(volume.shape, jnp.float32),
             pltpu.SMEM(tile_block.shape, jnp.int32),
             pltpu.SMEM(tile_cells.shape, jnp.int32),
-            pltpu.SemaphoreType.DMA((3,)),
+            pltpu.SemaphoreType.DMA((2,)),
         ],
         compiler_params=pltpu.CompilerParams(vmem_limit_bytes=VMEM_BYTES // 2),
         name="back_project",

time: 50.1 us -> 50.1 us (level)
  no operation moved by 1% of the time
where the time goes in v8:
time: 50.1 us; the launch traced here: 49.9 us
  starting transfers between devices  21.4 us (43%)
  waiting for transfers between devices  16.2 us (32%)
  Pallas kernels  11.5 us (23%)
  between operations  0.73 us (1%)
    ppermute x16, starting transfers between devices, swap_all(): return lax.ppermute(cells, axis, [(i, i ^ flip) for i in range(count)])  17.9 us
    ppermute x16, waiting for transfers between devices, swap_all(): return lax.ppermute(cells, axis, [(i, i ^ flip) for i in range(count)])  14.5 us
    pallas_call x1, Pallas kernels, project(): pl.pallas_call(functools.partial(project_kernel, plan, shape), out_shape=...  3.9 us
    ppermute x2, starting transfers between devices, shift_all(): lax.ppermute(cells, axis, [(i, (i + step) % count) for i in range(count)])  3.45 us
    pallas_call x1, Pallas kernels, smooth(): pl.pallas_call(functools.partial(smooth_kernel, sizes), out_shape=(jax.Sh...  3.24 us
    pallas_call x1, Pallas kernels, turn(): pl.pallas_call(functools.partial(turn_kernel, shape), out_shape=pltpu.VME...  2.21 us
    pallas_call x1, Pallas kernels, back_project(): pl.pallas_call(functools.partial(back_kernel, plan, shape), out_shape=jax...  2.09 us
    ppermute x2, waiting for transfers between devices, shift_all(): lax.ppermute(cells, axis, [(i, (i + step) % count) for i in range(count)])  1.75 us
  transfers between devices with their start and end apart: 18, of which 13 were waited for; matrix products, arithmetic and copies ran while one was open for 0% of the time, Pallas kernels for 4%

profile of v8, /device:TPU:0, one launch (start us, length us, event | category | flops | bytes accessed | tf_op | source)
XLA Modules:
  0.0 49.9 jit_solution(5006558491491954513)
XLA Ops:
  0.6 3.9 %project.1 = (f32[10,24,256]{2,1,0:T(8,128)S(1)}, f32[2,24,256]{2,1,0:T(8,128)S(1)}, f32[2,24,256]{2,1,0:T(8,128)S(1)}, f32[2,3,8,256]{3,2,1,0:T(8,128)S(1)}, bf16[2,8,4,2,128,256]{5,4,3,2,1,0:T(8,128)(2,1)S(1)}) custom-call(f32[2,8,512]{2,1,0:T(8,128)} %vol_ref.1, bf16[2,8,4,2,128,256]{5,4,3,2,1,0:T(8,128)(2,1)} %foot_hbm.1, s32[2,4,2,8]{3,2,1,0:T(2,128)} %bitcast.2, ...), custom_call_target="tpu_custom_call" | custom-call | tf_op jit(solution)/shard_map/project/pallas_call | solution.py:158
  4.5 0.5 %collective-permute-start = (f32[2,24,256]{2,1,0:T(8,128)S(1)}, f32[2,24,256]{2,1,0:T(8,128)S(1)}, u32[]{:S(2)}, u32[]{:S(2)}) collective-permute-start(f32[2,24,256]{2,1,0:T(8,128)S(1)} %get-tuple-element.16), channel_id=1, source_target_pairs={{0,4},{4,8},{8,12},{12,16},{16,20},{20,24},{24,28},{28,0},{1,5},{5... | collective-permute-start | bytes 147464 | tf_op jit(solution)/shard_map/ppermute | solution.py:44
  5.0 2.9 %collective-permute-start.1 = (f32[2,24,256]{2,1,0:T(8,128)S(1)}, f32[2,24,256]{2,1,0:T(8,128)S(1)}, u32[]{:S(2)}, u32[]{:S(2)}) collective-permute-start(f32[2,24,256]{2,1,0:T(8,128)S(1)} %get-tuple-element.17), channel_id=1, source_target_pairs={{0,28},{4,0},{8,4},{12,8},{16,12},{20,16},{24,20},{28,24},{1,29},{... | collective-permute-start | bytes 147464 | tf_op jit(solution)/shard_map/ppermute | solution.py:44
  8.0 1.7 %collective-permute-done.below_ref = f32[2,24,256]{2,1,0:T(8,128)S(1)} collective-permute-done((f32[2,24,256]{2,1,0:T(8,128)S(1)}, f32[2,24,256]{2,1,0:T(8,128)S(1)}, u32[]{:S(2)}, u32[]{:S(2)}) %collective-permute-start) | collective-permute-done | bytes 49184 | tf_op jit(solution)/shard_map/ppermute | solution.py:44
  9.7 0.1 shares.1
  9.8 4.4 %collective-permute-start.2 = (f32[3,24,256]{2,1,0:T(8,128)S(1)}, f32[3,24,256]{2,1,0:T(8,128)S(1)}, u32[]{:S(2)}, u32[]{:S(2)}) collective-permute-start(f32[3,24,256]{2,1,0:T(8,128)S(1)} %get-tuple-element.19), channel_id=1, source_target_pairs={{0,3},{1,2},{2,1},{3,0},{4,7},{5,6},{6,5},{7,4},{8,11},{9,10},{10,... | collective-permute-start | bytes 221192 | tf_op jit(solution)/shard_map/ppermute | solution.py:53
  14.2 0.6 %collective-permute-start.4 = (f32[3,24,256]{2,1,0:T(8,128)S(1)}, f32[3,24,256]{2,1,0:T(8,128)S(1)}, u32[]{:S(2)}, u32[]{:S(2)}) collective-permute-start(f32[3,24,256]{2,1,0:T(8,128)S(1)} %get-tuple-element.21), channel_id=1, source_target_pairs={{0,2},{1,3},{2,0},{3,1},{4,6},{5,7},{6,4},{7,5},{8,10},{9,11},{10,... | collective-permute-start | bytes 221192 | tf_op jit(solution)/shard_map/ppermute | solution.py:53
  14.8 2.2 %turn.1.ready_ref.foot = bf16[2,8,4,2,256,128]{5,4,3,2,1,0:T(8,128)(2,1)S(1)} custom-call(bf16[2,8,4,2,128,256]{5,4,3,2,1,0:T(8,128)(2,1)S(1)} %get-tuple-element.14.foot), custom_call_target="tpu_custom_call" | custom-call | bytes 16777216 | tf_op jit(solution)/shard_map/turn/pallas_call | solution.py:267
  17.1 0.3 collective-permute-done.2.rest_1_
  17.4 2.8 %collective-permute-done.3.rest_2_ = f32[3,24,256]{2,1,0:T(8,128)S(1)} collective-permute-done((f32[3,24,256]{2,1,0:T(8,128)S(1)}, f32[3,24,256]{2,1,0:T(8,128)S(1)}, u32[]{:S(2)}, u32[]{:S(2)}) %collective-permute-start.3) | collective-permute-done | bytes 73760 | tf_op jit(solution)/shard_map/ppermute | solution.py:53
  20.2 1.1 %collective-permute-done.4.rest_3_ = f32[3,24,256]{2,1,0:T(8,128)S(1)} collective-permute-done((f32[3,24,256]{2,1,0:T(8,128)S(1)}, f32[3,24,256]{2,1,0:T(8,128)S(1)}, u32[]{:S(2)}, u32[]{:S(2)}) %collective-permute-start.4) | collective-permute-done | bytes 73760 | tf_op jit(solution)/shard_map/ppermute | solution.py:53
  21.4 1.4 %collective-permute-start.7 = (bf16[48,256]{1,0:T(8,128)(2,1)S(1)}, bf16[48,256]{1,0:T(8,128)(2,1)S(1)}, u32[]{:S(2)}, u32[]{:S(2)}) collective-permute-start(bf16[48,256]{1,0:T(8,128)(2,1)S(1)} %get-tuple-element.23.rest_0_), channel_id=1, source_target_pairs={{0,3},{1,2},{2,1},{3,0},{4,7},{5,6},{6,5},{7,4},{8,11},{9,10},{10,... | collective-permute-start | bytes 73736 | tf_op jit(solution)/shard_map/ppermute | solution.py:53
  22.8 0.5 collective-permute-start.6
  23.3 2.5 %collective-permute-start.5 = (bf16[48,256]{1,0:T(8,128)(2,1)S(1)}, bf16[48,256]{1,0:T(8,128)(2,1)S(1)}, u32[]{:S(2)}, u32[]{:S(2)}) collective-permute-start(bf16[48,256]{1,0:T(8,128)(2,1)S(1)} %get-tuple-element.23.rest_0_), channel_id=1, source_target_pairs={{0,1},{1,0},{2,3},{3,2},{4,5},{5,4},{6,7},{7,6},{8,9},{9,8},{10,11... | collective-permute-start | bytes 73736 | tf_op jit(solution)/shard_map/ppermute | solution.py:53
  25.8 1.2 %collective-permute-done.7.rest_3_ = bf16[48,256]{1,0:T(8,128)(2,1)S(1)} collective-permute-done((bf16[48,256]{1,0:T(8,128)(2,1)S(1)}, bf16[48,256]{1,0:T(8,128)(2,1)S(1)}, u32[]{:S(2)}, u32[]{:S(2)}) %collective-permute-start.7) | collective-permute-done | bytes 24608 | tf_op jit(solution)/shard_map/ppermute | solution.py:53
  27.1 0.5 collective-permute-done.6.rest_2_
  27.6 0.2 collective-permute-done.5.rest_1_
  27.8 2.1 %back_project.1 = f32[9,8,128]{2,1,0:T(8,128)S(1)} custom-call(f32[2,8,512]{2,1,0:T(8,128)S(1)} %copy-done, bf16[2,8,4,2,256,128]{5,4,3,2,1,0:T(8,128)(2,1)S(1)} %turn.1.ready_ref.foot, s32[2,4,2,8]{3,2,1,0:T(2,128)S(1)} %bitcast.3, s32[2,4,2,8]{3,2,1,0:T(2,128)S(1)} %bitcast.5, bf16[48,256]{1,0:T(8,128)(2,1)S(1)} %get-tuple-element.23.rest_0_, ...), custom_call_target="tpu_custom_call" | custom-call | tf_op jit(solution)/shard_map/back_project/pallas_call | solution.py:335
  29.9 2.5 %collective-permute-start.10 = (f32[9,8,128]{2,1,0:T(8,128)S(1)}, f32[9,8,128]{2,1,0:T(8,128)S(1)}, u32[]{:S(2)}, u32[]{:S(2)}) collective-permute-start(f32[9,8,128]{2,1,0:T(8,128)S(1)} %back_project.1), channel_id=1, source_target_pairs={{0,3},{1,2},{2,1},{3,0},{4,7},{5,6},{6,5},{7,4},{8,11},{9,10},{10,... | collective-permute-start | bytes 110600 | tf_op jit(solution)/shard_map/ppermute | solution.py:53
  32.4 0.9 %collective-permute-start.9 = (f32[9,8,128]{2,1,0:T(8,128)S(1)}, f32[9,8,128]{2,1,0:T(8,128)S(1)}, u32[]{:S(2)}, u32[]{:S(2)}) collective-permute-start(f32[9,8,128]{2,1,0:T(8,128)S(1)} %back_project.1), channel_id=1, source_target_pairs={{0,2},{1,3},{2,0},{3,1},{4,6},{5,7},{6,4},{7,5},{8,10},{9,11},{10,... | collective-permute-start | bytes 110600 | tf_op jit(solution)/shard_map/ppermute | solution.py:53
  33.3 1.1 %collective-permute-start.8 = (f32[9,8,128]{2,1,0:T(8,128)S(1)}, f32[9,8,128]{2,1,0:T(8,128)S(1)}, u32[]{:S(2)}, u32[]{:S(2)}) collective-permute-start(f32[9,8,128]{2,1,0:T(8,128)S(1)} %back_project.1), channel_id=1, source_target_pairs={{0,1},{1,0},{2,3},{3,2},{4,5},{5,4},{6,7},{7,6},{8,9},{9,8},{10,11... | collective-permute-start | bytes 110600 | tf_op jit(solution)/shard_map/ppermute | solution.py:53
  34.4 3.3 %collective-permute-done.8 = f32[9,8,128]{2,1,0:T(8,128)S(1)} collective-permute-done((f32[9,8,128]{2,1,0:T(8,128)S(1)}, f32[9,8,128]{2,1,0:T(8,128)S(1)}, u32[]{:S(2)}, u32[]{:S(2)}) %collective-permute-start.8) | collective-permute-done | bytes 36896 | tf_op jit(solution)/shard_map/ppermute | solution.py:53
  37.7 1.3 %collective-permute-start.13 = (f32[33,8,128]{2,1,0:T(8,128)S(1)}, f32[33,8,128]{2,1,0:T(8,128)S(1)}, u32[]{:S(2)}, u32[]{:S(2)}) collective-permute-start(f32[33,8,128]{2,1,0:T(8,128)S(1)} %constant_dynamic-update-slice_fusion.rest_0_), channel_id=1, source_target_pairs={{0,24},{4,28},{8,16},{12,20},{16,8},{20,12},{24,0},{28,4},{1,25},{... | collective-permute-start | bytes 405512 | tf_op jit(solution)/shard_map/ppermute | solution.py:53
  39.0 0.8 %collective-permute-start.12 = (f32[33,8,128]{2,1,0:T(8,128)S(1)}, f32[33,8,128]{2,1,0:T(8,128)S(1)}, u32[]{:S(2)}, u32[]{:S(2)}) collective-permute-start(f32[33,8,128]{2,1,0:T(8,128)S(1)} %constant_dynamic-update-slice_fusion.rest_0_), channel_id=1, source_target_pairs={{0,16},{4,20},{8,24},{12,28},{16,0},{20,4},{24,8},{28,12},{1,17},{... | collective-permute-start | bytes 405512 | tf_op jit(solution)/shard_map/ppermute | solution.py:53
  39.8 1.4 %collective-permute-start.11 = (f32[33,8,128]{2,1,0:T(8,128)S(1)}, f32[33,8,128]{2,1,0:T(8,128)S(1)}, u32[]{:S(2)}, u32[]{:S(2)}) collective-permute-start(f32[33,8,128]{2,1,0:T(8,128)S(1)} %constant_dynamic-update-slice_fusion.rest_0_), channel_id=1, source_target_pairs={{0,8},{4,12},{8,0},{12,4},{16,24},{20,28},{24,16},{28,20},{1,9},{5... | collective-permute-start | bytes 405512 | tf_op jit(solution)/shard_map/ppermute | solution.py:53
  41.3 2.5 %collective-permute-done.13.rest_3_ = f32[33,8,128]{2,1,0:T(8,128)S(1)} collective-permute-done((f32[33,8,128]{2,1,0:T(8,128)S(1)}, f32[33,8,128]{2,1,0:T(8,128)S(1)}, u32[]{:S(2)}, u32[]{:S(2)}) %collective-permute-start.13) | collective-permute-done | bytes 135200 | tf_op jit(solution)/shard_map/ppermute | solution.py:53
  43.8 1.3 %collective-permute-done.12.rest_2_ = f32[33,8,128]{2,1,0:T(8,128)S(1)} collective-permute-done((f32[33,8,128]{2,1,0:T(8,128)S(1)}, f32[33,8,128]{2,1,0:T(8,128)S(1)}, u32[]{:S(2)}, u32[]{:S(2)}) %collective-permute-start.12) | collective-permute-done | bytes 135200 | tf_op jit(solution)/shard_map/ppermute | solution.py:53
  45.1 0.1 collective-permute-done.11.rest_1_
  45.2 0.4 collective-permute-start.16
  45.6 0.8 %collective-permute-done.15.rest_5_ = f32[33,8,128]{2,1,0:T(8,128)S(1)} collective-permute-done((f32[33,8,128]{2,1,0:T(8,128)S(1)}, f32[33,8,128]{2,1,0:T(8,128)S(1)}, u32[]{:S(2)}, u32[]{:S(2)}) %collective-permute-start.15) | collective-permute-done | bytes 135200 | tf_op jit(solution)/shard_map/ppermute | solution.py:53
  46.5 0.2 collective-permute-done.16.rest_6_
  46.7 3.2 %smooth.1 = (f32[2,8,512]{2,1,0:T(8,128)}, f32[2,4096]{1,0:T(2,128)}) custom-call(f32[2,2,8,256]{3,2,1,0:T(8,128)S(1)} %get-tuple-element.22.exact_ref, f32[33,8,128]{2,1,0:T(8,128)S(1)} %constant_dynamic-update-slice_fusion.rest_0_, f32[33,8,128]{2,1,0:T(8,128)S(1)} %collective-permute-done.11.rest_1_, f32[33,8,128]{2,1,0:T(8,128)S(1)} %collective-permute-done.12.rest_2_, ...), custom_call_target="tpu_custom_call" | custom-call | tf_op jit(solution)/shard_map/smooth/pallas_call | solution.py:472
  (21 shorter events, 0.2 us)
Async XLA Ops:
  4.5 5.2 %collective-permute-start = (f32[2,24,256]{2,1,0:T(8,128)S(1)}, f32[2,24,256]{2,1,0:T(8,128)S(1)}, u32[]{:S(2)}, u32[]{:S(2)}) collective-permute-start(f32[2,24,256]{2,1,0:T(8,128)S(1)} %get-tuple-element.16), channel_id=1, source_target_pairs={{0,4},{4,8},{8,12},{12,16},{16,20},{20,24},{24,28},{28,0},{1,5},{5... | collective-permute-start | bytes 147464 | tf_op jit(solution)/shard_map/ppermute | solution.py:44
  5.0 4.7 %collective-permute-start.1 = (f32[2,24,256]{2,1,0:T(8,128)S(1)}, f32[2,24,256]{2,1,0:T(8,128)S(1)}, u32[]{:S(2)}, u32[]{:S(2)}) collective-permute-start(f32[2,24,256]{2,1,0:T(8,128)S(1)} %get-tuple-element.17), channel_id=1, source_target_pairs={{0,28},{4,0},{8,4},{12,8},{16,12},{20,16},{24,20},{28,24},{1,29},{... | collective-permute-start | bytes 147464 | tf_op jit(solution)/shard_map/ppermute | solution.py:44
  9.8 7.6 %collective-permute-start.2 = (f32[3,24,256]{2,1,0:T(8,128)S(1)}, f32[3,24,256]{2,1,0:T(8,128)S(1)}, u32[]{:S(2)}, u32[]{:S(2)}) collective-permute-start(f32[3,24,256]{2,1,0:T(8,128)S(1)} %get-tuple-element.19), channel_id=1, source_target_pairs={{0,3},{1,2},{2,1},{3,0},{4,7},{5,6},{6,5},{7,4},{8,11},{9,10},{10,... | collective-permute-start | bytes 221192 | tf_op jit(solution)/shard_map/ppermute | solution.py:53
  14.2 6.0 %collective-permute-start.3 = (f32[3,24,256]{2,1,0:T(8,128)S(1)}, f32[3,24,256]{2,1,0:T(8,128)S(1)}, u32[]{:S(2)}, u32[]{:S(2)}) collective-permute-start(f32[3,24,256]{2,1,0:T(8,128)S(1)} %get-tuple-element.20), channel_id=1, source_target_pairs={{0,1},{1,0},{2,3},{3,2},{4,5},{5,4},{6,7},{7,6},{8,9},{9,8},{10,11... | collective-permute-start | bytes 221192 | tf_op jit(solution)/shard_map/ppermute | solution.py:53
  14.2 7.1 %collective-permute-start.4 = (f32[3,24,256]{2,1,0:T(8,128)S(1)}, f32[3,24,256]{2,1,0:T(8,128)S(1)}, u32[]{:S(2)}, u32[]{:S(2)}) collective-permute-start(f32[3,24,256]{2,1,0:T(8,128)S(1)} %get-tuple-element.21), channel_id=1, source_target_pairs={{0,2},{1,3},{2,0},{3,1},{4,6},{5,7},{6,4},{7,5},{8,10},{9,11},{10,... | collective-permute-start | bytes 221192 | tf_op jit(solution)/shard_map/ppermute | solution.py:53
  17.0 10.8 %copy-start = (f32[2,8,512]{2,1,0:T(8,128)S(1)}, f32[2,8,512]{2,1,0:T(8,128)}, u32[]{:S(2)}) copy-start(f32[2,8,512]{2,1,0:T(8,128)} %vol_ref.1) | copy-start | bytes 98308
  17.1 10.8 %copy-start.1 = (s32[2,8,4,2]{1,3,2,0:T(2,128)S(1)}, s32[2,8,4,2]{1,3,2,0:T(2,128)}, u32[]{:S(2)}) copy-start(s32[2,8,4,2]{1,3,2,0:T(2,128)} %param.7) | copy-start | bytes 1540
  17.1 10.8 %copy-start.2 = (s32[2,8,4,2]{1,3,2,0:T(2,128)S(1)}, s32[2,8,4,2]{1,3,2,0:T(2,128)}, u32[]{:S(2)}) copy-start(s32[2,8,4,2]{1,3,2,0:T(2,128)} %param.8) | copy-start | bytes 1540
  21.4 5.7 %collective-permute-start.7 = (bf16[48,256]{1,0:T(8,128)(2,1)S(1)}, bf16[48,256]{1,0:T(8,128)(2,1)S(1)}, u32[]{:S(2)}, u32[]{:S(2)}) collective-permute-start(bf16[48,256]{1,0:T(8,128)(2,1)S(1)} %get-tuple-element.23.rest_0_), channel_id=1, source_target_pairs={{0,3},{1,2},{2,1},{3,0},{4,7},{5,6},{6,5},{7,4},{8,11},{9,10},{10,... | collective-permute-start | bytes 73736 | tf_op jit(solution)/shard_map/ppermute | solution.py:53
  22.8 4.7 %collective-permute-start.6 = (bf16[48,256]{1,0:T(8,128)(2,1)S(1)}, bf16[48,256]{1,0:T(8,128)(2,1)S(1)}, u32[]{:S(2)}, u32[]{:S(2)}) collective-permute-start(bf16[48,256]{1,0:T(8,128)(2,1)S(1)} %get-tuple-element.23.rest_0_), channel_id=1, source_target_pairs={{0,2},{1,3},{2,0},{3,1},{4,6},{5,7},{6,4},{7,5},{8,10},{9,11},{10,... | collective-permute-start | bytes 73736 | tf_op jit(solution)/shard_map/ppermute | solution.py:53
  23.3 4.5 %collective-permute-start.5 = (bf16[48,256]{1,0:T(8,128)(2,1)S(1)}, bf16[48,256]{1,0:T(8,128)(2,1)S(1)}, u32[]{:S(2)}, u32[]{:S(2)}) collective-permute-start(bf16[48,256]{1,0:T(8,128)(2,1)S(1)} %get-tuple-element.23.rest_0_), channel_id=1, source_target_pairs={{0,1},{1,0},{2,3},{3,2},{4,5},{5,4},{6,7},{7,6},{8,9},{9,8},{10,11... | collective-permute-start | bytes 73736 | tf_op jit(solution)/shard_map/ppermute | solution.py:53
  29.9 7.7 %collective-permute-start.10 = (f32[9,8,128]{2,1,0:T(8,128)S(1)}, f32[9,8,128]{2,1,0:T(8,128)S(1)}, u32[]{:S(2)}, u32[]{:S(2)}) collective-permute-start(f32[9,8,128]{2,1,0:T(8,128)S(1)} %back_project.1), channel_id=1, source_target_pairs={{0,3},{1,2},{2,1},{3,0},{4,7},{5,6},{6,5},{7,4},{8,11},{9,10},{10,... | collective-permute-start | bytes 110600 | tf_op jit(solution)/shard_map/ppermute | solution.py:53
  32.4 5.2 %collective-permute-start.9 = (f32[9,8,128]{2,1,0:T(8,128)S(1)}, f32[9,8,128]{2,1,0:T(8,128)S(1)}, u32[]{:S(2)}, u32[]{:S(2)}) collective-permute-start(f32[9,8,128]{2,1,0:T(8,128)S(1)} %back_project.1), channel_id=1, source_target_pairs={{0,2},{1,3},{2,0},{3,1},{4,6},{5,7},{6,4},{7,5},{8,10},{9,11},{10,... | collective-permute-start | bytes 110600 | tf_op jit(solution)/shard_map/ppermute | solution.py:53
  33.3 4.4 %collective-permute-start.8 = (f32[9,8,128]{2,1,0:T(8,128)S(1)}, f32[9,8,128]{2,1,0:T(8,128)S(1)}, u32[]{:S(2)}, u32[]{:S(2)}) collective-permute-start(f32[9,8,128]{2,1,0:T(8,128)S(1)} %back_project.1), channel_id=1, source_target_pairs={{0,1},{1,0},{2,3},{3,2},{4,5},{5,4},{6,7},{7,6},{8,9},{9,8},{10,11... | collective-permute-start | bytes 110600 | tf_op jit(solution)/shard_map/ppermute | solution.py:53
  37.7 6.1 %collective-permute-start.13 = (f32[33,8,128]{2,1,0:T(8,128)S(1)}, f32[33,8,128]{2,1,0:T(8,128)S(1)}, u32[]{:S(2)}, u32[]{:S(2)}) collective-permute-start(f32[33,8,128]{2,1,0:T(8,128)S(1)} %constant_dynamic-update-slice_fusion.rest_0_), channel_id=1, source_target_pairs={{0,24},{4,28},{8,16},{12,20},{16,8},{20,12},{24,0},{28,4},{1,25},{... | collective-permute-start | bytes 405512 | tf_op jit(solution)/shard_map/ppermute | solution.py:53
  39.0 6.1 %collective-permute-start.12 = (f32[33,8,128]{2,1,0:T(8,128)S(1)}, f32[33,8,128]{2,1,0:T(8,128)S(1)}, u32[]{:S(2)}, u32[]{:S(2)}) collective-permute-start(f32[33,8,128]{2,1,0:T(8,128)S(1)} %constant_dynamic-update-slice_fusion.rest_0_), channel_id=1, source_target_pairs={{0,16},{4,20},{8,24},{12,28},{16,0},{20,4},{24,8},{28,12},{1,17},{... | collective-permute-start | bytes 405512 | tf_op jit(solution)/shard_map/ppermute | solution.py:53
  39.8 5.4 %collective-permute-start.11 = (f32[33,8,128]{2,1,0:T(8,128)S(1)}, f32[33,8,128]{2,1,0:T(8,128)S(1)}, u32[]{:S(2)}, u32[]{:S(2)}) collective-permute-start(f32[33,8,128]{2,1,0:T(8,128)S(1)} %constant_dynamic-update-slice_fusion.rest_0_), channel_id=1, source_target_pairs={{0,8},{4,12},{8,0},{12,4},{16,24},{20,28},{24,16},{28,20},{1,9},{5... | collective-permute-start | bytes 405512 | tf_op jit(solution)/shard_map/ppermute | solution.py:53
  41.3 4.4 %collective-permute-start.17 = (f32[33,8,128]{2,1,0:T(8,128)S(1)}, f32[33,8,128]{2,1,0:T(8,128)S(1)}, u32[]{:S(2)}, u32[]{:S(2)}) collective-permute-start(f32[33,8,128]{2,1,0:T(8,128)S(1)} %constant_dynamic-update-slice_fusion.rest_0_), channel_id=1, source_target_pairs={{0,4},{4,0},{8,12},{12,8},{16,20},{20,16},{24,28},{28,24},{1,5},{5... | collective-permute-start | bytes 405512 | tf_op jit(solution)/shard_map/ppermute | solution.py:53
  43.8 1.9 %collective-permute-start.14 = (f32[33,8,128]{2,1,0:T(8,128)S(1)}, f32[33,8,128]{2,1,0:T(8,128)S(1)}, u32[]{:S(2)}, u32[]{:S(2)}) collective-permute-start(f32[33,8,128]{2,1,0:T(8,128)S(1)} %collective-permute-done.13.rest_3_), channel_id=1, source_target_pairs={{0,4},{4,0},{8,12},{12,8},{16,20},{20,16},{24,28},{28,24},{1,5},{5... | collective-permute-start | bytes 405512 | tf_op jit(solution)/shard_map/ppermute | solution.py:53
  45.1 1.4 %collective-permute-start.15 = (f32[33,8,128]{2,1,0:T(8,128)S(1)}, f32[33,8,128]{2,1,0:T(8,128)S(1)}, u32[]{:S(2)}, u32[]{:S(2)}) collective-permute-start(f32[33,8,128]{2,1,0:T(8,128)S(1)} %collective-permute-done.12.rest_2_), channel_id=1, source_target_pairs={{0,4},{4,0},{8,12},{12,8},{16,20},{20,16},{24,28},{28,24},{1,5},{5... | collective-permute-start | bytes 405512 | tf_op jit(solution)/shard_map/ppermute | solution.py:53
  45.2 1.4 %collective-permute-start.16 = (f32[33,8,128]{2,1,0:T(8,128)S(1)}, f32[33,8,128]{2,1,0:T(8,128)S(1)}, u32[]{:S(2)}, u32[]{:S(2)}) collective-permute-start(f32[33,8,128]{2,1,0:T(8,128)S(1)} %collective-permute-done.11.rest_1_), channel_id=1, source_target_pairs={{0,4},{4,0},{8,12},{12,8},{16,20},{20,16},{24,28},{28,24},{1,5},{5... | collective-permute-start | bytes 405512 | tf_op jit(solution)/shard_map/ppermute | solution.py:53
